TPU v7x, 32 devices: a whole 2x2x4 slice. The times are simulated.
32 devices in a mesh: groups: 2 (over y), src: 16 (over z, x, core).
Axes of the slice: x: 2, y: 2, z: 4, core: 2. Of those that a mesh axis runs over, the one named last changes fastest.
Arguments:
- src_latent: float32 [64, 8192], P(None, ('groups', 'src')), parts along dimension 1, may hold values from -0.75 to 0.75
- src_potential: float32 [2, 8192], P(None, ('groups', 'src')), parts along dimension 1, may hold values from 0.3 to 0.7
- tgt_latent: float32 [64, 4096], P(None, ('groups', 'src')), parts along dimension 1, may hold values from -0.75 to 0.75
- tgt_potential: float32 [2, 4096], P(None, ('groups', 'src')), parts along dimension 1, may hold values from 0.3 to 0.7
Outputs:
- grad_src: float32 [64, 8192], P(None, ('groups', 'src')), parts along dimension 1
- grad_tgt: float32 [64, 4096], P(None, ('groups', 'src')), parts along dimension 1
There are 2 independent parts, one for each index of `groups`. A program takes and returns all parts, laid end to end along the dimension named above; each array names one. Nothing has to cross between parts.
All inputs are finite; a program needn't handle non-finite values.
Results may differ from a plain program's by a relative error of at most 0.0003.
Values sent between devices are 32-bit elements; how exact they have to be, the bound alone decides.
No kernel may reach another device: no remote copies, remote signals or barrier semaphores. Data moves between devices by JAX's collectives and lax.ppermute only.
A program may use at most 64 MiB of HBM per device.

v0:
```python
import math

import jax
import jax.numpy as jnp
from jax import lax
from jax.sharding import PartitionSpec as P

epsilon = 0.1
highest = lax.Precision.HIGHEST


def pair_kernel(left_lat, left_pot, left_first, right_lat, right_pot, right_first, self_pair):
    inner_prod = lax.dot_general(
        left_lat,
        right_lat,
        (((0,), (0,)), ((), ())),
        precision=highest,
        preferred_element_type=jnp.float32,
    )
    pair_cost = (
        0.5 * jnp.sum(left_lat * left_lat, 0)[:, None]
        + 0.5 * jnp.sum(right_lat * right_lat, 0)[None, :]
        - inner_prod
    )
    weight = jnp.exp((left_pot[:, None] + right_pot[None, :] - pair_cost) / epsilon)
    if self_pair:
        rows_id = left_first + lax.iota(jnp.int32, left_lat.shape[1])
        cols_id = right_first + lax.iota(jnp.int32, right_lat.shape[1])
        weight = jnp.where(rows_id[:, None] == cols_id[None, :], jnp.float32(0.0), weight)
    return weight


def sweep_pairs(left_lat, left_pot, left_first, piece_lat, piece_pot, self_pair, want_right):
    piece_count = piece_lat.shape[1]
    block_width = math.gcd(piece_count, 512)
    block_total = piece_count // block_width

    def block_step(running, block_index):
        block_begin = block_index * block_width
        block_cols = lax.dynamic_slice_in_dim(piece_lat, block_begin, block_width, 1)
        block_pot = lax.dynamic_slice_in_dim(piece_pot, block_begin, block_width, 0)
        weight = pair_kernel(
            left_lat, left_pot, left_first, block_cols, block_pot, block_begin, self_pair
        )
        mixed_sum = lax.dot_general(
            block_cols,
            weight,
            (((1,), (1,)), ((), ())),
            precision=highest,
            preferred_element_type=jnp.float32,
        )
        running = running + left_lat * jnp.sum(weight, 1)[None, :] - mixed_sum
        if want_right:
            back_sum = jnp.dot(
                left_lat, weight, precision=highest, preferred_element_type=jnp.float32
            )
            return (running, block_cols * jnp.sum(weight, 0)[None, :] - back_sum)
        return (running, None)

    running, right_terms = lax.scan(
        block_step, jnp.zeros(left_lat.shape, jnp.float32), jnp.arange(block_total, dtype=jnp.int32)
    )
    if want_right:
        right_terms = jnp.transpose(right_terms, (1, 0, 2)).reshape(left_lat.shape[0], piece_count)
    return (running, right_terms)


def body(src_latent, src_potential, tgt_latent, tgt_potential):
    src_count = src_latent.shape[1]
    tgt_count = tgt_latent.shape[1]
    devices = lax.axis_size("src")
    device_place = lax.axis_index("src")
    src_first = device_place * src_count
    tgt_first = device_place * tgt_count
    total_src = src_count * devices
    total_tgt = tgt_count * devices
    zero_tgt = jnp.zeros(tgt_latent.shape, jnp.float32)
    self_y = zero_tgt
    piece_lat = lax.all_gather(tgt_latent, "src", axis=1, tiled=True)
    piece_pot = lax.all_gather(tgt_potential, "src", axis=1, tiled=True)
    left_term, right_term = sweep_pairs(
        src_latent, src_potential[0], src_first, piece_lat, piece_pot[0], False, True
    )
    cross_x = left_term
    partial_value = right_term
    cross_x, partial_value, self_y = (cross_x, partial_value, self_y)
    cross_y = lax.psum_scatter(partial_value, "src", scatter_dimension=1, tiled=True)
    self_y = sweep_pairs(
        tgt_latent,
        tgt_potential[1],
        tgt_first,
        lax.all_gather(tgt_latent, "src", axis=1, tiled=True),
        lax.all_gather(tgt_potential, "src", axis=1, tiled=True)[1],
        True,
        False,
    )[0]
    cross_part = cross_y
    piece_lat = lax.all_gather(src_latent, "src", axis=1, tiled=True)
    piece_pot = lax.all_gather(src_potential, "src", axis=1, tiled=True)
    self_x = sweep_pairs(
        src_latent, src_potential[1], src_first, piece_lat, piece_pot[1], True, False
    )[0]
    self_x, cross_part = (self_x, cross_part)
    grad_src = cross_x / total_tgt - self_x / total_src
    grad_tgt = cross_part / total_src - self_y / total_tgt
    return (grad_src, grad_tgt)


def solution(mesh):
    in_specs = (
        P(None, ("groups", "src")),
        P(None, ("groups", "src")),
        P(None, ("groups", "src")),
        P(None, ("groups", "src")),
    )
    out_specs = (P(None, ("groups", "src")), P(None, ("groups", "src")))
    return jax.shard_map(body, mesh=mesh, in_specs=in_specs, out_specs=out_specs, check_vma=False)
```

profile of v0, /device:TPU:0, one launch (start us, length us, event | category | flops | bytes accessed | tf_op | source)
XLA Modules:
  0.0 207.7 jit_solution(11275068441182799626)
XLA Ops:
  7.3 24.9 %all_gather.15 = f32[64,2048]{1,0:T(8,128)S(1)} all-gather(f32[64,128]{1,0:T(8,128)} %param.12), channel_id=1, replica_groups=mesh['groups'=2,'src'=16] {'src'}, dimensions={1}, use_global_device_ids=true | all-gather | bytes 557056 | tf_op jit(solution)/shard_map/all_gather | solution.py:79
  32.2 17.4 %all_gather.14 = f32[2,2048]{1,0:T(2,128)S(1)} all-gather(f32[2,128]{1,0:T(2,128)S(1)} %copy-done.4), channel_id=1, replica_groups=mesh['groups'=2,'src'=16] {'src'}, dimensions={1}, use_global_device_ids=true | all-gather | bytes 17408 | tf_op jit(solution)/shard_map/all_gather | solution.py:80
  50.3 13.0 %while.41 = (s32[]{:T(128)}, f32[64,256]{1,0:T(8,128)S(1)}, f32[4,64,512]{2,1,0:T(8,128)S(1)}, f32[1,256]{1,0:T(1,128)S(1)}, s32[4]{0:T(128)S(1)}, /*index=5*/f3...) while((s32[]{:T(128)}, f32[64,256]{1,0:T(8,128)S(1)}, ...), condition=%wide.region_5.6_spmd.clone, body=%wide.region_1.5_spmd.clone.sunk | while | flops 303103488 | bytes 2580697 | solution.py:60
  51.7 0.8 fusion.62
  55.0 0.8 fusion.62
  58.2 0.8 fusion.62
  61.5 0.8 fusion.62
  63.4 0.9 copy.7
  64.3 0.7 all-gather.2.cloned.1.call-update
  65.1 9.7 %while.43 = (s32[]{:T(128)}, f32[64,128]{1,0:T(8,128)S(1)}, s32[]{:T(128)}, s32[4]{0:T(128)S(1)}, f32[1,128]{1,0:T(1,128)S(1)}, /*index=5*/f32[2048]{0:T(1024)S(...) while((s32[]{:T(128)}, f32[64,128]{1,0:T(8,128)S(1)}, ...), condition=%wide.region_15.16_spmd.clone, body=%wide.region_12.15_spmd.clone.sunk | while | flops 101286528 | bytes 1071321 | solution.py:60
  66.5 0.7 fusion.71
  68.9 0.7 fusion.71
  71.4 0.7 fusion.71
  73.8 0.7 fusion.71
  74.8 18.9 %all_gather.16 = f32[2,4096]{1,0:T(2,128)S(1)} all-gather(f32[2,256]{1,0:T(2,128)S(1)} %copy-done.3), channel_id=1, replica_groups=mesh['groups'=2,'src'=16] {'src'}, dimensions={1}, use_global_device_ids=true | all-gather | bytes 34816 | tf_op jit(solution)/shard_map/all_gather | solution.py:99
  93.8 24.9 %reduce-scatter.2.cloned.1.call-done = f32[64,128]{1,0:T(8,128)} async-done(((f32[64,2048]{1,0:T(8,128)}), f32[64,128]{1,0:T(8,128)}) %reduce-scatter.2.cloned.1.call-update) | async-done | bytes 32784 | tf_op jit(solution)/shard_map/reduce_scatter | solution.py:87
  118.7 1.4 multiply_subtract_fusion.1
  120.1 36.9 %all-gather.2.cloned.1.call-done = f32[64,4096]{1,0:T(8,128)} async-done(((f32[64,256]{1,0:T(8,128)}), f32[64,4096]{1,0:T(8,128)}) %all-gather.2.cloned.1.call-update) | async-done | bytes 1048592 | tf_op jit(solution)/shard_map/all_gather | solution.py:98
  156.9 43.3 %while.42 = (s32[]{:T(128)}, f32[64,256]{1,0:T(8,128)S(1)}, s32[]{:T(128)}, s32[8]{0:T(128)S(1)}, f32[1,256]{1,0:T(1,128)S(1)}, /*index=5*/f32[4096]{0:T(1024)S(...) while((s32[]{:T(128)}, f32[64,256]{1,0:T(8,128)S(1)}, ...), condition=%wide.region_9.10_spmd.clone, body=%wide.region_6.0_spmd.clone.sunk | while | flops 202507008 | bytes 1730777 | solution.py:60
  158.3 0.9 multiply_reduce_fusion.9
  159.3 1.7 fusion.67
  161.0 1.3 convolution_subtract_fusion.7
  162.3 0.7 dynamic_slice.103
  163.7 0.9 multiply_reduce_fusion.9
  164.7 1.7 fusion.67
  166.4 1.3 convolution_subtract_fusion.7
  167.7 0.7 dynamic_slice.103
  169.1 0.9 multiply_reduce_fusion.9
  170.2 1.7 fusion.67
  171.8 1.3 convolution_subtract_fusion.7
  173.2 0.7 dynamic_slice.103
  174.5 0.9 multiply_reduce_fusion.9
  175.6 1.7 fusion.67
  177.3 1.3 convolution_subtract_fusion.7
  179.9 0.9 multiply_reduce_fusion.9
  181.0 1.7 fusion.67
  182.7 1.3 convolution_subtract_fusion.7
  184.0 0.7 dynamic_slice.103
  185.4 0.9 multiply_reduce_fusion.9
  186.4 1.7 fusion.67
  188.1 1.3 convolution_subtract_fusion.7
  189.4 0.7 dynamic_slice.103
  190.8 0.9 multiply_reduce_fusion.9
  191.8 1.7 fusion.67
  193.5 1.3 convolution_subtract_fusion.7
  196.2 0.9 multiply_reduce_fusion.9
  197.2 1.7 fusion.67
  198.9 1.3 convolution_subtract_fusion.7
  (130 shorter events, 15.3 us)
Async XLA Ops:
  7.2 111.5 %reduce-scatter.2.cloned.1.call-start = ((), (), s32[]{:S(2)}) async-start(), calls=%async_computation.2 | async-start | bytes 557056 | tf_op jit(solution)/shard_map/reduce_scatter | solution.py:87
  7.2 25.0 %copy-start.4 = (f32[2,128]{1,0:T(2,128)S(1)}, f32[2,128]{1,0:T(2,128)}, u32[]{:S(2)}) copy-start(f32[2,128]{1,0:T(2,128)} %param.13) | copy-start | bytes 3076
  7.2 43.1 %copy-start = (f32[64,256]{1,0:T(8,128)S(1)}, f32[64,256]{1,0:T(8,128)}, u32[]{:S(2)}) copy-start(f32[64,256]{1,0:T(8,128)} %param.10) | copy-start | bytes 196612
  49.6 0.7 copy-start.3
  64.3 0.8 copy-start.2
  64.3 92.6 %all-gather.2.cloned.1.call-start = ((), (), s32[]{:S(2)}) async-start(), calls=%async_computation.1 | async-start | bytes 1114112 | tf_op jit(solution)/shard_map/all_gather | solution.py:98
  93.8 63.2 %copy-start.1 = (f32[64,256]{1,0:T(8,128)S(1)}, f32[64,256]{1,0:T(8,128)}, u32[]{:S(2)}) copy-start(f32[64,256]{1,0:T(8,128)} %param.10) | copy-start | bytes 196612
Sparse Core Ops, SparseCore 0:
  64.4 54.2 reduce-scatter.1
  121.1 35.8 all-gather.1
where the time goes:
time: 209 us; the launch traced here: 208 us
  waiting for transfers between devices  62.5 us (30%)
  blocking collectives  61.3 us (29%)
  matrix products  35.3 us (17%)
  between operations  14.2 us (7%)
  local copies, waits for them, and re-layouts  13 us (6%)
  loops' own time  11.4 us (5%)
  other arithmetic  10 us (5%)
    all_gather x1, waiting for transfers between devices, body(): piece_lat = lax.all_gather(src_latent, 'src', axis=1, tiled=True)  36.9 us
    all_gather x1, blocking collectives, body(): piece_lat = lax.all_gather(tgt_latent, 'src', axis=1, tiled=True)  24.9 us
    reduce_scatter x1, waiting for transfers between devices, body(): lax.psum_scatter(partial_value, 'src', scatter_dimension=1, tiled=True)  24.9 us
    dot_general x16, matrix products, pair_kernel(): lax.dot_general(left_lat, right_lat, (((0,), (0,)), ((), ())), precision=...  19.7 us
    all_gather x1, blocking collectives, body(): piece_pot = lax.all_gather(src_potential, 'src', axis=1, tiled=True)  18.9 us
    all_gather x1, blocking collectives, body(): piece_pot = lax.all_gather(tgt_potential, 'src', axis=1, tiled=True)  17.4 us
    dot_general x16, matrix products, block_step(): lax.dot_general(block_cols, weight, (((1,), (1,)), ((), ())), precision=h...  13.1 us
    another operation x3, loops' own time, sweep_pairs(): lax.scan(block_step, jnp.zeros(left_lat.shape, jnp.float32), jnp.arange(b...  11.4 us
  transfers between devices with their start and end apart: 2, of which 2 were waited for; matrix products, arithmetic and copies ran while one was open for 4% of the time, Pallas kernels for 0%

commit v1 on v0

v1 whole, which is shorter than its diff:
```python
import functools
import math

import jax
import jax.numpy as jnp
from jax import lax
from jax.experimental import pallas as pl
from jax.experimental.pallas import tpu as pltpu
from jax.sharding import PartitionSpec as P

SCALE = math.log2(math.e) / 0.1
LANES = 128
f32 = jnp.float32
bf16 = jnp.bfloat16


def split(value):
    high = value.astype(bf16).astype(f32)
    return high, value - high


def pack_kernel(slabs, feats, src_ref, srcp_ref, tgt_ref, tgtp_ref, out_ref):
    src_slabs = src_ref.shape[1] // LANES
    out_ref[slabs * feats :, :] = jnp.zeros((out_ref.shape[0] - slabs * feats, LANES), f32)
    for slab in range(slabs):
        ref, pot, at = (src_ref, srcp_ref, slab) if slab < src_slabs else (tgt_ref, tgtp_ref, slab - src_slabs)
        cols = slice(at * LANES, (at + 1) * LANES)
        out_ref[slab * feats : (slab + 1) * feats, :] = ref[:, cols]
        for which in range(2):
            row = slabs * feats + which * slabs + slab
            out_ref[row : row + 1, :] = pot[which : which + 1, cols]


def pair_kernel(shape, num_rows, num_cols, own, totals, *refs):
    feats, src_slabs, tgt_slabs = shape
    slabs = src_slabs + tgt_slabs
    rows, cols = refs[:num_rows], refs[num_rows : num_rows + num_cols]
    rest = refs[num_rows + num_cols :]
    keep_ref, send_ref, lhs_ref, rvec_ref = rest[-4:]
    prev = rest[:-4]

    def cell_terms(ref, slab):
        value = ref[slab * feats : (slab + 1) * feats, :]
        norm = 0.5 * jnp.sum(value * value, 0, keepdims=True)
        pots = [
            SCALE * (ref[slabs * feats + which * slabs + slab :][:1, :] - norm)
            for which in range(2)
        ]
        return value, pots

    def place(row, slab):
        if slab < src_slabs:
            return (row * src_slabs + slab) * LANES
        return (num_rows * src_slabs + row * tgt_slabs + slab - src_slabs) * LANES

    for row in range(num_rows):
        for slab in range(slabs):
            value, pots = cell_terms(rows[row], slab)
            high, low = split(value * SCALE)
            high, low = high.astype(bf16), low.astype(bf16)
            at = slice(place(row, slab), place(row, slab) + LANES)
            lhs_ref[0:feats, at] = high
            lhs_ref[feats : 2 * feats, at] = high
            lhs_ref[2 * feats : 3 * feats, at] = low
            lhs_ref[3 * feats :, at] = low
            for which in range(2):
                rvec_ref[which : which + 1, at] = pots[which]

    groups = []
    for kind, first, last in ((0, 0, src_slabs), (1, src_slabs, slabs)):
        members = [(col, slab) for col in range(num_cols) for slab in range(first, last)]
        width = 2
        for at in range(0, len(members), width):
            groups.append((kind, members[at : at + width]))

    prepared = []
    for kind, members in groups:
        trans, values, vecs = [], [], []
        for col, slab in members:
            value, pots = cell_terms(cols[col], slab)
            high, low = split(value)
            mid, least = split(low)
            both = jnp.concatenate([high, low], 0).T.astype(bf16)
            trans.append(jnp.concatenate([both, both], 1))
            stack = jnp.concatenate([high, mid, least, jnp.ones((16, LANES), f32)], 0)
            values.append(stack.astype(bf16))
            vecs.append(jnp.concatenate(pots + [jnp.zeros((6, LANES), f32)], 0).T)
        value = jnp.concatenate(values, 1)
        prepared.append(
            (kind, members, jnp.concatenate(trans, 0), jnp.concatenate([value, value], 1), jnp.concatenate(vecs, 0))
        )

    src_width = num_rows * src_slabs * LANES
    tgt_width = num_rows * tgt_slabs * LANES
    tile = 256
    results = {}
    for begin in range(0, src_width + tgt_width, tile):
        row_kind = 0 if begin < src_width else 1
        at = slice(begin, begin + tile)
        sums = [None, None]
        for kind, members, trans, value, vecs in prepared:
            which = 1 if kind == row_kind else 0
            power = jnp.dot(trans, lhs_ref[:, at], preferred_element_type=f32)
            power = power + (rvec_ref[which : which + 1, at] + vecs[:, which : which + 1])
            weight = jnp.exp2(power)
            if own and kind == row_kind:
                for pos, (col, slab) in enumerate(members):
                    if col == 0:
                        spot = place(0, slab)
                        if begin <= spot < begin + tile:
                            row_id = lax.broadcasted_iota(jnp.int32, weight.shape, 0) - pos * LANES
                            col_id = lax.broadcasted_iota(jnp.int32, weight.shape, 1) - (spot - begin)
                            same = (row_id == col_id) & (row_id >= 0) & (row_id < LANES)
                            weight = jnp.where(same, 0.0, weight)
            high, low = split(weight)
            both = jnp.concatenate([high.astype(bf16), low.astype(bf16)], 0)
            part = jnp.dot(value, both, preferred_element_type=f32)
            sums[kind] = part if sums[kind] is None else sums[kind] + part
        mixed = [s[0:feats] + s[feats : 2 * feats] + s[2 * feats : 3 * feats] for s in sums]
        mass = [s[3 * feats : 3 * feats + 1] for s in sums]
        sign = 1.0 if row_kind == 0 else -1.0
        inv = [sign / totals[0], sign / totals[1]]
        own_mass = mass[1] * inv[1] - mass[0] * inv[0]
        own_mixed = mixed[1] * inv[1] - mixed[0] * inv[0]
        for half in range(tile // LANES):
            spot = begin + half * LANES
            if row_kind == 0:
                row, slab = divmod(spot // LANES, src_slabs)
            else:
                row, slab = divmod((spot - src_width) // LANES, tgt_slabs)
                slab += src_slabs
            piece = slice(half * LANES, (half + 1) * LANES)
            value = rows[row][slab * feats : (slab + 1) * feats, :]
            grad = value * own_mass[:, piece] - own_mixed[:, piece]
            ref = (keep_ref, send_ref)[row % 2]
            out_at = slice(((row // 2) * slabs + slab) * LANES, ((row // 2) * slabs + slab + 1) * LANES)
            if prev:
                grad = grad + prev[row % 2][:, out_at]
            ref[:, out_at] = grad


def pair_terms(rows, cols, shape, own, totals, prev=()):
    feats, src_slabs, tgt_slabs = shape
    slabs = src_slabs + tgt_slabs
    out = jax.ShapeDtypeStruct((feats, len(rows) // 2 * slabs * LANES), f32)
    vmem = pl.BlockSpec(memory_space=pltpu.VMEM)
    args = [*rows, *cols, *prev]
    pairs = len(rows) * len(cols) * (slabs * LANES) ** 2
    return pl.pallas_call(
        functools.partial(pair_kernel, shape, len(rows), len(cols), own, totals),
        out_shape=(out, out),
        in_specs=[vmem] * len(args),
        out_specs=(vmem, vmem),
        scratch_shapes=[
            pltpu.VMEM((4 * feats, len(rows) * slabs * LANES), bf16),
            pltpu.VMEM((8, len(rows) * slabs * LANES), f32),
        ],
        compiler_params=pltpu.CompilerParams(vmem_limit_bytes=32 * 2**20),
        cost_estimate=pl.CostEstimate(flops=pairs * 1300, bytes_accessed=4 * 2**20, transcendentals=pairs),
    )(*args)


def body(src_latent, src_potential, tgt_latent, tgt_potential):
    feats, src_count = src_latent.shape
    tgt_count = tgt_latent.shape[1]
    src_slabs, tgt_slabs = src_count // LANES, tgt_count // LANES
    shape = (feats, src_slabs, tgt_slabs)
    slabs = src_slabs + tgt_slabs
    devices = lax.axis_size("src")
    totals = (src_count * devices, tgt_count * devices)
    pot_rows = -(-2 * slabs // 8) * 8
    vmem = pl.BlockSpec(memory_space=pltpu.VMEM)
    packed = pl.pallas_call(
        functools.partial(pack_kernel, slabs, feats),
        out_shape=jax.ShapeDtypeStruct((slabs * feats + pot_rows, LANES), f32),
        in_specs=[vmem] * 4,
        out_specs=vmem,
    )(src_latent, src_potential, tgt_latent, tgt_potential)

    def swap(value, bits):
        return lax.ppermute(value, "src", [(i, i ^ bits) for i in range(devices)])

    rows = [packed] + [swap(packed, k) for k in (1, 2, 3)]
    cols = [packed] + [swap(packed, k) for k in range(4, devices, 4)]
    prev = ()
    for at in range(0, len(cols), 4):
        prev = pair_terms(rows, cols[at : at + 4], shape, at == 0, totals, prev)
    keep, send = prev
    wide = slabs * LANES
    near = swap(send, 1)
    far = swap(keep[:, wide:] + near[:, wide:], 2)
    grad = keep[:, :wide] + near[:, :wide] + far
    return grad[:, :src_count], grad[:, src_count:]


def solution(mesh):
    spec = P(None, ("groups", "src"))
    return jax.shard_map(body, mesh=mesh, in_specs=(spec,) * 4, out_specs=(spec, spec), check_vma=False)
```

time: 209 us -> 29.7 us (0.14)
  blocking collectives: 61.3 us -> 0 us
  waiting for transfers between devices: 62.5 us -> 11.3 us
  matrix products: 35.3 us -> 0 us
  between operations: 14.2 us -> 0.68 us
  loops' own time: 11.4 us -> 0 us
  local copies, waits for them, and re-layouts: 13 us -> 2.14 us
  other arithmetic: 10 us -> 0.04 us
  starting transfers between devices: 0.08 us -> 8.99 us
  Pallas kernels: 0 us -> 6.35 us
    all_gather x3 -> x0, blocking collectives: 61.3 us -> none  [the longest x1 24.9 us: body(): piece_lat = lax.all_gather(tgt_latent, 'src', axis=1, tiled=True)]
    all_gather x1 -> x0, waiting for transfers between devices: 36.9 us -> none  [body(): piece_lat = lax.all_gather(src_latent, 'src', axis=1, tiled=True)]
    dot_general x36 -> x0, matrix products: 35.3 us -> none  [the longest x16 19.7 us: pair_kernel(): lax.dot_general(left_lat, right_lat, (((0,), (0,)), ((), ())), precision=...]
    reduce_scatter x1 -> x0, waiting for transfers between devices: 24.9 us -> none  [body(): lax.psum_scatter(partial_value, 'src', scatter_dimension=1, tiled=True)]
    another operation x3 -> x0, loops' own time: 11.4 us -> none  [sweep_pairs(): lax.scan(block_step, jnp.zeros(left_lat.shape, jnp.float32), jnp.arange(b...]
    dynamic_slice x32 -> x0, local copies, waits for them, and re-layouts: 11.4 us -> none  [the longest x16 10.1 us: sweep_pairs(): lax.scan(block_step, jnp.zeros(left_lat.shape, jnp.float32), jnp.arange(b...]
    ppermute x0 -> x8, waiting for transfers between devices: none -> 11.3 us  [swap(): return lax.ppermute(value, 'src', [(i, i ^ bits) for i in range(devices)])]
    ppermute x0 -> x8, starting transfers between devices: none -> 8.99 us  [swap(): return lax.ppermute(value, 'src', [(i, i ^ bits) for i in range(devices)])]
  transfers between devices with their start and end apart: 2 -> 8, of which waited for: 2 -> 4; matrix products, arithmetic and copies ran while one was open for 4% -> 0% of each run, Pallas kernels for 0% -> 0%
where the time goes in v1:
time: 29.7 us; the launch traced here: 29.5 us
  waiting for transfers between devices  11.3 us (38%)
  starting transfers between devices  8.99 us (30%)
  Pallas kernels  6.35 us (21%)
  local copies, waits for them, and re-layouts  2.14 us (7%)
  between operations  0.68 us (2%)
    ppermute x8, waiting for transfers between devices, swap(): return lax.ppermute(value, 'src', [(i, i ^ bits) for i in range(devices)])  11.3 us
    ppermute x8, starting transfers between devices, swap(): return lax.ppermute(value, 'src', [(i, i ^ bits) for i in range(devices)])  8.99 us
    pallas_call x1, Pallas kernels, pair_terms(): pl.pallas_call(functools.partial(pair_kernel, shape, len(rows), len(cols)...  4.84 us
    pallas_call x1, Pallas kernels, body(): pl.pallas_call(functools.partial(pack_kernel, slabs, feats), out_shape=ja...  1.51 us
    slice x2, local copies, waits for them, and re-layouts, body(): return (grad[:, :src_count], grad[:, src_count:])  1.25 us
    unnamed x2, local copies, waits for them, and re-layouts  0.89 us
  transfers between devices with their start and end apart: 8, of which 4 were waited for; matrix products, arithmetic and copies ran while one was open for 0% of the time, Pallas kernels for 0%

profile of v1, /device:TPU:0, one launch (start us, length us, event | category | flops | bytes accessed | tf_op | source)
XLA Modules:
  0.0 29.5 jit_solution(8743634573352914984)
XLA Ops:
  0.6 1.5 %shard_map.59.refs_0_.refs_4_ = f32[200,128]{1,0:T(8,128)} custom-call(f32[64,256]{1,0:T(8,128)} %src_ref.1, f32[2,256]{1,0:T(2,128)} %srcp_ref.1, f32[64,128]{1,0:T(8,128)} %tgt_ref.1, f32[2,128]{1,0:T(2,128)} %tgtp_ref.1), custom_call_target="tpu_custom_call" | custom-call | tf_op jit(solution)/shard_map/pallas_call | solution.py:173
  2.1 5.0 %collective-permute-start.5 = (f32[200,128]{1,0:T(8,128)}, f32[200,128]{1,0:T(8,128)S(1)}, u32[]{:S(2)}, u32[]{:S(2)}) collective-permute-start(f32[200,128]{1,0:T(8,128)} %shard_map.59.refs_0_.refs_4_), channel_id=1, source_target_pairs={{0,12},{1,13},{2,14},{3,15},{4,8},{5,9},{6,10},{7,11},{8,4},{9,5},... | collective-permute-start | bytes 307208 | tf_op jit(solution)/shard_map/ppermute | solution.py:181
  7.2 0.0 collective-permute-start.4
  7.2 0.6 %collective-permute-start.3 = (f32[200,128]{1,0:T(8,128)}, f32[200,128]{1,0:T(8,128)S(1)}, u32[]{:S(2)}, u32[]{:S(2)}) collective-permute-start(f32[200,128]{1,0:T(8,128)} %shard_map.59.refs_0_.refs_4_), channel_id=1, source_target_pairs={{0,4},{1,5},{2,6},{3,7},{4,0},{5,1},{6,2},{7,3},{8,12},{9,13},{10,... | collective-permute-start | bytes 307208 | tf_op jit(solution)/shard_map/ppermute | solution.py:181
  7.8 0.4 %collective-permute-start.2 = (f32[200,128]{1,0:T(8,128)}, f32[200,128]{1,0:T(8,128)S(1)}, u32[]{:S(2)}, u32[]{:S(2)}) collective-permute-start(f32[200,128]{1,0:T(8,128)} %shard_map.59.refs_0_.refs_4_), channel_id=1, source_target_pairs={{0,3},{1,2},{2,1},{3,0},{4,7},{5,6},{6,5},{7,4},{8,11},{9,10},{10,... | collective-permute-start | bytes 307208 | tf_op jit(solution)/shard_map/ppermute | solution.py:181
  8.1 1.4 %collective-permute-start.1 = (f32[200,128]{1,0:T(8,128)}, f32[200,128]{1,0:T(8,128)S(1)}, u32[]{:S(2)}, u32[]{:S(2)}) collective-permute-start(f32[200,128]{1,0:T(8,128)} %shard_map.59.refs_0_.refs_4_), channel_id=1, source_target_pairs={{0,2},{1,3},{2,0},{3,1},{4,6},{5,7},{6,4},{7,5},{8,10},{9,11},{10,... | collective-permute-start | bytes 307208 | tf_op jit(solution)/shard_map/ppermute | solution.py:181
  9.5 1.7 %collective-permute-done.5.refs_7_ = f32[200,128]{1,0:T(8,128)S(1)} collective-permute-done((f32[200,128]{1,0:T(8,128)}, f32[200,128]{1,0:T(8,128)S(1)}, u32[]{:S(2)}, u32[]{:S(2)}) %collective-permute-start.5) | collective-permute-done | bytes 102432 | tf_op jit(solution)/shard_map/ppermute | solution.py:181
  11.2 0.0 collective-permute-start
  11.2 4.8 %collective-permute-done.4.refs_6_ = f32[200,128]{1,0:T(8,128)S(1)} collective-permute-done((f32[200,128]{1,0:T(8,128)}, f32[200,128]{1,0:T(8,128)S(1)}, u32[]{:S(2)}, u32[]{:S(2)}) %collective-permute-start.4) | collective-permute-done | bytes 102432 | tf_op jit(solution)/shard_map/ppermute | solution.py:181
  16.0 0.0 collective-permute-done.3.refs_5_
  16.0 0.0 collective-permute-done.2.refs_3_
  16.0 0.0 collective-permute-done.1.refs_2_
  16.0 0.0 collective-permute-done.refs_1_
  16.0 0.0 copy-start
  16.1 0.9 %copy-done = f32[200,128]{1,0:T(8,128)S(1)} copy-done((f32[200,128]{1,0:T(8,128)S(1)}, f32[200,128]{1,0:T(8,128)}, u32[]{:S(2)}) %copy-start) | copy-done | bytes 102424
  16.9 4.8 %shard_map.60 = (f32[64,768]{1,0:T(8,128)S(1)}, f32[64,768]{1,0:T(8,128)S(1)}) custom-call(f32[200,128]{1,0:T(8,128)S(1)} %copy-done, f32[200,128]{1,0:T(8,128)S(1)} %collective-permute-done.refs_1_, f32[200,128]{1,0:T(8,128)S(1)} %collective-permute-done.1.refs_2_, f32[200,128]{1,0:T(8,128)S(1)} %collective-permute-done.2.refs_3_, f32[200,128]{1,0:T(8,128)S(1)} %copy-done, ...), custom_call_target="tpu_custom_call" | custom-call | flops 3067084800 | bytes 4194304 | tf_op jit(solution)/shard_map/pallas_call | solution.py:149
  21.8 0.1 collective-permute-start.6
  21.9 1.4 %collective-permute-done.6 = f32[64,768]{1,0:T(8,128)S(1)} collective-permute-done((f32[64,768]{1,0:T(8,128)S(1)}, f32[64,768]{1,0:T(8,128)S(1)}, u32[]{:S(2)}, u32[]{:S(2)}) %collective-permute-start.6) | collective-permute-done | bytes 196640 | tf_op jit(solution)/shard_map/ppermute | solution.py:181
  23.3 1.6 %collective-permute-start.7 = (f32[64,384]{1,0:T(8,128)S(1)}, f32[64,384]{1,0:T(8,128)S(1)}, u32[]{:S(2)}, u32[]{:S(2)}) collective-permute-start(f32[64,384]{1,0:T(8,128)S(1)} %slice_add_fusion), channel_id=1, source_target_pairs={{0,2},{1,3},{2,0},{3,1},{4,6},{5,7},{6,4},{7,5},{8,10},{9,11},{10,... | collective-permute-start | bytes 294920 | tf_op jit(solution)/shard_map/ppermute | solution.py:181
  24.9 3.3 %collective-permute-done.7 = f32[64,384]{1,0:T(8,128)S(1)} collective-permute-done((f32[64,384]{1,0:T(8,128)S(1)}, f32[64,384]{1,0:T(8,128)S(1)}, u32[]{:S(2)}, u32[]{:S(2)}) %collective-permute-start.7) | collective-permute-done | bytes 98336 | tf_op jit(solution)/shard_map/ppermute | solution.py:181
  28.2 0.6 %slice.27 = f32[64,128]{1,0:T(8,128)} slice(f32[64,384]{1,0:T(8,128)S(1)} %fusion), slice={[0:64], [256:384]} | slice | bytes 65536 | tf_op jit(solution)/shard_map/slice | solution.py:193
  28.9 0.6 %slice.26 = f32[64,256]{1,0:T(8,128)} slice(f32[64,384]{1,0:T(8,128)S(1)} %fusion), slice={[0:64], [0:256]} | slice | bytes 131072 | tf_op jit(solution)/shard_map/slice | solution.py:193
  (2 shorter events, 0.0 us)
Async XLA Ops:
  2.1 9.1 %collective-permute-start.5 = (f32[200,128]{1,0:T(8,128)}, f32[200,128]{1,0:T(8,128)S(1)}, u32[]{:S(2)}, u32[]{:S(2)}) collective-permute-start(f32[200,128]{1,0:T(8,128)} %shard_map.59.refs_0_.refs_4_), channel_id=1, source_target_pairs={{0,12},{1,13},{2,14},{3,15},{4,8},{5,9},{6,10},{7,11},{8,4},{9,5},... | collective-permute-start | bytes 307208 | tf_op jit(solution)/shard_map/ppermute | solution.py:181
  7.2 8.8 %collective-permute-start.4 = (f32[200,128]{1,0:T(8,128)}, f32[200,128]{1,0:T(8,128)S(1)}, u32[]{:S(2)}, u32[]{:S(2)}) collective-permute-start(f32[200,128]{1,0:T(8,128)} %shard_map.59.refs_0_.refs_4_), channel_id=1, source_target_pairs={{0,8},{1,9},{2,10},{3,11},{4,12},{5,13},{6,14},{7,15},{8,0},{9,1},... | collective-permute-start | bytes 307208 | tf_op jit(solution)/shard_map/ppermute | solution.py:181
  7.2 8.8 %collective-permute-start.3 = (f32[200,128]{1,0:T(8,128)}, f32[200,128]{1,0:T(8,128)S(1)}, u32[]{:S(2)}, u32[]{:S(2)}) collective-permute-start(f32[200,128]{1,0:T(8,128)} %shard_map.59.refs_0_.refs_4_), channel_id=1, source_target_pairs={{0,4},{1,5},{2,6},{3,7},{4,0},{5,1},{6,2},{7,3},{8,12},{9,13},{10,... | collective-permute-start | bytes 307208 | tf_op jit(solution)/shard_map/ppermute | solution.py:181
  7.8 8.3 %collective-permute-start.2 = (f32[200,128]{1,0:T(8,128)}, f32[200,128]{1,0:T(8,128)S(1)}, u32[]{:S(2)}, u32[]{:S(2)}) collective-permute-start(f32[200,128]{1,0:T(8,128)} %shard_map.59.refs_0_.refs_4_), channel_id=1, source_target_pairs={{0,3},{1,2},{2,1},{3,0},{4,7},{5,6},{6,5},{7,4},{8,11},{9,10},{10,... | collective-permute-start | bytes 307208 | tf_op jit(solution)/shard_map/ppermute | solution.py:181
  8.1 7.9 %collective-permute-start.1 = (f32[200,128]{1,0:T(8,128)}, f32[200,128]{1,0:T(8,128)S(1)}, u32[]{:S(2)}, u32[]{:S(2)}) collective-permute-start(f32[200,128]{1,0:T(8,128)} %shard_map.59.refs_0_.refs_4_), channel_id=1, source_target_pairs={{0,2},{1,3},{2,0},{3,1},{4,6},{5,7},{6,4},{7,5},{8,10},{9,11},{10,... | collective-permute-start | bytes 307208 | tf_op jit(solution)/shard_map/ppermute | solution.py:181
  11.2 4.8 %collective-permute-start = (f32[200,128]{1,0:T(8,128)}, f32[200,128]{1,0:T(8,128)S(1)}, u32[]{:S(2)}, u32[]{:S(2)}) collective-permute-start(f32[200,128]{1,0:T(8,128)} %shard_map.59.refs_0_.refs_4_), channel_id=1, source_target_pairs={{0,1},{1,0},{2,3},{3,2},{4,5},{5,4},{6,7},{7,6},{8,9},{9,8},{10,11... | collective-permute-start | bytes 307208 | tf_op jit(solution)/shard_map/ppermute | solution.py:181
  16.0 0.9 %copy-start = (f32[200,128]{1,0:T(8,128)S(1)}, f32[200,128]{1,0:T(8,128)}, u32[]{:S(2)}) copy-start(f32[200,128]{1,0:T(8,128)} %shard_map.59.refs_0_.refs_4_) | copy-start | bytes 307204
  21.8 1.5 %collective-permute-start.6 = (f32[64,768]{1,0:T(8,128)S(1)}, f32[64,768]{1,0:T(8,128)S(1)}, u32[]{:S(2)}, u32[]{:S(2)}) collective-permute-start(f32[64,768]{1,0:T(8,128)S(1)} %get-tuple-element.5), channel_id=1, source_target_pairs={{0,1},{1,0},{2,3},{3,2},{4,5},{5,4},{6,7},{7,6},{8,9},{9,8},{10,11... | collective-permute-start | bytes 589832 | tf_op jit(solution)/shard_map/ppermute | solution.py:181
  23.3 4.9 %collective-permute-start.7 = (f32[64,384]{1,0:T(8,128)S(1)}, f32[64,384]{1,0:T(8,128)S(1)}, u32[]{:S(2)}, u32[]{:S(2)}) collective-permute-start(f32[64,384]{1,0:T(8,128)S(1)} %slice_add_fusion), channel_id=1, source_target_pairs={{0,2},{1,3},{2,0},{3,1},{4,6},{5,7},{6,4},{7,5},{8,10},{9,11},{10,... | collective-permute-start | bytes 294920 | tf_op jit(solution)/shard_map/ppermute | solution.py:181

commit v2 on v1

v2 whole, which is shorter than its diff:
```python
import functools
import math

import jax
import jax.numpy as jnp
from jax import lax
from jax.experimental import pallas as pl
from jax.experimental.pallas import tpu as pltpu
from jax.sharding import PartitionSpec as P

SCALE = math.log2(math.e) / 0.1
LANES = 128
f32 = jnp.float32
bf16 = jnp.bfloat16


def split(value):
    high = value.astype(bf16).astype(f32)
    return high, value - high


def pack_kernel(slabs, feats, src_ref, srcp_ref, tgt_ref, tgtp_ref, out_ref):
    src_slabs = src_ref.shape[1] // LANES
    out_ref[slabs * feats :, :] = jnp.zeros((out_ref.shape[0] - slabs * feats, LANES), f32)
    for slab in range(slabs):
        ref, pot, at = (src_ref, srcp_ref, slab) if slab < src_slabs else (tgt_ref, tgtp_ref, slab - src_slabs)
        cols = slice(at * LANES, (at + 1) * LANES)
        out_ref[slab * feats : (slab + 1) * feats, :] = ref[:, cols]
        for which in range(2):
            row = slabs * feats + which * slabs + slab
            out_ref[row : row + 1, :] = pot[which : which + 1, cols]


def pair_kernel(shape, num_rows, num_cols, own, totals, *refs):
    feats, src_slabs, tgt_slabs = shape
    slabs = src_slabs + tgt_slabs
    rows, cols = refs[:num_rows], refs[num_rows : num_rows + num_cols]
    prev = refs[num_rows + num_cols : -num_rows - 2]
    outs, lhs_ref, rvec_ref = refs[-num_rows - 2 : -2], refs[-2], refs[-1]

    def cell_terms(ref, slab):
        value = ref[slab * feats : (slab + 1) * feats, :]
        norm = 0.5 * jnp.sum(value * value, 0, keepdims=True)
        first = slabs * feats + slab
        pots = [SCALE * (ref[first + which * slabs : first + which * slabs + 1, :] - norm) for which in range(2)]
        return value, pots

    row_slabs = [(row, slab) for row in range(num_rows) for slab in range(src_slabs)]
    src_width = len(row_slabs) * LANES
    row_slabs += [(row, slab) for row in range(num_rows) for slab in range(src_slabs, slabs)]
    for place, (row, slab) in enumerate(row_slabs):
        value, pots = cell_terms(rows[row], slab)
        high, low = split(value * SCALE)
        high, low = high.astype(bf16), low.astype(bf16)
        at = slice(place * LANES, (place + 1) * LANES)
        lhs_ref[0:feats, at] = high
        lhs_ref[feats : 2 * feats, at] = high
        lhs_ref[2 * feats : 3 * feats, at] = low
        lhs_ref[3 * feats :, at] = low
        for which in range(2):
            rvec_ref[which : which + 1, at] = pots[which]

    prepared = []
    for kind, first, last in ((0, 0, src_slabs), (1, src_slabs, slabs)):
        of_kind = [(col, slab) for col in range(num_cols) for slab in range(first, last)]
        for begin in range(0, len(of_kind), 2):
            members = of_kind[begin : begin + 2]
            trans, values, vecs = [], [], []
            for col, slab in members:
                value, pots = cell_terms(cols[col], slab)
                high, low = split(value)
                mid, least = split(low)
                both = jnp.concatenate([high, low], 0).T.astype(bf16)
                trans.append(jnp.concatenate([both, both], 1))
                stack = jnp.concatenate([high, mid, least, jnp.ones((16, LANES), f32)], 0)
                values.append(stack.astype(bf16))
                vecs.append(jnp.concatenate(pots + [jnp.zeros((6, LANES), f32)], 0).T)
            value = jnp.concatenate(values, 1)
            value = jnp.concatenate([value, value], 1)
            prepared.append((kind, members, jnp.concatenate(trans, 0), value, jnp.concatenate(vecs, 0)))

    begin = 0
    while begin < len(row_slabs):
        row_kind = 0 if begin * LANES < src_width else 1
        tile = row_slabs[begin : begin + 2]
        at = slice(begin * LANES, (begin + len(tile)) * LANES)
        begin += len(tile)
        sums = [None, None]
        for kind, members, trans, value, vecs in prepared:
            which = 1 if kind == row_kind else 0
            power = jnp.dot(trans, lhs_ref[:, at], preferred_element_type=f32)
            power = power + (rvec_ref[which : which + 1, at] + vecs[:, which : which + 1])
            weight = jnp.exp2(power)
            if own and kind == row_kind:
                for down, member in enumerate(members):
                    for across, other in enumerate(tile):
                        if member == other and member[0] == 0:
                            row_id = lax.broadcasted_iota(jnp.int32, weight.shape, 0) - down * LANES
                            col_id = lax.broadcasted_iota(jnp.int32, weight.shape, 1) - across * LANES
                            same = (row_id == col_id) & (row_id >= 0) & (row_id < LANES)
                            weight = jnp.where(same, 0.0, weight)
            high, low = split(weight)
            both = jnp.concatenate([high.astype(bf16), low.astype(bf16)], 0)
            part = jnp.dot(value, both, preferred_element_type=f32)
            sums[kind] = part if sums[kind] is None else sums[kind] + part
        sign = 1.0 if row_kind == 0 else -1.0
        total = sums[1] * (sign / totals[1]) - sums[0] * (sign / totals[0])
        mixed = total[0:feats] + total[feats : 2 * feats] + total[2 * feats : 3 * feats]
        mass = total[3 * feats : 3 * feats + 1]
        for across, (row, slab) in enumerate(tile):
            piece = slice(across * LANES, (across + 1) * LANES)
            value = rows[row][slab * feats : (slab + 1) * feats, :]
            grad = value * mass[:, piece] - mixed[:, piece]
            spot = slice(slab * LANES, (slab + 1) * LANES)
            if prev:
                grad = grad + prev[row][:, spot]
            outs[row][:, spot] = grad


def pair_terms(rows, cols, prev, own, shape, totals, cost=0):
    feats, src_slabs, tgt_slabs = shape
    width = (src_slabs + tgt_slabs) * LANES
    vmem = pl.BlockSpec(memory_space=pltpu.VMEM)
    args = [*rows, *cols, *prev]
    pairs = len(rows) * len(cols) * width**2
    return pl.pallas_call(
        functools.partial(pair_kernel, shape, len(rows), len(cols), own, totals),
        out_shape=[jax.ShapeDtypeStruct((feats, width), f32)] * len(rows),
        in_specs=[vmem] * len(args),
        out_specs=[vmem] * len(rows),
        scratch_shapes=[
            pltpu.VMEM((4 * feats, len(rows) * width), bf16),
            pltpu.VMEM((8, len(rows) * width), f32),
        ],
        compiler_params=pltpu.CompilerParams(vmem_limit_bytes=32 * 2**20),
        cost_estimate=pl.CostEstimate(flops=cost, bytes_accessed=2**20, transcendentals=0),
    )(*args)


def finish_kernel(mine_ref, near_ref, far_ref, src_ref, tgt_ref):
    count = src_ref.shape[1]
    src_ref[...] = mine_ref[:, :count] + near_ref[:, :count] + far_ref[:, :count]
    tgt_ref[...] = mine_ref[:, count:] + near_ref[:, count:] + far_ref[:, count:]


def body(src_latent, src_potential, tgt_latent, tgt_potential):
    feats, src_count = src_latent.shape
    tgt_count = tgt_latent.shape[1]
    src_slabs, tgt_slabs = src_count // LANES, tgt_count // LANES
    shape = (feats, src_slabs, tgt_slabs)
    slabs = src_slabs + tgt_slabs
    devices = lax.axis_size("src")
    totals = (src_count * devices, tgt_count * devices)
    pot_rows = -(-2 * slabs // 8) * 8
    vmem = pl.BlockSpec(memory_space=pltpu.VMEM)
    packed = pl.pallas_call(
        functools.partial(pack_kernel, slabs, feats),
        out_shape=jax.ShapeDtypeStruct((slabs * feats + pot_rows, LANES), f32),
        in_specs=[vmem] * 4,
        out_specs=vmem,
    )(src_latent, src_potential, tgt_latent, tgt_potential)

    def swap(value, bits):
        return lax.ppermute(value, "src", [(i, i ^ bits) for i in range(devices)])

    def terms(rows, cols, prev, own=False, cost=0):
        return pair_terms(rows, cols, prev, own, shape, totals, cost)

    across = swap(packed, 2)
    beside = swap(packed, 1)
    from_z = {k: swap(packed, k) for k in range(4, devices, 4)}
    rows = [packed, beside, across, swap(across, 1)]
    arrival = sorted(from_z, key=lambda k: (k % 8 == 0, -k))
    partial = terms(rows[:2], [packed], (), True, 10**10) + terms(rows[2:], [packed], ())
    partial = terms(rows, [from_z[arrival[0]]], partial)
    for k in arrival[1:-1]:
        partial = terms(rows, [from_z[k]], partial)
    last = from_z[arrival[-1]]
    to_across, to_corner = terms(rows[2:], [last], partial[2:])
    corner = swap(to_corner, 1)
    mine, to_beside = terms(rows[:2], [last], partial[:2])
    far = swap(to_across + corner, 2)
    near = swap(to_beside, 1)
    return pl.pallas_call(
        finish_kernel,
        out_shape=[jax.ShapeDtypeStruct(src_latent.shape, f32), jax.ShapeDtypeStruct(tgt_latent.shape, f32)],
        in_specs=[vmem] * 3,
        out_specs=[vmem] * 2,
        compiler_params=pltpu.CompilerParams(vmem_limit_bytes=4 * 2**20),
    )(mine, near, far)


def solution(mesh):
    spec = P(None, ("groups", "src"))
    return jax.shard_map(body, mesh=mesh, in_specs=(spec,) * 4, out_specs=(spec, spec), check_vma=False)
```

time: 29.7 us -> 27 us (0.909)
  waiting for transfers between devices: 11.3 us -> 5.18 us
  Pallas kernels: 6.35 us -> 11.4 us
  local copies, waits for them, and re-layouts: 2.14 us -> 0.91 us
  starting transfers between devices: 8.99 us -> 8.57 us
    ppermute x8 -> x9, waiting for transfers between devices: 11.3 us -> 5.18 us  [swap(): return lax.ppermute(value, 'src', [(i, i ^ bits) for i in range(devices)])]
    pallas_call x1 -> x6, Pallas kernels: 4.84 us -> 9.2 us  [pair_terms(): pl.pallas_call(functools.partial(pair_kernel, shape, len(rows), len(cols)...]
    slice x2 -> x0, local copies, waits for them, and re-layouts: 1.25 us -> none  [body(): return (grad[:, :src_count], grad[:, src_count:])]
    pallas_call x0 -> x1, Pallas kernels: none -> 0.66 us  [body(): pl.pallas_call(finish_kernel, out_shape=[jax.ShapeDtypeStruct(src_latent....]
    ppermute x8 -> x9, starting transfers between devices: 8.99 us -> 8.57 us  [swap(): return lax.ppermute(value, 'src', [(i, i ^ bits) for i in range(devices)])]
    unnamed x2 -> x4, local copies, waits for them, and re-layouts: 0.89 us -> 0.91 us
  transfers between devices with their start and end apart: 8 -> 9, of which waited for: 4 -> 4; matrix products, arithmetic and copies ran while one was open for 0% -> 0% of each run, Pallas kernels for 0% -> 30%
where the time goes in v2:
time: 27 us; the launch traced here: 26.8 us
  Pallas kernels  11.4 us (42%)
  starting transfers between devices  8.57 us (32%)
  waiting for transfers between devices  5.18 us (19%)
  local copies, waits for them, and re-layouts  0.91 us (3%)
  between operations  0.73 us (3%)
    pallas_call x6, Pallas kernels, pair_terms(): pl.pallas_call(functools.partial(pair_kernel, shape, len(rows), len(cols)...  9.2 us
    ppermute x9, starting transfers between devices, swap(): return lax.ppermute(value, 'src', [(i, i ^ bits) for i in range(devices)])  8.57 us
    ppermute x9, waiting for transfers between devices, swap(): return lax.ppermute(value, 'src', [(i, i ^ bits) for i in range(devices)])  5.18 us
    pallas_call x1, Pallas kernels, body(): pl.pallas_call(functools.partial(pack_kernel, slabs, feats), out_shape=ja...  1.53 us
    unnamed x4, local copies, waits for them, and re-layouts  0.91 us
    pallas_call x1, Pallas kernels, body(): pl.pallas_call(finish_kernel, out_shape=[jax.ShapeDtypeStruct(src_latent....  0.66 us
  transfers between devices with their start and end apart: 9, of which 4 were waited for; matrix products, arithmetic and copies ran while one was open for 0% of the time, Pallas kernels for 30%

profile of v2, /device:TPU:0, one launch (start us, length us, event | category | flops | bytes accessed | tf_op | source)
XLA Modules:
  0.0 26.8 jit_solution(11927611408912154808)
XLA Ops:
  0.6 1.5 %shard_map.59.refs_0_.refs_2_ = f32[200,128]{1,0:T(8,128)} custom-call(f32[64,256]{1,0:T(8,128)} %src_ref.1, f32[2,256]{1,0:T(2,128)} %srcp_ref.1, f32[64,128]{1,0:T(8,128)} %tgt_ref.1, f32[2,128]{1,0:T(2,128)} %tgtp_ref.1), custom_call_target="tpu_custom_call" | custom-call | tf_op jit(solution)/shard_map/pallas_call | solution.py:156
  2.2 2.9 %collective-permute-start.2 = (f32[200,128]{1,0:T(8,128)}, f32[200,128]{1,0:T(8,128)S(1)}, u32[]{:S(2)}, u32[]{:S(2)}) collective-permute-start(f32[200,128]{1,0:T(8,128)} %shard_map.59.refs_0_.refs_2_), channel_id=1, source_target_pairs={{0,2},{1,3},{2,0},{3,1},{4,6},{5,7},{6,4},{7,5},{8,10},{9,11},{10,... | collective-permute-start | bytes 307208 | tf_op jit(solution)/shard_map/ppermute | solution.py:164
  5.1 0.0 collective-permute-start
  5.1 3.6 %collective-permute-start.5 = (f32[200,128]{1,0:T(8,128)}, f32[200,128]{1,0:T(8,128)S(1)}, u32[]{:S(2)}, u32[]{:S(2)}) collective-permute-start(f32[200,128]{1,0:T(8,128)} %shard_map.59.refs_0_.refs_2_), channel_id=1, source_target_pairs={{0,12},{1,13},{2,14},{3,15},{4,8},{5,9},{6,10},{7,11},{8,4},{9,5},... | collective-permute-start | bytes 307208 | tf_op jit(solution)/shard_map/ppermute | solution.py:164
  8.7 0.0 collective-permute-start.4
  8.7 0.8 %collective-permute-start.1 = (f32[200,128]{1,0:T(8,128)}, f32[200,128]{1,0:T(8,128)S(1)}, u32[]{:S(2)}, u32[]{:S(2)}) collective-permute-start(f32[200,128]{1,0:T(8,128)} %shard_map.59.refs_0_.refs_2_), channel_id=1, source_target_pairs={{0,8},{1,9},{2,10},{3,11},{4,12},{5,13},{6,14},{7,15},{8,0},{9,1},... | collective-permute-start | bytes 307208 | tf_op jit(solution)/shard_map/ppermute | solution.py:164
  9.5 0.0 collective-permute-done.2.refs_0_.refs_2_
  9.5 0.0 collective-permute-start.3
  9.5 0.0 collective-permute-done.refs_1_
  9.5 0.0 copy-start
  9.5 0.9 %copy-done = f32[200,128]{1,0:T(8,128)S(1)} copy-done((f32[200,128]{1,0:T(8,128)S(1)}, f32[200,128]{1,0:T(8,128)}, u32[]{:S(2)}) %copy-start) | copy-done | bytes 102424
  10.4 0.0 copy-start.1
  10.4 1.2 %shard_map.60 = (f32[64,384]{1,0:T(8,128)S(1)}, f32[64,384]{1,0:T(8,128)S(1)}) custom-call(f32[200,128]{1,0:T(8,128)S(1)} %copy-done, f32[200,128]{1,0:T(8,128)S(1)} %collective-permute-done.refs_1_, f32[200,128]{1,0:T(8,128)S(1)} %copy-done), custom_call_target="tpu_custom_call" | custom-call | flops 10000000000 | bytes 1048576 | tf_op jit(solution)/shard_map/pallas_call | solution.py:126
  11.6 0.0 collective-permute-done.3.refs_1_.refs_3_
  11.7 0.0 copy-done.1
  11.7 1.2 %shard_map.61 = (f32[64,384]{1,0:T(8,128)S(1)}, f32[64,384]{1,0:T(8,128)S(1)}) custom-call(f32[200,128]{1,0:T(8,128)S(1)} %collective-permute-done.2.refs_0_.refs_2_, f32[200,128]{1,0:T(8,128)S(1)} %collective-permute-done.3.refs_1_.refs_3_, f32[200,128]{1,0:T(8,128)S(1)} %copy-done.1), custom_call_target="tpu_custom_call" | custom-call | bytes 1048576 | tf_op jit(solution)/shard_map/pallas_call | solution.py:126
  12.9 0.0 collective-permute-done.5.refs_4_
  12.9 2.1 %shard_map.62 = (f32[64,384]{1,0:T(8,128)S(1)}, f32[64,384]{1,0:T(8,128)S(1)}, f32[64,384]{1,0:T(8,128)S(1)}, f32[64,384]{1,0:T(8,128)S(1)}) custom-call(f32[200,128]{1,0:T(8,128)S(1)} %copy-done.1, f32[200,128]{1,0:T(8,128)S(1)} %collective-permute-done.refs_1_, f32[200,128]{1,0:T(8,128)S(1)} %collective-permute-done.2.refs_0_.refs_2_, ...), custom_call_target="tpu_custom_call" | custom-call | bytes 1048576 | tf_op jit(solution)/shard_map/pallas_call | solution.py:126
  15.1 0.7 %collective-permute-done.4.refs_4_ = f32[200,128]{1,0:T(8,128)S(1)} collective-permute-done((f32[200,128]{1,0:T(8,128)}, f32[200,128]{1,0:T(8,128)S(1)}, u32[]{:S(2)}, u32[]{:S(2)}) %collective-permute-start.4) | collective-permute-done | bytes 102432 | tf_op jit(solution)/shard_map/ppermute | solution.py:164
  15.8 2.1 %shard_map.63 = (f32[64,384]{1,0:T(8,128)S(1)}, f32[64,384]{1,0:T(8,128)S(1)}, f32[64,384]{1,0:T(8,128)S(1)}, f32[64,384]{1,0:T(8,128)S(1)}) custom-call(f32[200,128]{1,0:T(8,128)S(1)} %copy-done.1, f32[200,128]{1,0:T(8,128)S(1)} %collective-permute-done.refs_1_, f32[200,128]{1,0:T(8,128)S(1)} %collective-permute-done.2.refs_0_.refs_2_, ...), custom_call_target="tpu_custom_call" | custom-call | bytes 1048576 | tf_op jit(solution)/shard_map/pallas_call | solution.py:126
  17.9 0.3 %collective-permute-done.1.refs_2_ = f32[200,128]{1,0:T(8,128)S(1)} collective-permute-done((f32[200,128]{1,0:T(8,128)}, f32[200,128]{1,0:T(8,128)S(1)}, u32[]{:S(2)}, u32[]{:S(2)}) %collective-permute-start.1) | collective-permute-done | bytes 102432 | tf_op jit(solution)/shard_map/ppermute | solution.py:164
  18.2 1.2 %shard_map.65 = (f32[64,384]{1,0:T(8,128)S(1)}, f32[64,384]{1,0:T(8,128)S(1)}) custom-call(f32[200,128]{1,0:T(8,128)S(1)} %collective-permute-done.2.refs_0_.refs_2_, f32[200,128]{1,0:T(8,128)S(1)} %collective-permute-done.3.refs_1_.refs_3_, f32[200,128]{1,0:T(8,128)S(1)} %collective-permute-done.1.refs_2_, f32[64,384]{1,0:T(8,128)S(1)} %get-tuple-element.30.refs_3_, ...), custom_call_target="tpu_custom_call" | custom-call | bytes 1048576 | tf_op jit(solution)/shard_map/pallas_call | solution.py:126
  19.4 0.1 collective-permute-start.7
  19.5 1.2 %shard_map.64 = (f32[64,384]{1,0:T(8,128)S(1)}, f32[64,384]{1,0:T(8,128)S(1)}) custom-call(f32[200,128]{1,0:T(8,128)S(1)} %copy-done.1, f32[200,128]{1,0:T(8,128)S(1)} %collective-permute-done.refs_1_, f32[200,128]{1,0:T(8,128)S(1)} %collective-permute-done.1.refs_2_, f32[64,384]{1,0:T(8,128)S(1)} %get-tuple-element.26.refs_3_, ...), custom_call_target="tpu_custom_call" | custom-call | bytes 1048576 | tf_op jit(solution)/shard_map/pallas_call | solution.py:126
  20.8 0.6 %collective-permute-start.6 = (f32[64,384]{1,0:T(8,128)S(1)}, f32[64,384]{1,0:T(8,128)S(1)}, u32[]{:S(2)}, u32[]{:S(2)}) collective-permute-start(f32[64,384]{1,0:T(8,128)S(1)} %get-tuple-element.29), channel_id=1, source_target_pairs={{0,1},{1,0},{2,3},{3,2},{4,5},{5,4},{6,7},{7,6},{8,9},{9,8},{10,11... | collective-permute-start | bytes 294920 | tf_op jit(solution)/shard_map/ppermute | solution.py:164
  21.3 0.0 collective-permute-done.7
  21.3 0.6 %collective-permute-start.8 = (f32[64,384]{1,0:T(8,128)S(1)}, f32[64,384]{1,0:T(8,128)S(1)}, u32[]{:S(2)}, u32[]{:S(2)}) collective-permute-start(f32[64,384]{1,0:T(8,128)S(1)} %add.3), channel_id=1, source_target_pairs={{0,2},{1,3},{2,0},{3,1},{4,6},{5,7},{6,4},{7,5},{8,10},{9,11},{10,... | collective-permute-start | bytes 294920 | tf_op jit(solution)/shard_map/ppermute | solution.py:164
  21.9 0.3 %collective-permute-done.6.near_ref = f32[64,384]{1,0:T(8,128)S(1)} collective-permute-done((f32[64,384]{1,0:T(8,128)S(1)}, f32[64,384]{1,0:T(8,128)S(1)}, u32[]{:S(2)}, u32[]{:S(2)}) %collective-permute-start.6) | collective-permute-done | bytes 98336 | tf_op jit(solution)/shard_map/ppermute | solution.py:164
  22.3 3.9 %collective-permute-done.8.far_ref = f32[64,384]{1,0:T(8,128)S(1)} collective-permute-done((f32[64,384]{1,0:T(8,128)S(1)}, f32[64,384]{1,0:T(8,128)S(1)}, u32[]{:S(2)}, u32[]{:S(2)}) %collective-permute-start.8) | collective-permute-done | bytes 98336 | tf_op jit(solution)/shard_map/ppermute | solution.py:164
  26.1 0.7 %shard_map.66 = (f32[64,256]{1,0:T(8,128)}, f32[64,128]{1,0:T(8,128)}) custom-call(f32[64,384]{1,0:T(8,128)S(1)} %get-tuple-element.28.mine_ref, f32[64,384]{1,0:T(8,128)S(1)} %collective-permute-done.6.near_ref, f32[64,384]{1,0:T(8,128)S(1)} %collective-permute-done.8.far_ref), custom_call_target="tpu_custom_call" | custom-call | tf_op jit(solution)/shard_map/pallas_call | solution.py:184
  (1 shorter events, 0.0 us)
Async XLA Ops:
  2.2 7.3 %collective-permute-start.2 = (f32[200,128]{1,0:T(8,128)}, f32[200,128]{1,0:T(8,128)S(1)}, u32[]{:S(2)}, u32[]{:S(2)}) collective-permute-start(f32[200,128]{1,0:T(8,128)} %shard_map.59.refs_0_.refs_2_), channel_id=1, source_target_pairs={{0,2},{1,3},{2,0},{3,1},{4,6},{5,7},{6,4},{7,5},{8,10},{9,11},{10,... | collective-permute-start | bytes 307208 | tf_op jit(solution)/shard_map/ppermute | solution.py:164
  5.1 4.4 %collective-permute-start = (f32[200,128]{1,0:T(8,128)}, f32[200,128]{1,0:T(8,128)S(1)}, u32[]{:S(2)}, u32[]{:S(2)}) collective-permute-start(f32[200,128]{1,0:T(8,128)} %shard_map.59.refs_0_.refs_2_), channel_id=1, source_target_pairs={{0,1},{1,0},{2,3},{3,2},{4,5},{5,4},{6,7},{7,6},{8,9},{9,8},{10,11... | collective-permute-start | bytes 307208 | tf_op jit(solution)/shard_map/ppermute | solution.py:164
  5.1 7.8 %collective-permute-start.5 = (f32[200,128]{1,0:T(8,128)}, f32[200,128]{1,0:T(8,128)S(1)}, u32[]{:S(2)}, u32[]{:S(2)}) collective-permute-start(f32[200,128]{1,0:T(8,128)} %shard_map.59.refs_0_.refs_2_), channel_id=1, source_target_pairs={{0,12},{1,13},{2,14},{3,15},{4,8},{5,9},{6,10},{7,11},{8,4},{9,5},... | collective-permute-start | bytes 307208 | tf_op jit(solution)/shard_map/ppermute | solution.py:164
  8.7 7.1 %collective-permute-start.4 = (f32[200,128]{1,0:T(8,128)}, f32[200,128]{1,0:T(8,128)S(1)}, u32[]{:S(2)}, u32[]{:S(2)}) collective-permute-start(f32[200,128]{1,0:T(8,128)} %shard_map.59.refs_0_.refs_2_), channel_id=1, source_target_pairs={{0,4},{1,5},{2,6},{3,7},{4,0},{5,1},{6,2},{7,3},{8,12},{9,13},{10,... | collective-permute-start | bytes 307208 | tf_op jit(solution)/shard_map/ppermute | solution.py:164
  8.7 9.5 %collective-permute-start.1 = (f32[200,128]{1,0:T(8,128)}, f32[200,128]{1,0:T(8,128)S(1)}, u32[]{:S(2)}, u32[]{:S(2)}) collective-permute-start(f32[200,128]{1,0:T(8,128)} %shard_map.59.refs_0_.refs_2_), channel_id=1, source_target_pairs={{0,8},{1,9},{2,10},{3,11},{4,12},{5,13},{6,14},{7,15},{8,0},{9,1},... | collective-permute-start | bytes 307208 | tf_op jit(solution)/shard_map/ppermute | solution.py:164
  9.5 2.2 %collective-permute-start.3 = (f32[200,128]{1,0:T(8,128)S(1)}, f32[200,128]{1,0:T(8,128)S(1)}, u32[]{:S(2)}, u32[]{:S(2)}) collective-permute-start(f32[200,128]{1,0:T(8,128)S(1)} %collective-permute-done.2.refs_0_.refs_2_), channel_id=1, source_target_pairs={{0,1},{1,0},{2,3},{3,2},{4,5},{5,4},{6,7},{7,6},{8,9},{9,8},{10,11... | collective-permute-start | bytes 307208 | tf_op jit(solution)/shard_map/ppermute | solution.py:164
  9.5 0.9 %copy-start = (f32[200,128]{1,0:T(8,128)S(1)}, f32[200,128]{1,0:T(8,128)}, u32[]{:S(2)}) copy-start(f32[200,128]{1,0:T(8,128)} %shard_map.59.refs_0_.refs_2_) | copy-start | bytes 307204
  10.4 1.2 %copy-start.1 = (f32[200,128]{1,0:T(8,128)S(1)}, f32[200,128]{1,0:T(8,128)}, u32[]{:S(2)}) copy-start(f32[200,128]{1,0:T(8,128)} %shard_map.59.refs_0_.refs_2_) | copy-start | bytes 307204
  19.4 1.9 %collective-permute-start.7 = (f32[64,384]{1,0:T(8,128)S(1)}, f32[64,384]{1,0:T(8,128)S(1)}, u32[]{:S(2)}, u32[]{:S(2)}) collective-permute-start(f32[64,384]{1,0:T(8,128)S(1)} %get-tuple-element.33), channel_id=1, source_target_pairs={{0,1},{1,0},{2,3},{3,2},{4,5},{5,4},{6,7},{7,6},{8,9},{9,8},{10,11... | collective-permute-start | bytes 294920 | tf_op jit(solution)/shard_map/ppermute | solution.py:164
  20.8 1.5 %collective-permute-start.6 = (f32[64,384]{1,0:T(8,128)S(1)}, f32[64,384]{1,0:T(8,128)S(1)}, u32[]{:S(2)}, u32[]{:S(2)}) collective-permute-start(f32[64,384]{1,0:T(8,128)S(1)} %get-tuple-element.29), channel_id=1, source_target_pairs={{0,1},{1,0},{2,3},{3,2},{4,5},{5,4},{6,7},{7,6},{8,9},{9,8},{10,11... | collective-permute-start | bytes 294920 | tf_op jit(solution)/shard_map/ppermute | solution.py:164
  21.3 4.8 %collective-permute-start.8 = (f32[64,384]{1,0:T(8,128)S(1)}, f32[64,384]{1,0:T(8,128)S(1)}, u32[]{:S(2)}, u32[]{:S(2)}) collective-permute-start(f32[64,384]{1,0:T(8,128)S(1)} %add.3), channel_id=1, source_target_pairs={{0,2},{1,3},{2,0},{3,1},{4,6},{5,7},{6,4},{7,5},{8,10},{9,11},{10,... | collective-permute-start | bytes 294920 | tf_op jit(solution)/shard_map/ppermute | solution.py:164

commit v3 on v2

v3 whole, which is shorter than its diff:
```python
import functools
import math

import jax
import jax.numpy as jnp
from jax import lax
from jax.experimental import pallas as pl
from jax.experimental.pallas import tpu as pltpu
from jax.sharding import PartitionSpec as P

SCALE = math.log2(math.e) / 0.1
LANES = 128
f32 = jnp.float32
bf16 = jnp.bfloat16


def split(value):
    high = value.astype(bf16).astype(f32)
    return high, value - high


def pack_kernel(slabs, feats, src_ref, srcp_ref, tgt_ref, tgtp_ref, out_ref):
    src_slabs = src_ref.shape[1] // LANES
    out_ref[slabs * feats :, :] = jnp.zeros((out_ref.shape[0] - slabs * feats, LANES), f32)
    for slab in range(slabs):
        ref, pot, at = (src_ref, srcp_ref, slab) if slab < src_slabs else (tgt_ref, tgtp_ref, slab - src_slabs)
        cols = slice(at * LANES, (at + 1) * LANES)
        out_ref[slab * feats : (slab + 1) * feats, :] = ref[:, cols]
        for which in range(2):
            row = slabs * feats + which * slabs + slab
            out_ref[row : row + 1, :] = pot[which : which + 1, cols]


def pair_kernel(shape, num_rows, num_cols, jobs, totals, prev_rows, joined, *refs):
    feats, src_slabs, tgt_slabs = shape
    slabs = src_slabs + tgt_slabs
    rows, cols = refs[:num_rows], refs[num_rows : num_rows + num_cols]
    num_outs = 1 if joined else num_rows
    prev = refs[num_rows + num_cols : -num_outs - 2]
    outs, lhs_ref, rvec_ref = refs[-num_outs - 2 : -2], refs[-2], refs[-1]
    if joined:
        width = slabs * LANES
        outs = [outs[0].at[:, row * width : (row + 1) * width] for row in range(num_rows)]
    sums_so_far = dict(zip(prev_rows, prev))

    def cell_terms(ref, slab):
        value = ref[slab * feats : (slab + 1) * feats, :]
        norm = 0.5 * jnp.sum(value * value, 0, keepdims=True)
        first = slabs * feats + slab
        pots = [SCALE * (ref[first + which * slabs : first + which * slabs + 1, :] - norm) for which in range(2)]
        return value, pots

    row_slabs = [(row, slab) for row in range(num_rows) for slab in range(src_slabs)]
    row_slabs += [(row, slab) for row in range(num_rows) for slab in range(src_slabs, slabs)]
    for place, (row, slab) in enumerate(row_slabs):
        value, pots = cell_terms(rows[row], slab)
        high, low = split(value * SCALE)
        high, low = high.astype(bf16), low.astype(bf16)
        at = slice(place * LANES, (place + 1) * LANES)
        lhs_ref[0:feats, at] = high
        lhs_ref[feats : 2 * feats, at] = high
        lhs_ref[2 * feats : 3 * feats, at] = low
        lhs_ref[3 * feats :, at] = low
        for which in range(2):
            rvec_ref[which : which + 1, at] = pots[which]

    @functools.cache
    def prepare(members):
        trans, values, vecs = [], [], []
        for col, slab in members:
            value, pots = cell_terms(cols[col], slab)
            high, low = split(value)
            mid, least = split(low)
            both = jnp.concatenate([high, low], 0).T.astype(bf16)
            trans.append(jnp.concatenate([both, both], 1))
            stack = jnp.concatenate([high, mid, least, jnp.ones((16, LANES), f32)], 0)
            values.append(stack.astype(bf16))
            vecs.append(jnp.concatenate(pots + [jnp.zeros((6, LANES), f32)], 0).T)
        value = jnp.concatenate(values, 1)
        return jnp.concatenate(trans, 0), jnp.concatenate([value, value], 1), jnp.concatenate(vecs, 0)

    def run_tile(tile, prepared, own):
        row_kind = 0 if tile[0][1] < src_slabs else 1
        place = row_slabs.index(tile[0])
        at = slice(place * LANES, (place + len(tile)) * LANES)
        sums = [None, None]
        for kind, members, (trans, value, vecs) in prepared:
            which = 1 if kind == row_kind else 0
            power = jnp.dot(trans, lhs_ref[:, at], preferred_element_type=f32)
            power = power + (rvec_ref[which : which + 1, at] + vecs[:, which : which + 1])
            weight = jnp.exp2(power)
            if own and kind == row_kind:
                for down, member in enumerate(members):
                    for across, other in enumerate(tile):
                        if member == other:
                            row_id = lax.broadcasted_iota(jnp.int32, weight.shape, 0) - down * LANES
                            col_id = lax.broadcasted_iota(jnp.int32, weight.shape, 1) - across * LANES
                            same = (row_id == col_id) & (row_id >= 0) & (row_id < LANES)
                            weight = jnp.where(same, 0.0, weight)
            high, low = split(weight)
            both = jnp.concatenate([high.astype(bf16), low.astype(bf16)], 0)
            part = jnp.dot(value, both, preferred_element_type=f32)
            sums[kind] = part if sums[kind] is None else sums[kind] + part
        sign = 1.0 if row_kind == 0 else -1.0
        total = sums[1] * (sign / totals[1]) - sums[0] * (sign / totals[0])
        mixed = total[0:feats] + total[feats : 2 * feats] + total[2 * feats : 3 * feats]
        mass = total[3 * feats : 3 * feats + 1]
        for across, (row, slab) in enumerate(tile):
            piece = slice(across * LANES, (across + 1) * LANES)
            value = rows[row][slab * feats : (slab + 1) * feats, :]
            grad = value * mass[:, piece] - mixed[:, piece]
            spot = slice(slab * LANES, (slab + 1) * LANES)
            if row in sums_so_far:
                grad = grad + sums_so_far[row][:, spot]
            outs[row][:, spot] = grad

    for job_rows, job_cols, own in jobs:
        prepared = []
        for kind, first, last in ((0, 0, src_slabs), (1, src_slabs, slabs)):
            of_kind = [(col, slab) for col in job_cols for slab in range(first, last)]
            for begin in range(0, len(of_kind), 2):
                members = of_kind[begin : begin + 2]
                prepared.append((kind, members, prepare(tuple(members))))
        for first, last in ((0, src_slabs), (src_slabs, slabs)):
            of_kind = [(row, slab) for row in job_rows for slab in range(first, last)]
            for begin in range(0, len(of_kind), 2):
                run_tile(of_kind[begin : begin + 2], prepared, own)
        for row in job_rows:
            sums_so_far[row] = outs[row]


def pair_terms(shape, totals, rows, cols, prev, jobs, cost=0, joined=False):
    feats, src_slabs, tgt_slabs = shape
    width = (src_slabs + tgt_slabs) * LANES
    vmem = pl.BlockSpec(memory_space=pltpu.VMEM)
    one = jax.ShapeDtypeStruct((feats, width), f32)
    prev_rows = [row for row, value in enumerate(prev) if value is not None]
    args = [*rows, *cols, *[prev[row] for row in prev_rows]]
    return pl.pallas_call(
        functools.partial(pair_kernel, shape, len(rows), len(cols), jobs, totals, prev_rows, joined),
        out_shape=jax.ShapeDtypeStruct((feats, len(rows) * width), f32) if joined else [one] * len(rows),
        in_specs=[vmem] * len(args),
        out_specs=vmem if joined else [vmem] * len(rows),
        scratch_shapes=[
            pltpu.VMEM((4 * feats, len(rows) * width), bf16),
            pltpu.VMEM((8, len(rows) * width), f32),
        ],
        compiler_params=pltpu.CompilerParams(vmem_limit_bytes=32 * 2**20),
        cost_estimate=pl.CostEstimate(flops=cost, bytes_accessed=2**20, transcendentals=0),
    )(*args)


def finish_kernel(mine_ref, near_ref, src_ref, tgt_ref):
    count = src_ref.shape[1]
    src_ref[...] = mine_ref[:, :count] + near_ref[:, :count]
    tgt_ref[...] = mine_ref[:, count:] + near_ref[:, count:]


def body(src_latent, src_potential, tgt_latent, tgt_potential):
    feats, src_count = src_latent.shape
    tgt_count = tgt_latent.shape[1]
    src_slabs, tgt_slabs = src_count // LANES, tgt_count // LANES
    shape = (feats, src_slabs, tgt_slabs)
    slabs = src_slabs + tgt_slabs
    devices = lax.axis_size("src")
    totals = (src_count * devices, tgt_count * devices)
    pot_rows = -(-2 * slabs // 8) * 8
    vmem = pl.BlockSpec(memory_space=pltpu.VMEM)
    packed = pl.pallas_call(
        functools.partial(pack_kernel, slabs, feats),
        out_shape=jax.ShapeDtypeStruct((slabs * feats + pot_rows, LANES), f32),
        in_specs=[vmem] * 4,
        out_specs=vmem,
    )(src_latent, src_potential, tgt_latent, tgt_potential)

    def swap(value, bits):
        return lax.ppermute(value, "src", [(i, i ^ bits) for i in range(devices)])

    terms = functools.partial(pair_terms, shape, totals)
    across = swap(packed, 2)
    beside = swap(packed, 1)
    from_z = {k: swap(packed, k) for k in range(4, devices, 4)}
    arrival = sorted(from_z, key=lambda k: (k % 8 == 0, -k))
    early, middle, last = from_z[arrival[0]], arrival[1:-1], from_z[arrival[-1]]
    near_z = from_z[middle[-1]]
    (mine,) = terms([packed], [packed], [None], [((0,), (0,), True)], 0)
    (mine,) = terms([packed], [early], [mine], [((0,), (0,), False)])
    mine, later, beside = lax.optimization_barrier((mine, across, beside))
    corner = swap(later, 1)
    near, wide = terms([beside, later], [packed, early], [None] * 2, [((0, 1), (0, 1), False)], 10000000000)
    corner, wide = lax.optimization_barrier((corner, wide))
    (sent,) = terms([corner], [packed, early], [None], [((0,), (0, 1), False)], 0)
    wide, sent = terms([across, corner], [near_z], [wide, sent], [((0, 1), (0,), False)])
    for at in range(0, len(middle) - 1, 2):
        group = [from_z[k] for k in middle[at : min(at + 2, len(middle) - 1)]]
        jobs = [((0, 1, 2, 3), tuple(range(len(group))), False)]
        mine, near, wide, sent = terms([packed, beside, across, corner], group, [mine, near, wide, sent], jobs)
    (sent,) = terms([corner], [last], [sent], [((0,), (0,), False)])
    got = swap(sent, 1)
    (wide,) = terms([across], [last], [wide], [((0,), (0,), False)])
    send = wide + got
    far = swap(send, 2)
    last, send = lax.optimization_barrier((last, send))
    mine, near = terms([packed, beside], [near_z, last], [mine, near], [((0, 1), (0, 1), False)])
    near = swap(near, 1)
    mine = mine + far
    return pl.pallas_call(
        finish_kernel,
        out_shape=[jax.ShapeDtypeStruct(src_latent.shape, f32), jax.ShapeDtypeStruct(tgt_latent.shape, f32)],
        in_specs=[vmem] * 2,
        out_specs=[vmem] * 2,
        compiler_params=pltpu.CompilerParams(vmem_limit_bytes=4 * 2**20),
    )(mine, near)


def solution(mesh):
    spec = P(None, ("groups", "src"))
    return jax.shard_map(body, mesh=mesh, in_specs=(spec,) * 4, out_specs=(spec, spec), check_vma=False)
```

time: 27 us -> 25.8 us (0.956)
  waiting for transfers between devices: 5.18 us -> 2.15 us
  Pallas kernels: 11.4 us -> 12.8 us
  starting transfers between devices: 8.57 us -> 8.9 us
    ppermute x9, waiting for transfers between devices: 5.18 us -> 2.15 us  [swap(): return lax.ppermute(value, 'src', [(i, i ^ bits) for i in range(devices)])]
    pallas_call x6 -> x8, Pallas kernels: 9.2 us -> 10.7 us  [pair_terms(): pl.pallas_call(functools.partial(pair_kernel, shape, len(rows), len(cols)...]
    ppermute x9, starting transfers between devices: 8.57 us -> 8.9 us  [swap(): return lax.ppermute(value, 'src', [(i, i ^ bits) for i in range(devices)])]
  transfers between devices with their start and end apart: 9 -> 9, of which waited for: 4 -> 2; matrix products, arithmetic and copies ran while one was open for 0% -> 0% of each run, Pallas kernels for 30% -> 38%
where the time goes in v3:
time: 25.8 us; the launch traced here: 25.6 us
  Pallas kernels  12.8 us (50%)
  starting transfers between devices  8.9 us (34%)
  waiting for transfers between devices  2.15 us (8%)
  local copies, waits for them, and re-layouts  0.93 us (4%)
  between operations  0.79 us (3%)
    pallas_call x8, Pallas kernels, pair_terms(): pl.pallas_call(functools.partial(pair_kernel, shape, len(rows), len(cols)...  10.7 us
    ppermute x9, starting transfers between devices, swap(): return lax.ppermute(value, 'src', [(i, i ^ bits) for i in range(devices)])  8.9 us
    ppermute x9, waiting for transfers between devices, swap(): return lax.ppermute(value, 'src', [(i, i ^ bits) for i in range(devices)])  2.15 us
    pallas_call x1, Pallas kernels, body(): pl.pallas_call(functools.partial(pack_kernel, slabs, feats), out_shape=ja...  1.5 us
    unnamed x4, local copies, waits for them, and re-layouts  0.93 us
    pallas_call x1, Pallas kernels, body(): pl.pallas_call(finish_kernel, out_shape=[jax.ShapeDtypeStruct(src_latent....  0.65 us
  transfers between devices with their start and end apart: 9, of which 2 were waited for; matrix products, arithmetic and copies ran while one was open for 0% of the time, Pallas kernels for 38%

profile of v3, /device:TPU:0, one launch (start us, length us, event | category | flops | bytes accessed | tf_op | source)
XLA Modules:
  0.0 25.6 jit_solution(12442977354937331767)
XLA Ops:
  0.6 1.5 %shard_map.59.refs_0_.refs_1_.refs_2_ = f32[200,128]{1,0:T(8,128)} custom-call(f32[64,256]{1,0:T(8,128)} %src_ref.1, f32[2,256]{1,0:T(2,128)} %srcp_ref.1, f32[64,128]{1,0:T(8,128)} %tgt_ref.1, f32[2,128]{1,0:T(2,128)} %tgtp_ref.1), custom_call_target="tpu_custom_call" | custom-call | tf_op jit(solution)/shard_map/pallas_call | solution.py:169
  2.1 5.0 %collective-permute-start = (f32[200,128]{1,0:T(8,128)}, f32[200,128]{1,0:T(8,128)S(1)}, u32[]{:S(2)}, u32[]{:S(2)}) collective-permute-start(f32[200,128]{1,0:T(8,128)} %shard_map.59.refs_0_.refs_1_.refs_2_), channel_id=1, source_target_pairs={{0,12},{1,13},{2,14},{3,15},{4,8},{5,9},{6,10},{7,11},{8,4},{9,5},... | collective-permute-start | bytes 307208 | tf_op jit(solution)/shard_map/ppermute | solution.py:177
  7.2 1.5 %collective-permute-start.1 = (f32[200,128]{1,0:T(8,128)}, f32[200,128]{1,0:T(8,128)S(1)}, u32[]{:S(2)}, u32[]{:S(2)}) collective-permute-start(f32[200,128]{1,0:T(8,128)} %shard_map.59.refs_0_.refs_1_.refs_2_), channel_id=1, source_target_pairs={{0,2},{1,3},{2,0},{3,1},{4,6},{5,7},{6,4},{7,5},{8,10},{9,11},{10,... | collective-permute-start | bytes 307208 | tf_op jit(solution)/shard_map/ppermute | solution.py:177
  8.7 0.0 collective-permute-start.2
  8.7 0.0 collective-permute-start.3
  8.7 0.8 %collective-permute-start.4 = (f32[200,128]{1,0:T(8,128)}, f32[200,128]{1,0:T(8,128)S(1)}, u32[]{:S(2)}, u32[]{:S(2)}) collective-permute-start(f32[200,128]{1,0:T(8,128)} %shard_map.59.refs_0_.refs_1_.refs_2_), channel_id=1, source_target_pairs={{0,8},{1,9},{2,10},{3,11},{4,12},{5,13},{6,14},{7,15},{8,0},{9,1},... | collective-permute-start | bytes 307208 | tf_op jit(solution)/shard_map/ppermute | solution.py:177
  9.5 0.0 copy-start
  9.5 0.9 %copy-done = f32[200,128]{1,0:T(8,128)S(1)} copy-done((f32[200,128]{1,0:T(8,128)S(1)}, f32[200,128]{1,0:T(8,128)}, u32[]{:S(2)}) %copy-start) | copy-done | bytes 102424
  10.4 0.0 copy-start.1
  10.4 1.1 %shard_map.60.refs_2_ = f32[64,384]{1,0:T(8,128)S(1)} custom-call(f32[200,128]{1,0:T(8,128)S(1)} %copy-done, f32[200,128]{1,0:T(8,128)S(1)} %copy-done), custom_call_target="tpu_custom_call" | custom-call | bytes 1048576 | tf_op jit(solution)/shard_map/pallas_call | solution.py:139
  11.5 0.0 collective-permute-done.refs_1_.refs_3_.refs_2_
  11.5 0.0 copy-done.1
  11.5 1.1 %shard_map.61.refs_4_ = f32[64,384]{1,0:T(8,128)S(1)} custom-call(f32[200,128]{1,0:T(8,128)S(1)} %copy-done.1, f32[200,128]{1,0:T(8,128)S(1)} %collective-permute-done.refs_1_.refs_3_.refs_2_, f32[64,384]{1,0:T(8,128)S(1)} %shard_map.60.refs_2_), custom_call_target="tpu_custom_call" | custom-call | bytes 1048576 | tf_op jit(solution)/shard_map/pallas_call | solution.py:139
  12.6 0.0 collective-permute-done.1.refs_1_.refs_0_
  12.6 0.0 collective-permute-done.2.refs_0_.refs_1_
  12.6 0.1 collective-permute-start.5
  12.7 1.9 %shard_map.62 = (f32[64,384]{1,0:T(8,128)S(1)}, f32[64,384]{1,0:T(8,128)S(1)}) custom-call(f32[200,128]{1,0:T(8,128)S(1)} %collective-permute-done.2.refs_0_.refs_1_, f32[200,128]{1,0:T(8,128)S(1)} %collective-permute-done.1.refs_1_.refs_0_, f32[200,128]{1,0:T(8,128)S(1)} %copy-done.1, f32[200,128]{1,0:T(8,128)S(1)} %collective-permute-done.refs_1_.refs_3_.refs_2_), custom_call_target="tpu_custom_call" | custom-call | flops 10000000000 | bytes 1048576 | tf_op jit(solution)/shard_map/pallas_call | solution.py:139
  14.6 0.0 collective-permute-done.5.refs_0_.refs_1_
  14.6 1.4 %shard_map.63.refs_4_ = f32[64,384]{1,0:T(8,128)S(1)} custom-call(f32[200,128]{1,0:T(8,128)S(1)} %collective-permute-done.5.refs_0_.refs_1_, f32[200,128]{1,0:T(8,128)S(1)} %copy-done.1, f32[200,128]{1,0:T(8,128)S(1)} %collective-permute-done.refs_1_.refs_3_.refs_2_), custom_call_target="tpu_custom_call" | custom-call | bytes 1048576 | tf_op jit(solution)/shard_map/pallas_call | solution.py:139
  16.0 0.0 collective-permute-done.3.refs_2_
  16.0 1.2 %shard_map.64 = (f32[64,384]{1,0:T(8,128)S(1)}, f32[64,384]{1,0:T(8,128)S(1)}) custom-call(f32[200,128]{1,0:T(8,128)S(1)} %collective-permute-done.1.refs_1_.refs_0_, f32[200,128]{1,0:T(8,128)S(1)} %collective-permute-done.5.refs_0_.refs_1_, f32[200,128]{1,0:T(8,128)S(1)} %collective-permute-done.3.refs_2_, f32[64,384]{1,0:T(8,128)S(1)} %get-tuple-element.18.refs_3_, ...), custom_call_target="tpu_custom_call" | custom-call | bytes 1048576 | tf_op jit(solution)/shard_map/pallas_call | solution.py:139
  17.2 0.1 collective-permute-done.4.refs_1_.refs_3_
  17.3 1.1 %shard_map.66 = f32[64,384]{1,0:T(8,128)S(1)} custom-call(f32[200,128]{1,0:T(8,128)S(1)} %collective-permute-done.5.refs_0_.refs_1_, f32[200,128]{1,0:T(8,128)S(1)} %collective-permute-done.4.refs_1_.refs_3_, f32[64,384]{1,0:T(8,128)S(1)} %get-tuple-element.20.refs_2_), custom_call_target="tpu_custom_call" | custom-call | bytes 1048576 | tf_op jit(solution)/shard_map/pallas_call | solution.py:139
  18.4 0.5 %collective-permute-start.6 = (f32[64,384]{1,0:T(8,128)S(1)}, f32[64,384]{1,0:T(8,128)S(1)}, u32[]{:S(2)}, u32[]{:S(2)}) collective-permute-start(f32[64,384]{1,0:T(8,128)S(1)} %shard_map.66), channel_id=1, source_target_pairs={{0,1},{1,0},{2,3},{3,2},{4,5},{5,4},{6,7},{7,6},{8,9},{9,8},{10,11... | collective-permute-start | bytes 294920 | tf_op jit(solution)/shard_map/ppermute | solution.py:177
  18.9 1.1 %shard_map.65 = f32[64,384]{1,0:T(8,128)S(1)} custom-call(f32[200,128]{1,0:T(8,128)S(1)} %collective-permute-done.1.refs_1_.refs_0_, f32[200,128]{1,0:T(8,128)S(1)} %collective-permute-done.4.refs_1_.refs_3_, f32[64,384]{1,0:T(8,128)S(1)} %get-tuple-element.19.refs_2_), custom_call_target="tpu_custom_call" | custom-call | bytes 1048576 | tf_op jit(solution)/shard_map/pallas_call | solution.py:139
  19.9 0.0 collective-permute-done.6
  20.0 1.0 %collective-permute-start.7 = (f32[64,384]{1,0:T(8,128)S(1)}, f32[64,384]{1,0:T(8,128)S(1)}, u32[]{:S(2)}, u32[]{:S(2)}) collective-permute-start(f32[64,384]{1,0:T(8,128)S(1)} %add.6), channel_id=1, source_target_pairs={{0,2},{1,3},{2,0},{3,1},{4,6},{5,7},{6,4},{7,5},{8,10},{9,11},{10,... | collective-permute-start | bytes 294920 | tf_op jit(solution)/shard_map/ppermute | solution.py:177
  20.9 1.9 %shard_map.67 = (f32[64,384]{1,0:T(8,128)S(1)}, f32[64,384]{1,0:T(8,128)S(1)}) custom-call(f32[200,128]{1,0:T(8,128)S(1)} %copy-done.1, f32[200,128]{1,0:T(8,128)S(1)} %collective-permute-done.2.refs_0_.refs_1_, f32[200,128]{1,0:T(8,128)S(1)} %collective-permute-done.3.refs_2_, f32[200,128]{1,0:T(8,128)S(1)} %collective-permute-done.4.refs_1_.refs_3_, ...), custom_call_target="tpu_custom_call" | custom-call | bytes 1048576 | tf_op jit(solution)/shard_map/pallas_call | solution.py:139
  22.8 0.1 collective-permute-start.8
  22.9 2.0 %collective-permute-done.7 = f32[64,384]{1,0:T(8,128)S(1)} collective-permute-done((f32[64,384]{1,0:T(8,128)S(1)}, f32[64,384]{1,0:T(8,128)S(1)}, u32[]{:S(2)}, u32[]{:S(2)}) %collective-permute-start.7) | collective-permute-done | bytes 98336 | tf_op jit(solution)/shard_map/ppermute | solution.py:177
  25.0 0.0 collective-permute-done.8.near_ref
  25.0 0.6 %shard_map.68 = (f32[64,256]{1,0:T(8,128)}, f32[64,128]{1,0:T(8,128)}) custom-call(f32[64,384]{1,0:T(8,128)S(1)} %add.7.mine_ref, f32[64,384]{1,0:T(8,128)S(1)} %collective-permute-done.8.near_ref), custom_call_target="tpu_custom_call" | custom-call | tf_op jit(solution)/shard_map/pallas_call | solution.py:207
  (2 shorter events, 0.0 us)
Async XLA Ops:
  2.1 9.3 %collective-permute-start = (f32[200,128]{1,0:T(8,128)}, f32[200,128]{1,0:T(8,128)S(1)}, u32[]{:S(2)}, u32[]{:S(2)}) collective-permute-start(f32[200,128]{1,0:T(8,128)} %shard_map.59.refs_0_.refs_1_.refs_2_), channel_id=1, source_target_pairs={{0,12},{1,13},{2,14},{3,15},{4,8},{5,9},{6,10},{7,11},{8,4},{9,5},... | collective-permute-start | bytes 307208 | tf_op jit(solution)/shard_map/ppermute | solution.py:177
  7.2 5.4 %collective-permute-start.1 = (f32[200,128]{1,0:T(8,128)}, f32[200,128]{1,0:T(8,128)S(1)}, u32[]{:S(2)}, u32[]{:S(2)}) collective-permute-start(f32[200,128]{1,0:T(8,128)} %shard_map.59.refs_0_.refs_1_.refs_2_), channel_id=1, source_target_pairs={{0,2},{1,3},{2,0},{3,1},{4,6},{5,7},{6,4},{7,5},{8,10},{9,11},{10,... | collective-permute-start | bytes 307208 | tf_op jit(solution)/shard_map/ppermute | solution.py:177
  8.7 3.9 %collective-permute-start.2 = (f32[200,128]{1,0:T(8,128)}, f32[200,128]{1,0:T(8,128)S(1)}, u32[]{:S(2)}, u32[]{:S(2)}) collective-permute-start(f32[200,128]{1,0:T(8,128)} %shard_map.59.refs_0_.refs_1_.refs_2_), channel_id=1, source_target_pairs={{0,1},{1,0},{2,3},{3,2},{4,5},{5,4},{6,7},{7,6},{8,9},{9,8},{10,11... | collective-permute-start | bytes 307208 | tf_op jit(solution)/shard_map/ppermute | solution.py:177
  8.7 7.3 %collective-permute-start.3 = (f32[200,128]{1,0:T(8,128)}, f32[200,128]{1,0:T(8,128)S(1)}, u32[]{:S(2)}, u32[]{:S(2)}) collective-permute-start(f32[200,128]{1,0:T(8,128)} %shard_map.59.refs_0_.refs_1_.refs_2_), channel_id=1, source_target_pairs={{0,4},{1,5},{2,6},{3,7},{4,0},{5,1},{6,2},{7,3},{8,12},{9,13},{10,... | collective-permute-start | bytes 307208 | tf_op jit(solution)/shard_map/ppermute | solution.py:177
  8.7 8.6 %collective-permute-start.4 = (f32[200,128]{1,0:T(8,128)}, f32[200,128]{1,0:T(8,128)S(1)}, u32[]{:S(2)}, u32[]{:S(2)}) collective-permute-start(f32[200,128]{1,0:T(8,128)} %shard_map.59.refs_0_.refs_1_.refs_2_), channel_id=1, source_target_pairs={{0,8},{1,9},{2,10},{3,11},{4,12},{5,13},{6,14},{7,15},{8,0},{9,1},... | collective-permute-start | bytes 307208 | tf_op jit(solution)/shard_map/ppermute | solution.py:177
  9.5 0.9 %copy-start = (f32[200,128]{1,0:T(8,128)S(1)}, f32[200,128]{1,0:T(8,128)}, u32[]{:S(2)}) copy-start(f32[200,128]{1,0:T(8,128)} %shard_map.59.refs_0_.refs_1_.refs_2_) | copy-start | bytes 307204
  10.4 1.1 %copy-start.1 = (f32[200,128]{1,0:T(8,128)S(1)}, f32[200,128]{1,0:T(8,128)}, u32[]{:S(2)}) copy-start(f32[200,128]{1,0:T(8,128)} %shard_map.59.refs_0_.refs_1_.refs_2_) | copy-start | bytes 307204
  12.6 2.0 %collective-permute-start.5 = (f32[200,128]{1,0:T(8,128)S(1)}, f32[200,128]{1,0:T(8,128)S(1)}, u32[]{:S(2)}, u32[]{:S(2)}) collective-permute-start(f32[200,128]{1,0:T(8,128)S(1)} %collective-permute-done.1.refs_1_.refs_0_), channel_id=1, source_target_pairs={{0,1},{1,0},{2,3},{3,2},{4,5},{5,4},{6,7},{7,6},{8,9},{9,8},{10,11... | collective-permute-start | bytes 307208 | tf_op jit(solution)/shard_map/ppermute | solution.py:177
  18.4 1.5 %collective-permute-start.6 = (f32[64,384]{1,0:T(8,128)S(1)}, f32[64,384]{1,0:T(8,128)S(1)}, u32[]{:S(2)}, u32[]{:S(2)}) collective-permute-start(f32[64,384]{1,0:T(8,128)S(1)} %shard_map.66), channel_id=1, source_target_pairs={{0,1},{1,0},{2,3},{3,2},{4,5},{5,4},{6,7},{7,6},{8,9},{9,8},{10,11... | collective-permute-start | bytes 294920 | tf_op jit(solution)/shard_map/ppermute | solution.py:177
  20.0 5.0 %collective-permute-start.7 = (f32[64,384]{1,0:T(8,128)S(1)}, f32[64,384]{1,0:T(8,128)S(1)}, u32[]{:S(2)}, u32[]{:S(2)}) collective-permute-start(f32[64,384]{1,0:T(8,128)S(1)} %add.6), channel_id=1, source_target_pairs={{0,2},{1,3},{2,0},{3,1},{4,6},{5,7},{6,4},{7,5},{8,10},{9,11},{10,... | collective-permute-start | bytes 294920 | tf_op jit(solution)/shard_map/ppermute | solution.py:177
  22.8 2.1 %collective-permute-start.8 = (f32[64,384]{1,0:T(8,128)S(1)}, f32[64,384]{1,0:T(8,128)S(1)}, u32[]{:S(2)}, u32[]{:S(2)}) collective-permute-start(f32[64,384]{1,0:T(8,128)S(1)} %get-tuple-element.25), channel_id=1, source_target_pairs={{0,1},{1,0},{2,3},{3,2},{4,5},{5,4},{6,7},{7,6},{8,9},{9,8},{10,11... | collective-permute-start | bytes 294920 | tf_op jit(solution)/shard_map/ppermute | solution.py:177

commit v4 on v3

--- a/solution.py
+++ b/solution.py
@@ -19,16 +19,26 @@
     return high, value - high
 
 
-def pack_kernel(slabs, feats, src_ref, srcp_ref, tgt_ref, tgtp_ref, out_ref):
+def pack_kernel(slabs, feats, src_ref, srcp_ref, tgt_ref, tgtp_ref, out_ref, srcp_held, tgtp_held, sems):
     src_slabs = src_ref.shape[1] // LANES
+    held = (srcp_held, tgtp_held)
+    copies = [pltpu.make_async_copy(ref, to, sems.at[at]) for at, (ref, to) in enumerate(zip((srcp_ref, tgtp_ref), held))]
+    for slab in range(slabs):
+        ref, at = (src_ref, slab) if slab < src_slabs else (tgt_ref, slab - src_slabs)
+        to = out_ref.at[slab * feats : (slab + 1) * feats, :]
+        copies.append(pltpu.make_async_copy(ref.at[:, at * LANES : (at + 1) * LANES], to, sems.at[2 + slab]))
+    for copy in copies:
+        copy.start()
     out_ref[slabs * feats :, :] = jnp.zeros((out_ref.shape[0] - slabs * feats, LANES), f32)
+    for copy in copies[:2]:
+        copy.wait()
     for slab in range(slabs):
-        ref, pot, at = (src_ref, srcp_ref, slab) if slab < src_slabs else (tgt_ref, tgtp_ref, slab - src_slabs)
-        cols = slice(at * LANES, (at + 1) * LANES)
-        out_ref[slab * feats : (slab + 1) * feats, :] = ref[:, cols]
+        pot, at = (srcp_held, slab) if slab < src_slabs else (tgtp_held, slab - src_slabs)
         for which in range(2):
             row = slabs * feats + which * slabs + slab
-            out_ref[row : row + 1, :] = pot[which : which + 1, cols]
+            out_ref[row : row + 1, :] = pot[which : which + 1, at * LANES : (at + 1) * LANES]
+    for copy in copies[2:]:
+        copy.wait()
 
 
 def pair_kernel(shape, num_rows, num_cols, jobs, totals, prev_rows, joined, *refs):
@@ -166,12 +176,20 @@
     totals = (src_count * devices, tgt_count * devices)
     pot_rows = -(-2 * slabs // 8) * 8
     vmem = pl.BlockSpec(memory_space=pltpu.VMEM)
+    hbm = pl.BlockSpec(memory_space=pltpu.HBM)
+    args = (src_latent, src_potential, tgt_latent, tgt_potential)
     packed = pl.pallas_call(
         functools.partial(pack_kernel, slabs, feats),
-        out_shape=jax.ShapeDtypeStruct((slabs * feats + pot_rows, LANES), f32),
-        in_specs=[vmem] * 4,
+        out_shape=pltpu.VMEM((slabs * feats + pot_rows, LANES), f32),
+        in_specs=[hbm] * 4,
         out_specs=vmem,
-    )(src_latent, src_potential, tgt_latent, tgt_potential)
+        scratch_shapes=[
+            pltpu.VMEM(src_potential.shape, f32),
+            pltpu.VMEM(tgt_potential.shape, f32),
+            pltpu.SemaphoreType.DMA((2 + slabs,)),
+        ],
+        compiler_params=pltpu.CompilerParams(vmem_limit_bytes=4 * 2**20),
+    )(*[pltpu.with_memory_space_constraint(arg, pltpu.HBM) for arg in args])
 
     def swap(value, bits):
         return lax.ppermute(value, "src", [(i, i ^ bits) for i in range(devices)])

time: 25.8 us -> 24.9 us (0.965)
  waiting for transfers between devices: 2.15 us -> 3.09 us
  local copies, waits for them, and re-layouts: 0.93 us -> 0 us
  Pallas kernels: 12.8 us -> 12.2 us
    ppermute x9, waiting for transfers between devices: 2.15 us -> 3.09 us  [swap(): return lax.ppermute(value, 'src', [(i, i ^ bits) for i in range(devices)])]
    unnamed x4 -> x0, local copies, waits for them, and re-layouts: 0.93 us -> none
    pallas_call x1, Pallas kernels: 1.5 us -> 0.87 us  [body(): pl.pallas_call(functools.partial(pack_kernel, slabs, feats), out_shape=pl...]
  transfers between devices with their start and end apart: 9 -> 9, of which waited for: 2 -> 5; matrix products, arithmetic and copies ran while one was open for 0% -> 0% of each run, Pallas kernels for 38% -> 39%
where the time goes in v4:
time: 24.9 us; the launch traced here: 24.7 us
  Pallas kernels  12.2 us (49%)
  starting transfers between devices  8.68 us (35%)
  waiting for transfers between devices  3.09 us (12%)
  between operations  0.75 us (3%)
    pallas_call x8, Pallas kernels, pair_terms(): pl.pallas_call(functools.partial(pair_kernel, shape, len(rows), len(cols)...  10.7 us
    ppermute x9, starting transfers between devices, swap(): return lax.ppermute(value, 'src', [(i, i ^ bits) for i in range(devices)])  8.68 us
    ppermute x9, waiting for transfers between devices, swap(): return lax.ppermute(value, 'src', [(i, i ^ bits) for i in range(devices)])  3.09 us
    pallas_call x1, Pallas kernels, body(): pl.pallas_call(functools.partial(pack_kernel, slabs, feats), out_shape=pl...  0.87 us
    pallas_call x1, Pallas kernels, body(): pl.pallas_call(finish_kernel, out_shape=[jax.ShapeDtypeStruct(src_latent....  0.65 us
  transfers between devices with their start and end apart: 9, of which 5 were waited for; matrix products, arithmetic and copies ran while one was open for 0% of the time, Pallas kernels for 39%

profile of v4, /device:TPU:0, one launch (start us, length us, event | category | flops | bytes accessed | tf_op | source)
XLA Modules:
  0.0 24.7 jit_solution(8903429801708509736)
XLA Ops:
  0.6 0.9 %shard_map.59.refs_0_.refs_1_.refs_2_ = f32[200,128]{1,0:T(8,128)S(1)} custom-call(f32[64,256]{1,0:T(8,128)} %src_ref.1, f32[2,256]{1,0:T(2,128)} %srcp_ref.1, f32[64,128]{1,0:T(8,128)} %tgt_ref.1, f32[2,128]{1,0:T(2,128)} %tgtp_ref.1), custom_call_target="tpu_custom_call" | custom-call | tf_op jit(solution)/shard_map/pallas_call | solution.py:181
  1.5 5.1 %collective-permute-start = (f32[200,128]{1,0:T(8,128)S(1)}, f32[200,128]{1,0:T(8,128)S(1)}, u32[]{:S(2)}, u32[]{:S(2)}) collective-permute-start(f32[200,128]{1,0:T(8,128)S(1)} %shard_map.59.refs_0_.refs_1_.refs_2_), channel_id=1, source_target_pairs={{0,12},{1,13},{2,14},{3,15},{4,8},{5,9},{6,10},{7,11},{8,4},{9,5},... | collective-permute-start | bytes 307208 | tf_op jit(solution)/shard_map/ppermute | solution.py:195
  6.6 1.5 %collective-permute-start.1 = (f32[200,128]{1,0:T(8,128)S(1)}, f32[200,128]{1,0:T(8,128)S(1)}, u32[]{:S(2)}, u32[]{:S(2)}) collective-permute-start(f32[200,128]{1,0:T(8,128)S(1)} %shard_map.59.refs_0_.refs_1_.refs_2_), channel_id=1, source_target_pairs={{0,2},{1,3},{2,0},{3,1},{4,6},{5,7},{6,4},{7,5},{8,10},{9,11},{10,... | collective-permute-start | bytes 307208 | tf_op jit(solution)/shard_map/ppermute | solution.py:195
  8.1 0.0 collective-permute-start.2
  8.1 0.0 collective-permute-start.3
  8.1 0.8 %collective-permute-start.4 = (f32[200,128]{1,0:T(8,128)S(1)}, f32[200,128]{1,0:T(8,128)S(1)}, u32[]{:S(2)}, u32[]{:S(2)}) collective-permute-start(f32[200,128]{1,0:T(8,128)S(1)} %shard_map.59.refs_0_.refs_1_.refs_2_), channel_id=1, source_target_pairs={{0,8},{1,9},{2,10},{3,11},{4,12},{5,13},{6,14},{7,15},{8,0},{9,1},... | collective-permute-start | bytes 307208 | tf_op jit(solution)/shard_map/ppermute | solution.py:195
  8.9 1.1 %shard_map.60.refs_2_ = f32[64,384]{1,0:T(8,128)S(1)} custom-call(f32[200,128]{1,0:T(8,128)S(1)} %shard_map.59.refs_0_.refs_1_.refs_2_, f32[200,128]{1,0:T(8,128)S(1)} %shard_map.59.refs_0_.refs_1_.refs_2_), custom_call_target="tpu_custom_call" | custom-call | bytes 1048576 | tf_op jit(solution)/shard_map/pallas_call | solution.py:149
  10.0 0.0 collective-permute-done.refs_1_.refs_3_.refs_2_
  10.0 1.1 %shard_map.61.refs_4_ = f32[64,384]{1,0:T(8,128)S(1)} custom-call(f32[200,128]{1,0:T(8,128)S(1)} %shard_map.59.refs_0_.refs_1_.refs_2_, f32[200,128]{1,0:T(8,128)S(1)} %collective-permute-done.refs_1_.refs_3_.refs_2_, f32[64,384]{1,0:T(8,128)S(1)} %shard_map.60.refs_2_), custom_call_target="tpu_custom_call" | custom-call | bytes 1048576 | tf_op jit(solution)/shard_map/pallas_call | solution.py:149
  11.1 0.2 collective-permute-done.1.refs_1_.refs_0_
  11.3 0.0 collective-permute-done.2.refs_0_.refs_1_
  11.3 0.0 collective-permute-start.5
  11.3 1.9 %shard_map.62 = (f32[64,384]{1,0:T(8,128)S(1)}, f32[64,384]{1,0:T(8,128)S(1)}) custom-call(f32[200,128]{1,0:T(8,128)S(1)} %collective-permute-done.2.refs_0_.refs_1_, f32[200,128]{1,0:T(8,128)S(1)} %collective-permute-done.1.refs_1_.refs_0_, f32[200,128]{1,0:T(8,128)S(1)} %shard_map.59.refs_0_.refs_1_.refs_2_, ...), custom_call_target="tpu_custom_call" | custom-call | flops 10000000000 | bytes 1048576 | tf_op jit(solution)/shard_map/pallas_call | solution.py:149
  13.2 0.0 collective-permute-done.5.refs_0_.refs_1_
  13.2 1.4 %shard_map.63.refs_4_ = f32[64,384]{1,0:T(8,128)S(1)} custom-call(f32[200,128]{1,0:T(8,128)S(1)} %collective-permute-done.5.refs_0_.refs_1_, f32[200,128]{1,0:T(8,128)S(1)} %shard_map.59.refs_0_.refs_1_.refs_2_, f32[200,128]{1,0:T(8,128)S(1)} %collective-permute-done.refs_1_.refs_3_.refs_2_), custom_call_target="tpu_custom_call" | custom-call | bytes 1048576 | tf_op jit(solution)/shard_map/pallas_call | solution.py:149
  14.6 0.1 collective-permute-done.3.refs_2_
  14.6 1.2 %shard_map.64 = (f32[64,384]{1,0:T(8,128)S(1)}, f32[64,384]{1,0:T(8,128)S(1)}) custom-call(f32[200,128]{1,0:T(8,128)S(1)} %collective-permute-done.1.refs_1_.refs_0_, f32[200,128]{1,0:T(8,128)S(1)} %collective-permute-done.5.refs_0_.refs_1_, f32[200,128]{1,0:T(8,128)S(1)} %collective-permute-done.3.refs_2_, f32[64,384]{1,0:T(8,128)S(1)} %get-tuple-element.18.refs_3_, ...), custom_call_target="tpu_custom_call" | custom-call | bytes 1048576 | tf_op jit(solution)/shard_map/pallas_call | solution.py:149
  15.9 0.7 %collective-permute-done.4.refs_1_.refs_3_ = f32[200,128]{1,0:T(8,128)S(1)} collective-permute-done((f32[200,128]{1,0:T(8,128)S(1)}, f32[200,128]{1,0:T(8,128)S(1)}, u32[]{:S(2)}, u32[]{:S(2)}) %collective-permute-start.4) | collective-permute-done | bytes 102432 | tf_op jit(solution)/shard_map/ppermute | solution.py:195
  16.6 1.1 %shard_map.66 = f32[64,384]{1,0:T(8,128)S(1)} custom-call(f32[200,128]{1,0:T(8,128)S(1)} %collective-permute-done.5.refs_0_.refs_1_, f32[200,128]{1,0:T(8,128)S(1)} %collective-permute-done.4.refs_1_.refs_3_, f32[64,384]{1,0:T(8,128)S(1)} %get-tuple-element.20.refs_2_), custom_call_target="tpu_custom_call" | custom-call | bytes 1048576 | tf_op jit(solution)/shard_map/pallas_call | solution.py:149
  17.6 0.1 collective-permute-start.6
  17.7 1.1 %shard_map.65 = f32[64,384]{1,0:T(8,128)S(1)} custom-call(f32[200,128]{1,0:T(8,128)S(1)} %collective-permute-done.1.refs_1_.refs_0_, f32[200,128]{1,0:T(8,128)S(1)} %collective-permute-done.4.refs_1_.refs_3_, f32[64,384]{1,0:T(8,128)S(1)} %get-tuple-element.19.refs_2_), custom_call_target="tpu_custom_call" | custom-call | bytes 1048576 | tf_op jit(solution)/shard_map/pallas_call | solution.py:149
  18.8 0.2 collective-permute-done.6
  19.0 1.1 %collective-permute-start.7 = (f32[64,384]{1,0:T(8,128)S(1)}, f32[64,384]{1,0:T(8,128)S(1)}, u32[]{:S(2)}, u32[]{:S(2)}) collective-permute-start(f32[64,384]{1,0:T(8,128)S(1)} %add.6), channel_id=1, source_target_pairs={{0,2},{1,3},{2,0},{3,1},{4,6},{5,7},{6,4},{7,5},{8,10},{9,11},{10,... | collective-permute-start | bytes 294920 | tf_op jit(solution)/shard_map/ppermute | solution.py:195
  20.2 1.9 %shard_map.67 = (f32[64,384]{1,0:T(8,128)S(1)}, f32[64,384]{1,0:T(8,128)S(1)}) custom-call(f32[200,128]{1,0:T(8,128)S(1)} %shard_map.59.refs_0_.refs_1_.refs_2_, f32[200,128]{1,0:T(8,128)S(1)} %collective-permute-done.2.refs_0_.refs_1_, f32[200,128]{1,0:T(8,128)S(1)} %collective-permute-done.3.refs_2_, ...), custom_call_target="tpu_custom_call" | custom-call | bytes 1048576 | tf_op jit(solution)/shard_map/pallas_call | solution.py:149
  22.1 0.1 collective-permute-start.8
  22.1 1.9 %collective-permute-done.7 = f32[64,384]{1,0:T(8,128)S(1)} collective-permute-done((f32[64,384]{1,0:T(8,128)S(1)}, f32[64,384]{1,0:T(8,128)S(1)}, u32[]{:S(2)}, u32[]{:S(2)}) %collective-permute-start.7) | collective-permute-done | bytes 98336 | tf_op jit(solution)/shard_map/ppermute | solution.py:195
  24.1 0.0 collective-permute-done.8.near_ref
  24.1 0.6 %shard_map.68 = (f32[64,256]{1,0:T(8,128)}, f32[64,128]{1,0:T(8,128)}) custom-call(f32[64,384]{1,0:T(8,128)S(1)} %add.7.mine_ref, f32[64,384]{1,0:T(8,128)S(1)} %collective-permute-done.8.near_ref), custom_call_target="tpu_custom_call" | custom-call | tf_op jit(solution)/shard_map/pallas_call | solution.py:225
  (2 shorter events, 0.0 us)
Async XLA Ops:
  1.5 8.5 %collective-permute-start = (f32[200,128]{1,0:T(8,128)S(1)}, f32[200,128]{1,0:T(8,128)S(1)}, u32[]{:S(2)}, u32[]{:S(2)}) collective-permute-start(f32[200,128]{1,0:T(8,128)S(1)} %shard_map.59.refs_0_.refs_1_.refs_2_), channel_id=1, source_target_pairs={{0,12},{1,13},{2,14},{3,15},{4,8},{5,9},{6,10},{7,11},{8,4},{9,5},... | collective-permute-start | bytes 307208 | tf_op jit(solution)/shard_map/ppermute | solution.py:195
  6.6 4.7 %collective-permute-start.1 = (f32[200,128]{1,0:T(8,128)S(1)}, f32[200,128]{1,0:T(8,128)S(1)}, u32[]{:S(2)}, u32[]{:S(2)}) collective-permute-start(f32[200,128]{1,0:T(8,128)S(1)} %shard_map.59.refs_0_.refs_1_.refs_2_), channel_id=1, source_target_pairs={{0,2},{1,3},{2,0},{3,1},{4,6},{5,7},{6,4},{7,5},{8,10},{9,11},{10,... | collective-permute-start | bytes 307208 | tf_op jit(solution)/shard_map/ppermute | solution.py:195
  8.1 3.2 %collective-permute-start.2 = (f32[200,128]{1,0:T(8,128)S(1)}, f32[200,128]{1,0:T(8,128)S(1)}, u32[]{:S(2)}, u32[]{:S(2)}) collective-permute-start(f32[200,128]{1,0:T(8,128)S(1)} %shard_map.59.refs_0_.refs_1_.refs_2_), channel_id=1, source_target_pairs={{0,1},{1,0},{2,3},{3,2},{4,5},{5,4},{6,7},{7,6},{8,9},{9,8},{10,11... | collective-permute-start | bytes 307208 | tf_op jit(solution)/shard_map/ppermute | solution.py:195
  8.1 6.5 %collective-permute-start.3 = (f32[200,128]{1,0:T(8,128)S(1)}, f32[200,128]{1,0:T(8,128)S(1)}, u32[]{:S(2)}, u32[]{:S(2)}) collective-permute-start(f32[200,128]{1,0:T(8,128)S(1)} %shard_map.59.refs_0_.refs_1_.refs_2_), channel_id=1, source_target_pairs={{0,4},{1,5},{2,6},{3,7},{4,0},{5,1},{6,2},{7,3},{8,12},{9,13},{10,... | collective-permute-start | bytes 307208 | tf_op jit(solution)/shard_map/ppermute | solution.py:195
  8.1 8.4 %collective-permute-start.4 = (f32[200,128]{1,0:T(8,128)S(1)}, f32[200,128]{1,0:T(8,128)S(1)}, u32[]{:S(2)}, u32[]{:S(2)}) collective-permute-start(f32[200,128]{1,0:T(8,128)S(1)} %shard_map.59.refs_0_.refs_1_.refs_2_), channel_id=1, source_target_pairs={{0,8},{1,9},{2,10},{3,11},{4,12},{5,13},{6,14},{7,15},{8,0},{9,1},... | collective-permute-start | bytes 307208 | tf_op jit(solution)/shard_map/ppermute | solution.py:195
  11.3 1.9 %collective-permute-start.5 = (f32[200,128]{1,0:T(8,128)S(1)}, f32[200,128]{1,0:T(8,128)S(1)}, u32[]{:S(2)}, u32[]{:S(2)}) collective-permute-start(f32[200,128]{1,0:T(8,128)S(1)} %collective-permute-done.1.refs_1_.refs_0_), channel_id=1, source_target_pairs={{0,1},{1,0},{2,3},{3,2},{4,5},{5,4},{6,7},{7,6},{8,9},{9,8},{10,11... | collective-permute-start | bytes 307208 | tf_op jit(solution)/shard_map/ppermute | solution.py:195
  17.6 1.4 %collective-permute-start.6 = (f32[64,384]{1,0:T(8,128)S(1)}, f32[64,384]{1,0:T(8,128)S(1)}, u32[]{:S(2)}, u32[]{:S(2)}) collective-permute-start(f32[64,384]{1,0:T(8,128)S(1)} %shard_map.66), channel_id=1, source_target_pairs={{0,1},{1,0},{2,3},{3,2},{4,5},{5,4},{6,7},{7,6},{8,9},{9,8},{10,11... | collective-permute-start | bytes 294920 | tf_op jit(solution)/shard_map/ppermute | solution.py:195
  19.0 5.1 %collective-permute-start.7 = (f32[64,384]{1,0:T(8,128)S(1)}, f32[64,384]{1,0:T(8,128)S(1)}, u32[]{:S(2)}, u32[]{:S(2)}) collective-permute-start(f32[64,384]{1,0:T(8,128)S(1)} %add.6), channel_id=1, source_target_pairs={{0,2},{1,3},{2,0},{3,1},{4,6},{5,7},{6,4},{7,5},{8,10},{9,11},{10,... | collective-permute-start | bytes 294920 | tf_op jit(solution)/shard_map/ppermute | solution.py:195
  22.1 2.0 %collective-permute-start.8 = (f32[64,384]{1,0:T(8,128)S(1)}, f32[64,384]{1,0:T(8,128)S(1)}, u32[]{:S(2)}, u32[]{:S(2)}) collective-permute-start(f32[64,384]{1,0:T(8,128)S(1)} %get-tuple-element.25), channel_id=1, source_target_pairs={{0,1},{1,0},{2,3},{3,2},{4,5},{5,4},{6,7},{7,6},{8,9},{9,8},{10,11... | collective-permute-start | bytes 294920 | tf_op jit(solution)/shard_map/ppermute | solution.py:195

commit v5 on v4

--- a/solution.py
+++ b/solution.py
@@ -41,29 +41,45 @@
         copy.wait()
 
 
-def pair_kernel(shape, num_rows, num_cols, jobs, totals, prev_rows, joined, *refs):
+def cell_terms(shape, ref, slab):
+    feats, src_slabs, tgt_slabs = shape
+    slabs = src_slabs + tgt_slabs
+    value = ref[slab * feats : (slab + 1) * feats, :]
+    norm = 0.5 * jnp.sum(value * value, 0, keepdims=True)
+    first = slabs * feats + slab
+    pots = [SCALE * (ref[first + which * slabs : first + which * slabs + 1, :] - norm) for which in range(2)]
+    return value, pots
+
+
+def store_row(shape, ref, lhs_ref, vec_ref):
+    feats, src_slabs, tgt_slabs = shape
+    for slab in range(src_slabs + tgt_slabs):
+        value, pots = cell_terms(shape, ref, slab)
+        high, low = split(value * SCALE)
+        both = jnp.concatenate([high, low], 0).T.astype(bf16)
+        at = slice(slab * LANES, (slab + 1) * LANES)
+        lhs_ref[at, 0:LANES] = both
+        lhs_ref[at, LANES:] = both
+        for which in range(2):
+            vec_ref[which, at, :] = jnp.broadcast_to(pots[which], (LANES, LANES)).T
+
+
+def pair_kernel(shape, num_rows, num_cols, jobs, totals, prev_rows, keep, *refs):
     feats, src_slabs, tgt_slabs = shape
     slabs = src_slabs + tgt_slabs
     rows, cols = refs[:num_rows], refs[num_rows : num_rows + num_cols]
-    num_outs = 1 if joined else num_rows
-    prev = refs[num_rows + num_cols : -num_outs - 2]
-    outs, lhs_ref, rvec_ref = refs[-num_outs - 2 : -2], refs[-2], refs[-1]
-    if joined:
-        width = slabs * LANES
-        outs = [outs[0].at[:, row * width : (row + 1) * width] for row in range(num_rows)]
+    lhs_ref, rvec_ref = refs[-2:]
+    refs = refs[num_rows + num_cols : -2]
+    prev, refs = refs[: len(prev_rows)], refs[len(prev_rows) :]
+    outs = refs[:num_rows]
+    if keep is not None:
+        store_row(shape, rows[keep], *refs[num_rows:])
     sums_so_far = dict(zip(prev_rows, prev))
-
-    def cell_terms(ref, slab):
-        value = ref[slab * feats : (slab + 1) * feats, :]
-        norm = 0.5 * jnp.sum(value * value, 0, keepdims=True)
-        first = slabs * feats + slab
-        pots = [SCALE * (ref[first + which * slabs : first + which * slabs + 1, :] - norm) for which in range(2)]
-        return value, pots
 
     row_slabs = [(row, slab) for row in range(num_rows) for slab in range(src_slabs)]
     row_slabs += [(row, slab) for row in range(num_rows) for slab in range(src_slabs, slabs)]
     for place, (row, slab) in enumerate(row_slabs):
-        value, pots = cell_terms(rows[row], slab)
+        value, pots = cell_terms(shape, rows[row], slab)
         high, low = split(value * SCALE)
         high, low = high.astype(bf16), low.astype(bf16)
         at = slice(place * LANES, (place + 1) * LANES)
@@ -78,7 +94,7 @@
     def prepare(members):
         trans, values, vecs = [], [], []
         for col, slab in members:
-            value, pots = cell_terms(cols[col], slab)
+            value, pots = cell_terms(shape, cols[col], slab)
             high, low = split(value)
             mid, least = split(low)
             both = jnp.concatenate([high, low], 0).T.astype(bf16)
@@ -139,18 +155,20 @@
             sums_so_far[row] = outs[row]
 
 
-def pair_terms(shape, totals, rows, cols, prev, jobs, cost=0, joined=False):
+def pair_terms(shape, totals, rows, cols, prev, jobs, cost=0, keep=None):
     feats, src_slabs, tgt_slabs = shape
     width = (src_slabs + tgt_slabs) * LANES
     vmem = pl.BlockSpec(memory_space=pltpu.VMEM)
-    one = jax.ShapeDtypeStruct((feats, width), f32)
     prev_rows = [row for row, value in enumerate(prev) if value is not None]
     args = [*rows, *cols, *[prev[row] for row in prev_rows]]
+    outs = [jax.ShapeDtypeStruct((feats, width), f32)] * len(rows)
+    if keep is not None:
+        outs += [jax.ShapeDtypeStruct((width, 4 * feats), bf16), jax.ShapeDtypeStruct((2, width, LANES), f32)]
     return pl.pallas_call(
-        functools.partial(pair_kernel, shape, len(rows), len(cols), jobs, totals, prev_rows, joined),
-        out_shape=jax.ShapeDtypeStruct((feats, len(rows) * width), f32) if joined else [one] * len(rows),
+        functools.partial(pair_kernel, shape, len(rows), len(cols), jobs, totals, prev_rows, keep),
+        out_shape=outs,
         in_specs=[vmem] * len(args),
-        out_specs=vmem if joined else [vmem] * len(rows),
+        out_specs=[vmem] * len(outs),
         scratch_shapes=[
             pltpu.VMEM((4 * feats, len(rows) * width), bf16),
             pltpu.VMEM((8, len(rows) * width), f32),
@@ -158,6 +176,59 @@
         compiler_params=pltpu.CompilerParams(vmem_limit_bytes=32 * 2**20),
         cost_estimate=pl.CostEstimate(flops=cost, bytes_accessed=2**20, transcendentals=0),
     )(*args)
+
+
+def late_kernel(shape, totals, block, lhs_ref, vec_ref, col, prev, out):
+    feats, src_slabs, tgt_slabs = shape
+    slabs = src_slabs + tgt_slabs
+    kinds = []
+    for first, last in ((0, src_slabs), (src_slabs, slabs)):
+        natural, values, vecs = [], [], [[], []]
+        for slab in range(first, last):
+            value, pots = cell_terms(shape, col, slab)
+            high, low = split(value)
+            mid, least = split(low)
+            high, low, mid, least = (part.astype(bf16) for part in (high, low, mid, least))
+            natural.append(jnp.concatenate([high, high, low, low], 0))
+            values.append(jnp.concatenate([high, mid, least, jnp.ones((16, LANES), bf16)], 0))
+            for which in range(2):
+                vecs[which].append(pots[which])
+        value = jnp.concatenate(values, 1)
+        value = jnp.concatenate([value, value], 1)
+        kinds.append((jnp.concatenate(natural, 1), value, [jnp.concatenate(vec, 1) for vec in vecs]))
+
+    for row_kind, (first, last) in enumerate(((0, src_slabs), (src_slabs, slabs))):
+        at = slice(first * LANES, last * LANES)
+        sums = []
+        for kind, (natural, value, vecs) in enumerate(kinds):
+            which = 1 if kind == row_kind else 0
+            power = jnp.dot(lhs_ref[at, :], natural, preferred_element_type=f32)
+            spread = jnp.concatenate([vec_ref[which, at, :]] * (natural.shape[1] // LANES), 1)
+            weight = jnp.exp2(power + (spread + vecs[which]))
+            high, low = split(weight)
+            both = jnp.concatenate([high.astype(bf16), low.astype(bf16)], 1)
+            sums.append(lax.dot_general(value, both, (((1,), (1,)), ((), ())), preferred_element_type=f32))
+        sign = 1.0 if row_kind == 0 else -1.0
+        total = sums[1] * (sign / totals[1]) - sums[0] * (sign / totals[0])
+        mixed = total[0:feats] + total[feats : 2 * feats] + total[2 * feats : 3 * feats]
+        mass = total[3 * feats : 3 * feats + 1]
+        for slab in range(first, last):
+            piece = slice((slab - first) * LANES, (slab - first + 1) * LANES)
+            spot = slice(slab * LANES, (slab + 1) * LANES)
+            value = block[slab * feats : (slab + 1) * feats, :]
+            out[:, spot] = value * mass[:, piece] - mixed[:, piece] + prev[:, spot]
+
+
+def late_terms(shape, totals, row, col, prev):
+    vmem = pl.BlockSpec(memory_space=pltpu.VMEM)
+    return pl.pallas_call(
+        functools.partial(late_kernel, shape, totals),
+        out_shape=jax.ShapeDtypeStruct(prev.shape, f32),
+        in_specs=[vmem] * 5,
+        out_specs=vmem,
+        compiler_params=pltpu.CompilerParams(vmem_limit_bytes=32 * 2**20),
+        cost_estimate=pl.CostEstimate(flops=0, bytes_accessed=2**20, transcendentals=0),
+    )(*row, col, prev)
 
 
 def finish_kernel(mine_ref, near_ref, src_ref, tgt_ref):
@@ -201,21 +272,21 @@
     arrival = sorted(from_z, key=lambda k: (k % 8 == 0, -k))
     early, middle, last = from_z[arrival[0]], arrival[1:-1], from_z[arrival[-1]]
     near_z = from_z[middle[-1]]
-    (mine,) = terms([packed], [packed], [None], [((0,), (0,), True)], 0)
-    (mine,) = terms([packed], [early], [mine], [((0,), (0,), False)])
+    (mine,) = terms([packed], [packed, early], [None], [((0,), (0, 1), True)])
     mine, later, beside = lax.optimization_barrier((mine, across, beside))
     corner = swap(later, 1)
-    near, wide = terms([beside, later], [packed, early], [None] * 2, [((0, 1), (0, 1), False)], 10000000000)
+    jobs = [((0, 1), (0, 1), False)]
+    near, wide, *row_later = terms([beside, later], [packed, early], [None] * 2, jobs, 10**10, 1)
     corner, wide = lax.optimization_barrier((corner, wide))
-    (sent,) = terms([corner], [packed, early], [None], [((0,), (0, 1), False)], 0)
+    sent, *row_corner = terms([corner], [packed, early], [None], [((0,), (0, 1), False)], 0, 0)
     wide, sent = terms([across, corner], [near_z], [wide, sent], [((0, 1), (0,), False)])
     for at in range(0, len(middle) - 1, 2):
         group = [from_z[k] for k in middle[at : min(at + 2, len(middle) - 1)]]
         jobs = [((0, 1, 2, 3), tuple(range(len(group))), False)]
         mine, near, wide, sent = terms([packed, beside, across, corner], group, [mine, near, wide, sent], jobs)
-    (sent,) = terms([corner], [last], [sent], [((0,), (0,), False)])
+    sent = late_terms(shape, totals, (corner, *row_corner), last, sent)
     got = swap(sent, 1)
-    (wide,) = terms([across], [last], [wide], [((0,), (0,), False)])
+    wide = late_terms(shape, totals, (across, *row_later), last, wide)
     send = wide + got
     far = swap(send, 2)
     last, send = lax.optimization_barrier((last, send))

time: 24.9 us -> 24.5 us (0.984)
  Pallas kernels: 12.2 us -> 10.8 us
  waiting for transfers between devices: 3.09 us -> 3.92 us
    pallas_call x8 -> x5, Pallas kernels: 10.7 us -> 7.8 us  [pair_terms(): pl.pallas_call(functools.partial(pair_kernel, shape, len(rows), len(cols)...]
    pallas_call x0 -> x2, Pallas kernels: none -> 1.52 us  [late_terms(): pl.pallas_call(functools.partial(late_kernel, shape, totals), out_shape=j...]
    ppermute x9, waiting for transfers between devices: 3.09 us -> 3.92 us  [swap(): return lax.ppermute(value, 'src', [(i, i ^ bits) for i in range(devices)])]
  transfers between devices with their start and end apart: 9 -> 9, of which waited for: 5 -> 6; matrix products, arithmetic and copies ran while one was open for 0% -> 0% of each run, Pallas kernels for 39% -> 35%
where the time goes in v5:
time: 24.5 us; the launch traced here: 24.3 us
  Pallas kernels  10.8 us (44%)
  starting transfers between devices  8.8 us (36%)
  waiting for transfers between devices  3.92 us (16%)
  between operations  0.72 us (3%)
    ppermute x9, starting transfers between devices, swap(): return lax.ppermute(value, 'src', [(i, i ^ bits) for i in range(devices)])  8.8 us
    pallas_call x5, Pallas kernels, pair_terms(): pl.pallas_call(functools.partial(pair_kernel, shape, len(rows), len(cols)...  7.8 us
    ppermute x9, waiting for transfers between devices, swap(): return lax.ppermute(value, 'src', [(i, i ^ bits) for i in range(devices)])  3.92 us
    pallas_call x2, Pallas kernels, late_terms(): pl.pallas_call(functools.partial(late_kernel, shape, totals), out_shape=j...  1.52 us
    pallas_call x1, Pallas kernels, body(): pl.pallas_call(functools.partial(pack_kernel, slabs, feats), out_shape=pl...  0.87 us
    pallas_call x1, Pallas kernels, body(): pl.pallas_call(finish_kernel, out_shape=[jax.ShapeDtypeStruct(src_latent....  0.65 us
  transfers between devices with their start and end apart: 9, of which 6 were waited for; matrix products, arithmetic and copies ran while one was open for 0% of the time, Pallas kernels for 35%

profile of v5, /device:TPU:0, one launch (start us, length us, event | category | flops | bytes accessed | tf_op | source)
XLA Modules:
  0.0 24.3 jit_solution(17628575476756720843)
XLA Ops:
  0.6 0.9 %shard_map.59.refs_0_.refs_1_.refs_2_ = f32[200,128]{1,0:T(8,128)S(1)} custom-call(f32[64,256]{1,0:T(8,128)} %src_ref.1, f32[2,256]{1,0:T(2,128)} %srcp_ref.1, f32[64,128]{1,0:T(8,128)} %tgt_ref.1, f32[2,128]{1,0:T(2,128)} %tgtp_ref.1), custom_call_target="tpu_custom_call" | custom-call | tf_op jit(solution)/shard_map/pallas_call | solution.py:252
  1.5 5.1 %collective-permute-start = (f32[200,128]{1,0:T(8,128)S(1)}, f32[200,128]{1,0:T(8,128)S(1)}, u32[]{:S(2)}, u32[]{:S(2)}) collective-permute-start(f32[200,128]{1,0:T(8,128)S(1)} %shard_map.59.refs_0_.refs_1_.refs_2_), channel_id=1, source_target_pairs={{0,12},{1,13},{2,14},{3,15},{4,8},{5,9},{6,10},{7,11},{8,4},{9,5},... | collective-permute-start | bytes 307208 | tf_op jit(solution)/shard_map/ppermute | solution.py:266
  6.6 1.5 %collective-permute-start.1 = (f32[200,128]{1,0:T(8,128)S(1)}, f32[200,128]{1,0:T(8,128)S(1)}, u32[]{:S(2)}, u32[]{:S(2)}) collective-permute-start(f32[200,128]{1,0:T(8,128)S(1)} %shard_map.59.refs_0_.refs_1_.refs_2_), channel_id=1, source_target_pairs={{0,2},{1,3},{2,0},{3,1},{4,6},{5,7},{6,4},{7,5},{8,10},{9,11},{10,... | collective-permute-start | bytes 307208 | tf_op jit(solution)/shard_map/ppermute | solution.py:266
  8.1 0.0 collective-permute-start.2
  8.1 0.0 collective-permute-start.3
  8.1 0.8 %collective-permute-start.4 = (f32[200,128]{1,0:T(8,128)S(1)}, f32[200,128]{1,0:T(8,128)S(1)}, u32[]{:S(2)}, u32[]{:S(2)}) collective-permute-start(f32[200,128]{1,0:T(8,128)S(1)} %shard_map.59.refs_0_.refs_1_.refs_2_), channel_id=1, source_target_pairs={{0,8},{1,9},{2,10},{3,11},{4,12},{5,13},{6,14},{7,15},{8,0},{9,1},... | collective-permute-start | bytes 307208 | tf_op jit(solution)/shard_map/ppermute | solution.py:266
  8.9 0.7 %collective-permute-done.refs_2_.refs_3_ = f32[200,128]{1,0:T(8,128)S(1)} collective-permute-done((f32[200,128]{1,0:T(8,128)S(1)}, f32[200,128]{1,0:T(8,128)S(1)}, u32[]{:S(2)}, u32[]{:S(2)}) %collective-permute-start) | collective-permute-done | bytes 102432 | tf_op jit(solution)/shard_map/ppermute | solution.py:266
  9.6 1.4 %shard_map.60.refs_4_ = f32[64,384]{1,0:T(8,128)S(1)} custom-call(f32[200,128]{1,0:T(8,128)S(1)} %shard_map.59.refs_0_.refs_1_.refs_2_, f32[200,128]{1,0:T(8,128)S(1)} %shard_map.59.refs_0_.refs_1_.refs_2_, f32[200,128]{1,0:T(8,128)S(1)} %collective-permute-done.refs_2_.refs_3_), custom_call_target="tpu_custom_call" | custom-call | bytes 1048576 | tf_op jit(solution)/shard_map/pallas_call | solution.py:167
  11.0 0.3 %collective-permute-done.1.refs_1_.refs_0_.block = f32[200,128]{1,0:T(8,128)S(1)} collective-permute-done((f32[200,128]{1,0:T(8,128)S(1)}, f32[200,128]{1,0:T(8,128)S(1)}, u32[]{:S(2)}, u32[]{:S(2)}) %collective-permute-start.1) | collective-permute-done | bytes 102432 | tf_op jit(solution)/shard_map/ppermute | solution.py:266
  11.3 0.0 collective-permute-done.2.refs_0_.refs_1_
  11.3 0.0 collective-permute-start.5
  11.3 1.9 %shard_map.61 = (f32[64,384]{1,0:T(8,128)S(1)}, f32[64,384]{1,0:T(8,128)S(1)}, bf16[384,256]{1,0:T(8,128)(2,1)S(1)}, f32[2,384,128]{2,1,0:T(8,128)S(1)}) custom-call(f32[200,128]{1,0:T(8,128)S(1)} %collective-permute-done.2.refs_0_.refs_1_, f32[200,128]{1,0:T(8,128)S(1)} %collective-permute-done.1.refs_1_.refs_0_.block, ...), custom_call_target="tpu_custom_call" | custom-call | flops 10000000000 | bytes 1048576 | tf_op jit(solution)/shard_map/pallas_call | solution.py:167
  13.2 0.0 collective-permute-done.5.refs_0_.refs_1_.block
  13.2 1.4 %shard_map.62 = (f32[64,384]{1,0:T(8,128)S(1)}, bf16[384,256]{1,0:T(8,128)(2,1)S(1)}, f32[2,384,128]{2,1,0:T(8,128)S(1)}) custom-call(f32[200,128]{1,0:T(8,128)S(1)} %collective-permute-done.5.refs_0_.refs_1_.block, f32[200,128]{1,0:T(8,128)S(1)} %shard_map.59.refs_0_.refs_1_.refs_2_, f32[200,128]{1,0:T(8,128)S(1)} %collective-permute-done.refs_2_.refs_3_), custom_call_target="tpu_custom_call" | custom-call | bytes 1048576 | tf_op jit(solution)/shard_map/pallas_call | solution.py:167
  14.6 0.1 collective-permute-done.3.refs_2_
  14.6 1.2 %shard_map.63 = (f32[64,384]{1,0:T(8,128)S(1)}, f32[64,384]{1,0:T(8,128)S(1)}) custom-call(f32[200,128]{1,0:T(8,128)S(1)} %collective-permute-done.1.refs_1_.refs_0_.block, f32[200,128]{1,0:T(8,128)S(1)} %collective-permute-done.5.refs_0_.refs_1_.block, f32[200,128]{1,0:T(8,128)S(1)} %collective-permute-done.3.refs_2_, ...), custom_call_target="tpu_custom_call" | custom-call | bytes 1048576 | tf_op jit(solution)/shard_map/pallas_call | solution.py:167
  15.9 0.7 %collective-permute-done.4.col.refs_3_ = f32[200,128]{1,0:T(8,128)S(1)} collective-permute-done((f32[200,128]{1,0:T(8,128)S(1)}, f32[200,128]{1,0:T(8,128)S(1)}, u32[]{:S(2)}, u32[]{:S(2)}) %collective-permute-start.4) | collective-permute-done | bytes 102432 | tf_op jit(solution)/shard_map/ppermute | solution.py:266
  16.6 0.8 %shard_map.65 = f32[64,384]{1,0:T(8,128)S(1)} custom-call(f32[200,128]{1,0:T(8,128)S(1)} %collective-permute-done.5.refs_0_.refs_1_.block, bf16[384,256]{1,0:T(8,128)(2,1)S(1)} %get-tuple-element.28.lhs_ref, f32[2,384,128]{2,1,0:T(8,128)S(1)} %get-tuple-element.29.vec_ref, f32[200,128]{1,0:T(8,128)S(1)} %collective-permute-done.4.col.refs_3_, ...), custom_call_target="tpu_custom_call" | custom-call | bytes 1048576 | tf_op jit(solution)/shard_map/pallas_call | solution.py:224
  17.3 0.1 collective-permute-start.6
  17.4 0.8 %shard_map.64 = f32[64,384]{1,0:T(8,128)S(1)} custom-call(f32[200,128]{1,0:T(8,128)S(1)} %collective-permute-done.1.refs_1_.refs_0_.block, bf16[384,256]{1,0:T(8,128)(2,1)S(1)} %get-tuple-element.21.lhs_ref, f32[2,384,128]{2,1,0:T(8,128)S(1)} %get-tuple-element.22.vec_ref, f32[200,128]{1,0:T(8,128)S(1)} %collective-permute-done.4.col.refs_3_, ...), custom_call_target="tpu_custom_call" | custom-call | bytes 1048576 | tf_op jit(solution)/shard_map/pallas_call | solution.py:224
  18.2 0.5 %collective-permute-done.6 = f32[64,384]{1,0:T(8,128)S(1)} collective-permute-done((f32[64,384]{1,0:T(8,128)S(1)}, f32[64,384]{1,0:T(8,128)S(1)}, u32[]{:S(2)}, u32[]{:S(2)}) %collective-permute-start.6) | collective-permute-done | bytes 98336 | tf_op jit(solution)/shard_map/ppermute | solution.py:266
  18.7 1.2 %collective-permute-start.7 = (f32[64,384]{1,0:T(8,128)S(1)}, f32[64,384]{1,0:T(8,128)S(1)}, u32[]{:S(2)}, u32[]{:S(2)}) collective-permute-start(f32[64,384]{1,0:T(8,128)S(1)} %add.6), channel_id=1, source_target_pairs={{0,2},{1,3},{2,0},{3,1},{4,6},{5,7},{6,4},{7,5},{8,10},{9,11},{10,... | collective-permute-start | bytes 294920 | tf_op jit(solution)/shard_map/ppermute | solution.py:266
  19.9 1.9 %shard_map.66 = (f32[64,384]{1,0:T(8,128)S(1)}, f32[64,384]{1,0:T(8,128)S(1)}) custom-call(f32[200,128]{1,0:T(8,128)S(1)} %shard_map.59.refs_0_.refs_1_.refs_2_, f32[200,128]{1,0:T(8,128)S(1)} %collective-permute-done.2.refs_0_.refs_1_, f32[200,128]{1,0:T(8,128)S(1)} %collective-permute-done.3.refs_2_, f32[200,128]{1,0:T(8,128)S(1)} %collective-permute-done.4.col.refs_3_, ...), custom_call_target="tpu_custom_call" | custom-call | bytes 1048576 | tf_op jit(solution)/shard_map/pallas_call | solution.py:167
  21.8 0.1 collective-permute-start.8
  21.9 1.7 %collective-permute-done.7 = f32[64,384]{1,0:T(8,128)S(1)} collective-permute-done((f32[64,384]{1,0:T(8,128)S(1)}, f32[64,384]{1,0:T(8,128)S(1)}, u32[]{:S(2)}, u32[]{:S(2)}) %collective-permute-start.7) | collective-permute-done | bytes 98336 | tf_op jit(solution)/shard_map/ppermute | solution.py:266
  23.6 0.0 collective-permute-done.8.near_ref
  23.6 0.6 %shard_map.67 = (f32[64,256]{1,0:T(8,128)}, f32[64,128]{1,0:T(8,128)}) custom-call(f32[64,384]{1,0:T(8,128)S(1)} %add.7.mine_ref, f32[64,384]{1,0:T(8,128)S(1)} %collective-permute-done.8.near_ref), custom_call_target="tpu_custom_call" | custom-call | tf_op jit(solution)/shard_map/pallas_call | solution.py:296
  (2 shorter events, 0.0 us)
Async XLA Ops:
  1.5 8.1 %collective-permute-start = (f32[200,128]{1,0:T(8,128)S(1)}, f32[200,128]{1,0:T(8,128)S(1)}, u32[]{:S(2)}, u32[]{:S(2)}) collective-permute-start(f32[200,128]{1,0:T(8,128)S(1)} %shard_map.59.refs_0_.refs_1_.refs_2_), channel_id=1, source_target_pairs={{0,12},{1,13},{2,14},{3,15},{4,8},{5,9},{6,10},{7,11},{8,4},{9,5},... | collective-permute-start | bytes 307208 | tf_op jit(solution)/shard_map/ppermute | solution.py:266
  6.6 4.7 %collective-permute-start.1 = (f32[200,128]{1,0:T(8,128)S(1)}, f32[200,128]{1,0:T(8,128)S(1)}, u32[]{:S(2)}, u32[]{:S(2)}) collective-permute-start(f32[200,128]{1,0:T(8,128)S(1)} %shard_map.59.refs_0_.refs_1_.refs_2_), channel_id=1, source_target_pairs={{0,2},{1,3},{2,0},{3,1},{4,6},{5,7},{6,4},{7,5},{8,10},{9,11},{10,... | collective-permute-start | bytes 307208 | tf_op jit(solution)/shard_map/ppermute | solution.py:266
  8.1 3.2 %collective-permute-start.2 = (f32[200,128]{1,0:T(8,128)S(1)}, f32[200,128]{1,0:T(8,128)S(1)}, u32[]{:S(2)}, u32[]{:S(2)}) collective-permute-start(f32[200,128]{1,0:T(8,128)S(1)} %shard_map.59.refs_0_.refs_1_.refs_2_), channel_id=1, source_target_pairs={{0,1},{1,0},{2,3},{3,2},{4,5},{5,4},{6,7},{7,6},{8,9},{9,8},{10,11... | collective-permute-start | bytes 307208 | tf_op jit(solution)/shard_map/ppermute | solution.py:266
  8.1 6.5 %collective-permute-start.3 = (f32[200,128]{1,0:T(8,128)S(1)}, f32[200,128]{1,0:T(8,128)S(1)}, u32[]{:S(2)}, u32[]{:S(2)}) collective-permute-start(f32[200,128]{1,0:T(8,128)S(1)} %shard_map.59.refs_0_.refs_1_.refs_2_), channel_id=1, source_target_pairs={{0,4},{1,5},{2,6},{3,7},{4,0},{5,1},{6,2},{7,3},{8,12},{9,13},{10,... | collective-permute-start | bytes 307208 | tf_op jit(solution)/shard_map/ppermute | solution.py:266
  8.1 8.4 %collective-permute-start.4 = (f32[200,128]{1,0:T(8,128)S(1)}, f32[200,128]{1,0:T(8,128)S(1)}, u32[]{:S(2)}, u32[]{:S(2)}) collective-permute-start(f32[200,128]{1,0:T(8,128)S(1)} %shard_map.59.refs_0_.refs_1_.refs_2_), channel_id=1, source_target_pairs={{0,8},{1,9},{2,10},{3,11},{4,12},{5,13},{6,14},{7,15},{8,0},{9,1},... | collective-permute-start | bytes 307208 | tf_op jit(solution)/shard_map/ppermute | solution.py:266
  11.3 1.9 %collective-permute-start.5 = (f32[200,128]{1,0:T(8,128)S(1)}, f32[200,128]{1,0:T(8,128)S(1)}, u32[]{:S(2)}, u32[]{:S(2)}) collective-permute-start(f32[200,128]{1,0:T(8,128)S(1)} %collective-permute-done.1.refs_1_.refs_0_.block), channel_id=1, source_target_pairs={{0,1},{1,0},{2,3},{3,2},{4,5},{5,4},{6,7},{7,6},{8,9},{9,8},{10,11... | collective-permute-start | bytes 307208 | tf_op jit(solution)/shard_map/ppermute | solution.py:266
  17.3 1.4 %collective-permute-start.6 = (f32[64,384]{1,0:T(8,128)S(1)}, f32[64,384]{1,0:T(8,128)S(1)}, u32[]{:S(2)}, u32[]{:S(2)}) collective-permute-start(f32[64,384]{1,0:T(8,128)S(1)} %shard_map.65), channel_id=1, source_target_pairs={{0,1},{1,0},{2,3},{3,2},{4,5},{5,4},{6,7},{7,6},{8,9},{9,8},{10,11... | collective-permute-start | bytes 294920 | tf_op jit(solution)/shard_map/ppermute | solution.py:266
  18.7 4.9 %collective-permute-start.7 = (f32[64,384]{1,0:T(8,128)S(1)}, f32[64,384]{1,0:T(8,128)S(1)}, u32[]{:S(2)}, u32[]{:S(2)}) collective-permute-start(f32[64,384]{1,0:T(8,128)S(1)} %add.6), channel_id=1, source_target_pairs={{0,2},{1,3},{2,0},{3,1},{4,6},{5,7},{6,4},{7,5},{8,10},{9,11},{10,... | collective-permute-start | bytes 294920 | tf_op jit(solution)/shard_map/ppermute | solution.py:266
  21.8 1.8 %collective-permute-start.8 = (f32[64,384]{1,0:T(8,128)S(1)}, f32[64,384]{1,0:T(8,128)S(1)}, u32[]{:S(2)}, u32[]{:S(2)}) collective-permute-start(f32[64,384]{1,0:T(8,128)S(1)} %get-tuple-element.35), channel_id=1, source_target_pairs={{0,1},{1,0},{2,3},{3,2},{4,5},{5,4},{6,7},{7,6},{8,9},{9,8},{10,11... | collective-permute-start | bytes 294920 | tf_op jit(solution)/shard_map/ppermute | solution.py:266

commit v6 on v5

--- a/solution.py
+++ b/solution.py
@@ -267,18 +267,19 @@
 
     terms = functools.partial(pair_terms, shape, totals)
     across = swap(packed, 2)
-    beside = swap(packed, 1)
     from_z = {k: swap(packed, k) for k in range(4, devices, 4)}
     arrival = sorted(from_z, key=lambda k: (k % 8 == 0, -k))
     early, middle, last = from_z[arrival[0]], arrival[1:-1], from_z[arrival[-1]]
     near_z = from_z[middle[-1]]
-    (mine,) = terms([packed], [packed, early], [None], [((0,), (0, 1), True)])
-    mine, later, beside = lax.optimization_barrier((mine, across, beside))
+    mine, *row_own = terms([packed], [packed], [None], [((0,), (0,), True)], 0, 0)
+    mine = late_terms(shape, totals, (packed, *row_own), early, mine)
+    mine, later, again = lax.optimization_barrier((mine, across, packed))
     corner = swap(later, 1)
-    jobs = [((0, 1), (0, 1), False)]
-    near, wide, *row_later = terms([beside, later], [packed, early], [None] * 2, jobs, 10**10, 1)
-    corner, wide = lax.optimization_barrier((corner, wide))
-    sent, *row_corner = terms([corner], [packed, early], [None], [((0,), (0, 1), False)], 0, 0)
+    beside = swap(again, 1)
+    wide, *row_later = terms([later], [packed, early], [None], [((0,), (0, 1), False)], 10**10, 0)
+    near = None
+    corner, beside, wide = lax.optimization_barrier((corner, beside, wide))
+    near, sent, *row_corner = terms([beside, corner], [packed, early], [None] * 2, [((0, 1), (0, 1), False)], 0, 1)
     wide, sent = terms([across, corner], [near_z], [wide, sent], [((0, 1), (0,), False)])
     for at in range(0, len(middle) - 1, 2):
         group = [from_z[k] for k in middle[at : min(at + 2, len(middle) - 1)]]

time: 24.5 us -> 24.3 us (level)
  waiting for transfers between devices: 3.92 us -> 2.33 us
  starting transfers between devices: 8.8 us -> 9.76 us
  Pallas kernels: 10.8 us -> 11.3 us
    ppermute x9, waiting for transfers between devices: 3.92 us -> 2.33 us  [swap(): return lax.ppermute(value, 'src', [(i, i ^ bits) for i in range(devices)])]
    ppermute x9, starting transfers between devices: 8.8 us -> 9.76 us  [swap(): return lax.ppermute(value, 'src', [(i, i ^ bits) for i in range(devices)])]
    pallas_call x2 -> x3, Pallas kernels: 1.52 us -> 2.29 us  [late_terms(): pl.pallas_call(functools.partial(late_kernel, shape, totals), out_shape=j...]
    pallas_call x5, Pallas kernels: 7.8 us -> 7.48 us  [pair_terms(): pl.pallas_call(functools.partial(pair_kernel, shape, len(rows), len(cols)...]
  transfers between devices with their start and end apart: 9 -> 9, of which waited for: 6 -> 4; matrix products, arithmetic and copies ran while one was open for 0% -> 0% of each run, Pallas kernels for 35% -> 37%
where the time goes in v6:
time: 24.3 us; the launch traced here: 24.1 us
  Pallas kernels  11.3 us (47%)
  starting transfers between devices  9.76 us (40%)
  waiting for transfers between devices  2.33 us (10%)
  between operations  0.75 us (3%)
    ppermute x9, starting transfers between devices, swap(): return lax.ppermute(value, 'src', [(i, i ^ bits) for i in range(devices)])  9.76 us
    pallas_call x5, Pallas kernels, pair_terms(): pl.pallas_call(functools.partial(pair_kernel, shape, len(rows), len(cols)...  7.48 us
    ppermute x9, waiting for transfers between devices, swap(): return lax.ppermute(value, 'src', [(i, i ^ bits) for i in range(devices)])  2.33 us
    pallas_call x3, Pallas kernels, late_terms(): pl.pallas_call(functools.partial(late_kernel, shape, totals), out_shape=j...  2.29 us
    pallas_call x1, Pallas kernels, body(): pl.pallas_call(functools.partial(pack_kernel, slabs, feats), out_shape=pl...  0.87 us
    pallas_call x1, Pallas kernels, body(): pl.pallas_call(finish_kernel, out_shape=[jax.ShapeDtypeStruct(src_latent....  0.65 us
  transfers between devices with their start and end apart: 9, of which 4 were waited for; matrix products, arithmetic and copies ran while one was open for 0% of the time, Pallas kernels for 37%

profile of v6, /device:TPU:0, one launch (start us, length us, event | category | flops | bytes accessed | tf_op | source)
XLA Modules:
  0.0 24.1 jit_solution(12967238072301377134)
XLA Ops:
  0.6 0.9 %shard_map.59.refs_0_.refs_1_.block.refs_2_ = f32[200,128]{1,0:T(8,128)S(1)} custom-call(f32[64,256]{1,0:T(8,128)} %src_ref.1, f32[2,256]{1,0:T(2,128)} %srcp_ref.1, f32[64,128]{1,0:T(8,128)} %tgt_ref.1, f32[2,128]{1,0:T(2,128)} %tgtp_ref.1), custom_call_target="tpu_custom_call" | custom-call | tf_op jit(solution)/shard_map/pallas_call | solution.py:252
  1.5 5.1 %collective-permute-start = (f32[200,128]{1,0:T(8,128)S(1)}, f32[200,128]{1,0:T(8,128)S(1)}, u32[]{:S(2)}, u32[]{:S(2)}) collective-permute-start(f32[200,128]{1,0:T(8,128)S(1)} %shard_map.59.refs_0_.refs_1_.block.refs_2_), channel_id=1, source_target_pairs={{0,12},{1,13},{2,14},{3,15},{4,8},{5,9},{6,10},{7,11},{8,4},{9,5},... | collective-permute-start | bytes 307208 | tf_op jit(solution)/shard_map/ppermute | solution.py:266
  6.6 1.5 %collective-permute-start.1 = (f32[200,128]{1,0:T(8,128)S(1)}, f32[200,128]{1,0:T(8,128)S(1)}, u32[]{:S(2)}, u32[]{:S(2)}) collective-permute-start(f32[200,128]{1,0:T(8,128)S(1)} %shard_map.59.refs_0_.refs_1_.block.refs_2_), channel_id=1, source_target_pairs={{0,2},{1,3},{2,0},{3,1},{4,6},{5,7},{6,4},{7,5},{8,10},{9,11},{10,... | collective-permute-start | bytes 307208 | tf_op jit(solution)/shard_map/ppermute | solution.py:266
  8.1 0.0 collective-permute-start.4
  8.1 0.8 %collective-permute-start.5 = (f32[200,128]{1,0:T(8,128)S(1)}, f32[200,128]{1,0:T(8,128)S(1)}, u32[]{:S(2)}, u32[]{:S(2)}) collective-permute-start(f32[200,128]{1,0:T(8,128)S(1)} %shard_map.59.refs_0_.refs_1_.block.refs_2_), channel_id=1, source_target_pairs={{0,8},{1,9},{2,10},{3,11},{4,12},{5,13},{6,14},{7,15},{8,0},{9,1},... | collective-permute-start | bytes 307208 | tf_op jit(solution)/shard_map/ppermute | solution.py:266
  8.9 1.1 %shard_map.60 = (f32[64,384]{1,0:T(8,128)S(1)}, bf16[384,256]{1,0:T(8,128)(2,1)S(1)}, f32[2,384,128]{2,1,0:T(8,128)S(1)}) custom-call(f32[200,128]{1,0:T(8,128)S(1)} %shard_map.59.refs_0_.refs_1_.block.refs_2_, f32[200,128]{1,0:T(8,128)S(1)} %shard_map.59.refs_0_.refs_1_.block.refs_2_), custom_call_target="tpu_custom_call" | custom-call | bytes 1048576 | tf_op jit(solution)/shard_map/pallas_call | solution.py:167
  10.0 0.3 %collective-permute-done.col.refs_2_.refs_3_ = f32[200,128]{1,0:T(8,128)S(1)} collective-permute-done((f32[200,128]{1,0:T(8,128)S(1)}, f32[200,128]{1,0:T(8,128)S(1)}, u32[]{:S(2)}, u32[]{:S(2)}) %collective-permute-start) | collective-permute-done | bytes 102432 | tf_op jit(solution)/shard_map/ppermute | solution.py:266
  10.3 0.8 %shard_map.61.refs_4_ = f32[64,384]{1,0:T(8,128)S(1)} custom-call(f32[200,128]{1,0:T(8,128)S(1)} %shard_map.59.refs_0_.refs_1_.block.refs_2_, bf16[384,256]{1,0:T(8,128)(2,1)S(1)} %get-tuple-element.23.lhs_ref, f32[2,384,128]{2,1,0:T(8,128)S(1)} %get-tuple-element.24.vec_ref, f32[200,128]{1,0:T(8,128)S(1)} %collective-permute-done.col.refs_2_.refs_3_, ...), custom_call_target="tpu_custom_call" | custom-call | bytes 1048576 | tf_op jit(solution)/shard_map/pallas_call | solution.py:224
  11.1 0.2 collective-permute-done.1.refs_0_.block
  11.3 0.0 collective-permute-start.2
  11.3 0.5 %collective-permute-start.3 = (f32[200,128]{1,0:T(8,128)S(1)}, f32[200,128]{1,0:T(8,128)S(1)}, u32[]{:S(2)}, u32[]{:S(2)}) collective-permute-start(f32[200,128]{1,0:T(8,128)S(1)} %shard_map.59.refs_0_.refs_1_.block.refs_2_), channel_id=1, source_target_pairs={{0,1},{1,0},{2,3},{3,2},{4,5},{5,4},{6,7},{7,6},{8,9},{9,8},{10,11... | collective-permute-start | bytes 307208 | tf_op jit(solution)/shard_map/ppermute | solution.py:266
  11.8 1.4 %shard_map.62 = (f32[64,384]{1,0:T(8,128)S(1)}, bf16[384,256]{1,0:T(8,128)(2,1)S(1)}, f32[2,384,128]{2,1,0:T(8,128)S(1)}) custom-call(f32[200,128]{1,0:T(8,128)S(1)} %collective-permute-done.1.refs_0_.block, f32[200,128]{1,0:T(8,128)S(1)} %shard_map.59.refs_0_.refs_1_.block.refs_2_, f32[200,128]{1,0:T(8,128)S(1)} %collective-permute-done.col.refs_2_.refs_3_), custom_call_target="tpu_custom_call" | custom-call | flops 10000000000 | bytes 1048576 | tf_op jit(solution)/shard_map/pallas_call | solution.py:167
  13.2 0.0 collective-permute-done.2.refs_1_.block
  13.2 0.0 collective-permute-done.3.refs_0_.refs_1_
  13.2 1.9 %shard_map.63 = (f32[64,384]{1,0:T(8,128)S(1)}, f32[64,384]{1,0:T(8,128)S(1)}, bf16[384,256]{1,0:T(8,128)(2,1)S(1)}, f32[2,384,128]{2,1,0:T(8,128)S(1)}) custom-call(f32[200,128]{1,0:T(8,128)S(1)} %collective-permute-done.3.refs_0_.refs_1_, f32[200,128]{1,0:T(8,128)S(1)} %collective-permute-done.2.refs_1_.block, ...), custom_call_target="tpu_custom_call" | custom-call | bytes 1048576 | tf_op jit(solution)/shard_map/pallas_call | solution.py:167
  15.1 0.0 collective-permute-done.4.refs_2_
  15.1 1.2 %shard_map.64 = (f32[64,384]{1,0:T(8,128)S(1)}, f32[64,384]{1,0:T(8,128)S(1)}) custom-call(f32[200,128]{1,0:T(8,128)S(1)} %collective-permute-done.1.refs_0_.block, f32[200,128]{1,0:T(8,128)S(1)} %collective-permute-done.2.refs_1_.block, f32[200,128]{1,0:T(8,128)S(1)} %collective-permute-done.4.refs_2_, f32[64,384]{1,0:T(8,128)S(1)} %get-tuple-element.33.refs_3_, ...), custom_call_target="tpu_custom_call" | custom-call | bytes 1048576 | tf_op jit(solution)/shard_map/pallas_call | solution.py:167
  16.4 0.0 collective-permute-done.5.col.refs_3_
  16.4 0.8 %shard_map.66 = f32[64,384]{1,0:T(8,128)S(1)} custom-call(f32[200,128]{1,0:T(8,128)S(1)} %collective-permute-done.2.refs_1_.block, bf16[384,256]{1,0:T(8,128)(2,1)S(1)} %get-tuple-element.36.lhs_ref, f32[2,384,128]{2,1,0:T(8,128)S(1)} %get-tuple-element.37.vec_ref, f32[200,128]{1,0:T(8,128)S(1)} %collective-permute-done.5.col.refs_3_, ...), custom_call_target="tpu_custom_call" | custom-call | bytes 1048576 | tf_op jit(solution)/shard_map/pallas_call | solution.py:224
  17.1 0.1 collective-permute-start.6
  17.2 0.8 %shard_map.65 = f32[64,384]{1,0:T(8,128)S(1)} custom-call(f32[200,128]{1,0:T(8,128)S(1)} %collective-permute-done.1.refs_0_.block, bf16[384,256]{1,0:T(8,128)(2,1)S(1)} %get-tuple-element.30.lhs_ref, f32[2,384,128]{2,1,0:T(8,128)S(1)} %get-tuple-element.31.vec_ref, f32[200,128]{1,0:T(8,128)S(1)} %collective-permute-done.5.col.refs_3_, ...), custom_call_target="tpu_custom_call" | custom-call | bytes 1048576 | tf_op jit(solution)/shard_map/pallas_call | solution.py:224
  18.0 0.5 %collective-permute-done.6 = f32[64,384]{1,0:T(8,128)S(1)} collective-permute-done((f32[64,384]{1,0:T(8,128)S(1)}, f32[64,384]{1,0:T(8,128)S(1)}, u32[]{:S(2)}, u32[]{:S(2)}) %collective-permute-start.6) | collective-permute-done | bytes 98336 | tf_op jit(solution)/shard_map/ppermute | solution.py:266
  18.5 1.7 %collective-permute-start.7 = (f32[64,384]{1,0:T(8,128)S(1)}, f32[64,384]{1,0:T(8,128)S(1)}, u32[]{:S(2)}, u32[]{:S(2)}) collective-permute-start(f32[64,384]{1,0:T(8,128)S(1)} %add.6), channel_id=1, source_target_pairs={{0,2},{1,3},{2,0},{3,1},{4,6},{5,7},{6,4},{7,5},{8,10},{9,11},{10,... | collective-permute-start | bytes 294920 | tf_op jit(solution)/shard_map/ppermute | solution.py:266
  20.2 1.9 %shard_map.67 = (f32[64,384]{1,0:T(8,128)S(1)}, f32[64,384]{1,0:T(8,128)S(1)}) custom-call(f32[200,128]{1,0:T(8,128)S(1)} %shard_map.59.refs_0_.refs_1_.block.refs_2_, f32[200,128]{1,0:T(8,128)S(1)} %collective-permute-done.3.refs_0_.refs_1_, f32[200,128]{1,0:T(8,128)S(1)} %collective-permute-done.4.refs_2_, ...), custom_call_target="tpu_custom_call" | custom-call | bytes 1048576 | tf_op jit(solution)/shard_map/pallas_call | solution.py:167
  22.1 0.1 collective-permute-start.8
  22.2 1.2 %collective-permute-done.7 = f32[64,384]{1,0:T(8,128)S(1)} collective-permute-done((f32[64,384]{1,0:T(8,128)S(1)}, f32[64,384]{1,0:T(8,128)S(1)}, u32[]{:S(2)}, u32[]{:S(2)}) %collective-permute-start.7) | collective-permute-done | bytes 98336 | tf_op jit(solution)/shard_map/ppermute | solution.py:266
  23.4 0.0 collective-permute-done.8.near_ref
  23.5 0.6 %shard_map.68 = (f32[64,256]{1,0:T(8,128)}, f32[64,128]{1,0:T(8,128)}) custom-call(f32[64,384]{1,0:T(8,128)S(1)} %add.7.mine_ref, f32[64,384]{1,0:T(8,128)S(1)} %collective-permute-done.8.near_ref), custom_call_target="tpu_custom_call" | custom-call | tf_op jit(solution)/shard_map/pallas_call | solution.py:297
  (2 shorter events, 0.0 us)
Async XLA Ops:
  1.5 8.8 %collective-permute-start = (f32[200,128]{1,0:T(8,128)S(1)}, f32[200,128]{1,0:T(8,128)S(1)}, u32[]{:S(2)}, u32[]{:S(2)}) collective-permute-start(f32[200,128]{1,0:T(8,128)S(1)} %shard_map.59.refs_0_.refs_1_.block.refs_2_), channel_id=1, source_target_pairs={{0,12},{1,13},{2,14},{3,15},{4,8},{5,9},{6,10},{7,11},{8,4},{9,5},... | collective-permute-start | bytes 307208 | tf_op jit(solution)/shard_map/ppermute | solution.py:266
  6.6 4.7 %collective-permute-start.1 = (f32[200,128]{1,0:T(8,128)S(1)}, f32[200,128]{1,0:T(8,128)S(1)}, u32[]{:S(2)}, u32[]{:S(2)}) collective-permute-start(f32[200,128]{1,0:T(8,128)S(1)} %shard_map.59.refs_0_.refs_1_.block.refs_2_), channel_id=1, source_target_pairs={{0,2},{1,3},{2,0},{3,1},{4,6},{5,7},{6,4},{7,5},{8,10},{9,11},{10,... | collective-permute-start | bytes 307208 | tf_op jit(solution)/shard_map/ppermute | solution.py:266
  8.1 7.0 %collective-permute-start.4 = (f32[200,128]{1,0:T(8,128)S(1)}, f32[200,128]{1,0:T(8,128)S(1)}, u32[]{:S(2)}, u32[]{:S(2)}) collective-permute-start(f32[200,128]{1,0:T(8,128)S(1)} %shard_map.59.refs_0_.refs_1_.block.refs_2_), channel_id=1, source_target_pairs={{0,4},{1,5},{2,6},{3,7},{4,0},{5,1},{6,2},{7,3},{8,12},{9,13},{10,... | collective-permute-start | bytes 307208 | tf_op jit(solution)/shard_map/ppermute | solution.py:266
  8.1 8.2 %collective-permute-start.5 = (f32[200,128]{1,0:T(8,128)S(1)}, f32[200,128]{1,0:T(8,128)S(1)}, u32[]{:S(2)}, u32[]{:S(2)}) collective-permute-start(f32[200,128]{1,0:T(8,128)S(1)} %shard_map.59.refs_0_.refs_1_.block.refs_2_), channel_id=1, source_target_pairs={{0,8},{1,9},{2,10},{3,11},{4,12},{5,13},{6,14},{7,15},{8,0},{9,1},... | collective-permute-start | bytes 307208 | tf_op jit(solution)/shard_map/ppermute | solution.py:266
  11.3 1.9 %collective-permute-start.2 = (f32[200,128]{1,0:T(8,128)S(1)}, f32[200,128]{1,0:T(8,128)S(1)}, u32[]{:S(2)}, u32[]{:S(2)}) collective-permute-start(f32[200,128]{1,0:T(8,128)S(1)} %collective-permute-done.1.refs_0_.block), channel_id=1, source_target_pairs={{0,1},{1,0},{2,3},{3,2},{4,5},{5,4},{6,7},{7,6},{8,9},{9,8},{10,11... | collective-permute-start | bytes 307208 | tf_op jit(solution)/shard_map/ppermute | solution.py:266
  11.3 1.9 %collective-permute-start.3 = (f32[200,128]{1,0:T(8,128)S(1)}, f32[200,128]{1,0:T(8,128)S(1)}, u32[]{:S(2)}, u32[]{:S(2)}) collective-permute-start(f32[200,128]{1,0:T(8,128)S(1)} %shard_map.59.refs_0_.refs_1_.block.refs_2_), channel_id=1, source_target_pairs={{0,1},{1,0},{2,3},{3,2},{4,5},{5,4},{6,7},{7,6},{8,9},{9,8},{10,11... | collective-permute-start | bytes 307208 | tf_op jit(solution)/shard_map/ppermute | solution.py:266
  17.1 1.4 %collective-permute-start.6 = (f32[64,384]{1,0:T(8,128)S(1)}, f32[64,384]{1,0:T(8,128)S(1)}, u32[]{:S(2)}, u32[]{:S(2)}) collective-permute-start(f32[64,384]{1,0:T(8,128)S(1)} %shard_map.66), channel_id=1, source_target_pairs={{0,1},{1,0},{2,3},{3,2},{4,5},{5,4},{6,7},{7,6},{8,9},{9,8},{10,11... | collective-permute-start | bytes 294920 | tf_op jit(solution)/shard_map/ppermute | solution.py:266
  18.5 4.9 %collective-permute-start.7 = (f32[64,384]{1,0:T(8,128)S(1)}, f32[64,384]{1,0:T(8,128)S(1)}, u32[]{:S(2)}, u32[]{:S(2)}) collective-permute-start(f32[64,384]{1,0:T(8,128)S(1)} %add.6), channel_id=1, source_target_pairs={{0,2},{1,3},{2,0},{3,1},{4,6},{5,7},{6,4},{7,5},{8,10},{9,11},{10,... | collective-permute-start | bytes 294920 | tf_op jit(solution)/shard_map/ppermute | solution.py:266
  22.1 1.4 %collective-permute-start.8 = (f32[64,384]{1,0:T(8,128)S(1)}, f32[64,384]{1,0:T(8,128)S(1)}, u32[]{:S(2)}, u32[]{:S(2)}) collective-permute-start(f32[64,384]{1,0:T(8,128)S(1)} %get-tuple-element.43), channel_id=1, source_target_pairs={{0,1},{1,0},{2,3},{3,2},{4,5},{5,4},{6,7},{7,6},{8,9},{9,8},{10,11... | collective-permute-start | bytes 294920 | tf_op jit(solution)/shard_map/ppermute | solution.py:266

commit v7 on v6

--- a/solution.py
+++ b/solution.py
@@ -99,11 +99,11 @@
             mid, least = split(low)
             both = jnp.concatenate([high, low], 0).T.astype(bf16)
             trans.append(jnp.concatenate([both, both], 1))
-            stack = jnp.concatenate([high, mid, least, jnp.ones((16, LANES), f32)], 0)
+            stack = jnp.concatenate([high, mid, jnp.ones((16, LANES), f32), least], 0)
             values.append(stack.astype(bf16))
             vecs.append(jnp.concatenate(pots + [jnp.zeros((6, LANES), f32)], 0).T)
         value = jnp.concatenate(values, 1)
-        return jnp.concatenate(trans, 0), jnp.concatenate([value, value], 1), jnp.concatenate(vecs, 0)
+        return jnp.concatenate(trans, 0), value, jnp.concatenate(vecs, 0)
 
     def run_tile(tile, prepared, own):
         row_kind = 0 if tile[0][1] < src_slabs else 1
@@ -124,13 +124,15 @@
                             same = (row_id == col_id) & (row_id >= 0) & (row_id < LANES)
                             weight = jnp.where(same, 0.0, weight)
             high, low = split(weight)
-            both = jnp.concatenate([high.astype(bf16), low.astype(bf16)], 0)
-            part = jnp.dot(value, both, preferred_element_type=f32)
+            part = jnp.dot(value, high.astype(bf16), preferred_element_type=f32)
+            most = 2 * feats + 16
+            fine = jnp.dot(value[:most], low.astype(bf16), preferred_element_type=f32)
+            part = jnp.concatenate([part[:most] + fine, part[most:]], 0)
             sums[kind] = part if sums[kind] is None else sums[kind] + part
         sign = 1.0 if row_kind == 0 else -1.0
         total = sums[1] * (sign / totals[1]) - sums[0] * (sign / totals[0])
-        mixed = total[0:feats] + total[feats : 2 * feats] + total[2 * feats : 3 * feats]
-        mass = total[3 * feats : 3 * feats + 1]
+        mixed = total[0:feats] + total[feats : 2 * feats] + total[2 * feats + 16 :]
+        mass = total[2 * feats : 2 * feats + 1]
         for across, (row, slab) in enumerate(tile):
             piece = slice(across * LANES, (across + 1) * LANES)
             value = rows[row][slab * feats : (slab + 1) * feats, :]

time: 24.3 us -> 23.9 us (0.984)
  Pallas kernels: 11.3 us -> 10.7 us
    pallas_call x5, Pallas kernels: 7.48 us -> 6.95 us  [pair_terms(): pl.pallas_call(functools.partial(pair_kernel, shape, len(rows), len(cols)...]
  transfers between devices with their start and end apart: 9 -> 9, of which waited for: 4 -> 4; matrix products, arithmetic and copies ran while one was open for 0% -> 0% of each run, Pallas kernels for 37% -> 36%
where the time goes in v7:
time: 23.9 us; the launch traced here: 23.7 us
  Pallas kernels  10.7 us (45%)
  starting transfers between devices  9.75 us (41%)
  waiting for transfers between devices  2.46 us (10%)
  between operations  0.75 us (3%)
    ppermute x9, starting transfers between devices, swap(): return lax.ppermute(value, 'src', [(i, i ^ bits) for i in range(devices)])  9.75 us
    pallas_call x5, Pallas kernels, pair_terms(): pl.pallas_call(functools.partial(pair_kernel, shape, len(rows), len(cols)...  6.95 us
    ppermute x9, waiting for transfers between devices, swap(): return lax.ppermute(value, 'src', [(i, i ^ bits) for i in range(devices)])  2.46 us
    pallas_call x3, Pallas kernels, late_terms(): pl.pallas_call(functools.partial(late_kernel, shape, totals), out_shape=j...  2.29 us
    pallas_call x1, Pallas kernels, body(): pl.pallas_call(functools.partial(pack_kernel, slabs, feats), out_shape=pl...  0.87 us
    pallas_call x1, Pallas kernels, body(): pl.pallas_call(finish_kernel, out_shape=[jax.ShapeDtypeStruct(src_latent....  0.65 us
  transfers between devices with their start and end apart: 9, of which 4 were waited for; matrix products, arithmetic and copies ran while one was open for 0% of the time, Pallas kernels for 36%

profile of v7, /device:TPU:0, one launch (start us, length us, event | category | flops | bytes accessed | tf_op | source)
XLA Modules:
  0.0 23.7 jit_solution(8061963364484213564)
XLA Ops:
  0.6 0.9 %shard_map.59.refs_0_.refs_1_.block.refs_2_ = f32[200,128]{1,0:T(8,128)S(1)} custom-call(f32[64,256]{1,0:T(8,128)} %src_ref.1, f32[2,256]{1,0:T(2,128)} %srcp_ref.1, f32[64,128]{1,0:T(8,128)} %tgt_ref.1, f32[2,128]{1,0:T(2,128)} %tgtp_ref.1), custom_call_target="tpu_custom_call" | custom-call | tf_op jit(solution)/shard_map/pallas_call | solution.py:254
  1.5 5.1 %collective-permute-start = (f32[200,128]{1,0:T(8,128)S(1)}, f32[200,128]{1,0:T(8,128)S(1)}, u32[]{:S(2)}, u32[]{:S(2)}) collective-permute-start(f32[200,128]{1,0:T(8,128)S(1)} %shard_map.59.refs_0_.refs_1_.block.refs_2_), channel_id=1, source_target_pairs={{0,12},{1,13},{2,14},{3,15},{4,8},{5,9},{6,10},{7,11},{8,4},{9,5},... | collective-permute-start | bytes 307208 | tf_op jit(solution)/shard_map/ppermute | solution.py:268
  6.6 1.5 %collective-permute-start.1 = (f32[200,128]{1,0:T(8,128)S(1)}, f32[200,128]{1,0:T(8,128)S(1)}, u32[]{:S(2)}, u32[]{:S(2)}) collective-permute-start(f32[200,128]{1,0:T(8,128)S(1)} %shard_map.59.refs_0_.refs_1_.block.refs_2_), channel_id=1, source_target_pairs={{0,2},{1,3},{2,0},{3,1},{4,6},{5,7},{6,4},{7,5},{8,10},{9,11},{10,... | collective-permute-start | bytes 307208 | tf_op jit(solution)/shard_map/ppermute | solution.py:268
  8.1 0.0 collective-permute-start.4
  8.1 0.8 %collective-permute-start.5 = (f32[200,128]{1,0:T(8,128)S(1)}, f32[200,128]{1,0:T(8,128)S(1)}, u32[]{:S(2)}, u32[]{:S(2)}) collective-permute-start(f32[200,128]{1,0:T(8,128)S(1)} %shard_map.59.refs_0_.refs_1_.block.refs_2_), channel_id=1, source_target_pairs={{0,8},{1,9},{2,10},{3,11},{4,12},{5,13},{6,14},{7,15},{8,0},{9,1},... | collective-permute-start | bytes 307208 | tf_op jit(solution)/shard_map/ppermute | solution.py:268
  8.9 1.0 %shard_map.60 = (f32[64,384]{1,0:T(8,128)S(1)}, bf16[384,256]{1,0:T(8,128)(2,1)S(1)}, f32[2,384,128]{2,1,0:T(8,128)S(1)}) custom-call(f32[200,128]{1,0:T(8,128)S(1)} %shard_map.59.refs_0_.refs_1_.block.refs_2_, f32[200,128]{1,0:T(8,128)S(1)} %shard_map.59.refs_0_.refs_1_.block.refs_2_), custom_call_target="tpu_custom_call" | custom-call | bytes 1048576 | tf_op jit(solution)/shard_map/pallas_call | solution.py:169
  9.9 0.4 %collective-permute-done.col.refs_2_.refs_3_ = f32[200,128]{1,0:T(8,128)S(1)} collective-permute-done((f32[200,128]{1,0:T(8,128)S(1)}, f32[200,128]{1,0:T(8,128)S(1)}, u32[]{:S(2)}, u32[]{:S(2)}) %collective-permute-start) | collective-permute-done | bytes 102432 | tf_op jit(solution)/shard_map/ppermute | solution.py:268
  10.3 0.8 %shard_map.61.refs_4_ = f32[64,384]{1,0:T(8,128)S(1)} custom-call(f32[200,128]{1,0:T(8,128)S(1)} %shard_map.59.refs_0_.refs_1_.block.refs_2_, bf16[384,256]{1,0:T(8,128)(2,1)S(1)} %get-tuple-element.23.lhs_ref, f32[2,384,128]{2,1,0:T(8,128)S(1)} %get-tuple-element.24.vec_ref, f32[200,128]{1,0:T(8,128)S(1)} %collective-permute-done.col.refs_2_.refs_3_, ...), custom_call_target="tpu_custom_call" | custom-call | bytes 1048576 | tf_op jit(solution)/shard_map/pallas_call | solution.py:226
  11.1 0.2 collective-permute-done.1.refs_0_.block
  11.3 0.0 collective-permute-start.2
  11.3 0.5 %collective-permute-start.3 = (f32[200,128]{1,0:T(8,128)S(1)}, f32[200,128]{1,0:T(8,128)S(1)}, u32[]{:S(2)}, u32[]{:S(2)}) collective-permute-start(f32[200,128]{1,0:T(8,128)S(1)} %shard_map.59.refs_0_.refs_1_.block.refs_2_), channel_id=1, source_target_pairs={{0,1},{1,0},{2,3},{3,2},{4,5},{5,4},{6,7},{7,6},{8,9},{9,8},{10,11... | collective-permute-start | bytes 307208 | tf_op jit(solution)/shard_map/ppermute | solution.py:268
  11.8 1.3 %shard_map.62 = (f32[64,384]{1,0:T(8,128)S(1)}, bf16[384,256]{1,0:T(8,128)(2,1)S(1)}, f32[2,384,128]{2,1,0:T(8,128)S(1)}) custom-call(f32[200,128]{1,0:T(8,128)S(1)} %collective-permute-done.1.refs_0_.block, f32[200,128]{1,0:T(8,128)S(1)} %shard_map.59.refs_0_.refs_1_.block.refs_2_, f32[200,128]{1,0:T(8,128)S(1)} %collective-permute-done.col.refs_2_.refs_3_), custom_call_target="tpu_custom_call" | custom-call | flops 10000000000 | bytes 1048576 | tf_op jit(solution)/shard_map/pallas_call | solution.py:169
  13.1 0.0 collective-permute-done.2.refs_1_.block
  13.1 0.0 collective-permute-done.3.refs_0_.refs_1_
  13.1 1.8 %shard_map.63 = (f32[64,384]{1,0:T(8,128)S(1)}, f32[64,384]{1,0:T(8,128)S(1)}, bf16[384,256]{1,0:T(8,128)(2,1)S(1)}, f32[2,384,128]{2,1,0:T(8,128)S(1)}) custom-call(f32[200,128]{1,0:T(8,128)S(1)} %collective-permute-done.3.refs_0_.refs_1_, f32[200,128]{1,0:T(8,128)S(1)} %collective-permute-done.2.refs_1_.block, ...), custom_call_target="tpu_custom_call" | custom-call | bytes 1048576 | tf_op jit(solution)/shard_map/pallas_call | solution.py:169
  14.9 0.0 collective-permute-done.4.refs_2_
  14.9 1.1 %shard_map.64 = (f32[64,384]{1,0:T(8,128)S(1)}, f32[64,384]{1,0:T(8,128)S(1)}) custom-call(f32[200,128]{1,0:T(8,128)S(1)} %collective-permute-done.1.refs_0_.block, f32[200,128]{1,0:T(8,128)S(1)} %collective-permute-done.2.refs_1_.block, f32[200,128]{1,0:T(8,128)S(1)} %collective-permute-done.4.refs_2_, f32[64,384]{1,0:T(8,128)S(1)} %get-tuple-element.33.refs_3_, ...), custom_call_target="tpu_custom_call" | custom-call | bytes 1048576 | tf_op jit(solution)/shard_map/pallas_call | solution.py:169
  16.0 0.0 collective-permute-done.5.col.refs_3_
  16.0 0.8 %shard_map.66 = f32[64,384]{1,0:T(8,128)S(1)} custom-call(f32[200,128]{1,0:T(8,128)S(1)} %collective-permute-done.2.refs_1_.block, bf16[384,256]{1,0:T(8,128)(2,1)S(1)} %get-tuple-element.36.lhs_ref, f32[2,384,128]{2,1,0:T(8,128)S(1)} %get-tuple-element.37.vec_ref, f32[200,128]{1,0:T(8,128)S(1)} %collective-permute-done.5.col.refs_3_, ...), custom_call_target="tpu_custom_call" | custom-call | bytes 1048576 | tf_op jit(solution)/shard_map/pallas_call | solution.py:226
  16.8 0.1 collective-permute-start.6
  16.8 0.8 %shard_map.65 = f32[64,384]{1,0:T(8,128)S(1)} custom-call(f32[200,128]{1,0:T(8,128)S(1)} %collective-permute-done.1.refs_0_.block, bf16[384,256]{1,0:T(8,128)(2,1)S(1)} %get-tuple-element.30.lhs_ref, f32[2,384,128]{2,1,0:T(8,128)S(1)} %get-tuple-element.31.vec_ref, f32[200,128]{1,0:T(8,128)S(1)} %collective-permute-done.5.col.refs_3_, ...), custom_call_target="tpu_custom_call" | custom-call | bytes 1048576 | tf_op jit(solution)/shard_map/pallas_call | solution.py:226
  17.6 0.5 %collective-permute-done.6 = f32[64,384]{1,0:T(8,128)S(1)} collective-permute-done((f32[64,384]{1,0:T(8,128)S(1)}, f32[64,384]{1,0:T(8,128)S(1)}, u32[]{:S(2)}, u32[]{:S(2)}) %collective-permute-start.6) | collective-permute-done | bytes 98336 | tf_op jit(solution)/shard_map/ppermute | solution.py:268
  18.1 1.7 %collective-permute-start.7 = (f32[64,384]{1,0:T(8,128)S(1)}, f32[64,384]{1,0:T(8,128)S(1)}, u32[]{:S(2)}, u32[]{:S(2)}) collective-permute-start(f32[64,384]{1,0:T(8,128)S(1)} %add.6), channel_id=1, source_target_pairs={{0,2},{1,3},{2,0},{3,1},{4,6},{5,7},{6,4},{7,5},{8,10},{9,11},{10,... | collective-permute-start | bytes 294920 | tf_op jit(solution)/shard_map/ppermute | solution.py:268
  19.8 1.8 %shard_map.67 = (f32[64,384]{1,0:T(8,128)S(1)}, f32[64,384]{1,0:T(8,128)S(1)}) custom-call(f32[200,128]{1,0:T(8,128)S(1)} %shard_map.59.refs_0_.refs_1_.block.refs_2_, f32[200,128]{1,0:T(8,128)S(1)} %collective-permute-done.3.refs_0_.refs_1_, f32[200,128]{1,0:T(8,128)S(1)} %collective-permute-done.4.refs_2_, ...), custom_call_target="tpu_custom_call" | custom-call | bytes 1048576 | tf_op jit(solution)/shard_map/pallas_call | solution.py:169
  21.7 0.1 collective-permute-start.8
  21.7 1.3 %collective-permute-done.7 = f32[64,384]{1,0:T(8,128)S(1)} collective-permute-done((f32[64,384]{1,0:T(8,128)S(1)}, f32[64,384]{1,0:T(8,128)S(1)}, u32[]{:S(2)}, u32[]{:S(2)}) %collective-permute-start.7) | collective-permute-done | bytes 98336 | tf_op jit(solution)/shard_map/ppermute | solution.py:268
  23.1 0.0 collective-permute-done.8.near_ref
  23.1 0.6 %shard_map.68 = (f32[64,256]{1,0:T(8,128)}, f32[64,128]{1,0:T(8,128)}) custom-call(f32[64,384]{1,0:T(8,128)S(1)} %add.7.mine_ref, f32[64,384]{1,0:T(8,128)S(1)} %collective-permute-done.8.near_ref), custom_call_target="tpu_custom_call" | custom-call | tf_op jit(solution)/shard_map/pallas_call | solution.py:299
  (2 shorter events, 0.0 us)
Async XLA Ops:
  1.5 8.8 %collective-permute-start = (f32[200,128]{1,0:T(8,128)S(1)}, f32[200,128]{1,0:T(8,128)S(1)}, u32[]{:S(2)}, u32[]{:S(2)}) collective-permute-start(f32[200,128]{1,0:T(8,128)S(1)} %shard_map.59.refs_0_.refs_1_.block.refs_2_), channel_id=1, source_target_pairs={{0,12},{1,13},{2,14},{3,15},{4,8},{5,9},{6,10},{7,11},{8,4},{9,5},... | collective-permute-start | bytes 307208 | tf_op jit(solution)/shard_map/ppermute | solution.py:268
  6.6 4.7 %collective-permute-start.1 = (f32[200,128]{1,0:T(8,128)S(1)}, f32[200,128]{1,0:T(8,128)S(1)}, u32[]{:S(2)}, u32[]{:S(2)}) collective-permute-start(f32[200,128]{1,0:T(8,128)S(1)} %shard_map.59.refs_0_.refs_1_.block.refs_2_), channel_id=1, source_target_pairs={{0,2},{1,3},{2,0},{3,1},{4,6},{5,7},{6,4},{7,5},{8,10},{9,11},{10,... | collective-permute-start | bytes 307208 | tf_op jit(solution)/shard_map/ppermute | solution.py:268
  8.1 6.8 %collective-permute-start.4 = (f32[200,128]{1,0:T(8,128)S(1)}, f32[200,128]{1,0:T(8,128)S(1)}, u32[]{:S(2)}, u32[]{:S(2)}) collective-permute-start(f32[200,128]{1,0:T(8,128)S(1)} %shard_map.59.refs_0_.refs_1_.block.refs_2_), channel_id=1, source_target_pairs={{0,4},{1,5},{2,6},{3,7},{4,0},{5,1},{6,2},{7,3},{8,12},{9,13},{10,... | collective-permute-start | bytes 307208 | tf_op jit(solution)/shard_map/ppermute | solution.py:268
  8.1 7.9 %collective-permute-start.5 = (f32[200,128]{1,0:T(8,128)S(1)}, f32[200,128]{1,0:T(8,128)S(1)}, u32[]{:S(2)}, u32[]{:S(2)}) collective-permute-start(f32[200,128]{1,0:T(8,128)S(1)} %shard_map.59.refs_0_.refs_1_.block.refs_2_), channel_id=1, source_target_pairs={{0,8},{1,9},{2,10},{3,11},{4,12},{5,13},{6,14},{7,15},{8,0},{9,1},... | collective-permute-start | bytes 307208 | tf_op jit(solution)/shard_map/ppermute | solution.py:268
  11.3 1.8 %collective-permute-start.2 = (f32[200,128]{1,0:T(8,128)S(1)}, f32[200,128]{1,0:T(8,128)S(1)}, u32[]{:S(2)}, u32[]{:S(2)}) collective-permute-start(f32[200,128]{1,0:T(8,128)S(1)} %collective-permute-done.1.refs_0_.block), channel_id=1, source_target_pairs={{0,1},{1,0},{2,3},{3,2},{4,5},{5,4},{6,7},{7,6},{8,9},{9,8},{10,11... | collective-permute-start | bytes 307208 | tf_op jit(solution)/shard_map/ppermute | solution.py:268
  11.3 1.8 %collective-permute-start.3 = (f32[200,128]{1,0:T(8,128)S(1)}, f32[200,128]{1,0:T(8,128)S(1)}, u32[]{:S(2)}, u32[]{:S(2)}) collective-permute-start(f32[200,128]{1,0:T(8,128)S(1)} %shard_map.59.refs_0_.refs_1_.block.refs_2_), channel_id=1, source_target_pairs={{0,1},{1,0},{2,3},{3,2},{4,5},{5,4},{6,7},{7,6},{8,9},{9,8},{10,11... | collective-permute-start | bytes 307208 | tf_op jit(solution)/shard_map/ppermute | solution.py:268
  16.8 1.4 %collective-permute-start.6 = (f32[64,384]{1,0:T(8,128)S(1)}, f32[64,384]{1,0:T(8,128)S(1)}, u32[]{:S(2)}, u32[]{:S(2)}) collective-permute-start(f32[64,384]{1,0:T(8,128)S(1)} %shard_map.66), channel_id=1, source_target_pairs={{0,1},{1,0},{2,3},{3,2},{4,5},{5,4},{6,7},{7,6},{8,9},{9,8},{10,11... | collective-permute-start | bytes 294920 | tf_op jit(solution)/shard_map/ppermute | solution.py:268
  18.1 4.9 %collective-permute-start.7 = (f32[64,384]{1,0:T(8,128)S(1)}, f32[64,384]{1,0:T(8,128)S(1)}, u32[]{:S(2)}, u32[]{:S(2)}) collective-permute-start(f32[64,384]{1,0:T(8,128)S(1)} %add.6), channel_id=1, source_target_pairs={{0,2},{1,3},{2,0},{3,1},{4,6},{5,7},{6,4},{7,5},{8,10},{9,11},{10,... | collective-permute-start | bytes 294920 | tf_op jit(solution)/shard_map/ppermute | solution.py:268
  21.7 1.4 %collective-permute-start.8 = (f32[64,384]{1,0:T(8,128)S(1)}, f32[64,384]{1,0:T(8,128)S(1)}, u32[]{:S(2)}, u32[]{:S(2)}) collective-permute-start(f32[64,384]{1,0:T(8,128)S(1)} %get-tuple-element.43), channel_id=1, source_target_pairs={{0,1},{1,0},{2,3},{3,2},{4,5},{5,4},{6,7},{7,6},{8,9},{9,8},{10,11... | collective-permute-start | bytes 294920 | tf_op jit(solution)/shard_map/ppermute | solution.py:268

commit v8 on v7

--- a/solution.py
+++ b/solution.py
@@ -233,10 +233,10 @@
     )(*row, col, prev)
 
 
-def finish_kernel(mine_ref, near_ref, src_ref, tgt_ref):
+def finish_kernel(mine_ref, far_ref, near_ref, src_ref, tgt_ref):
     count = src_ref.shape[1]
-    src_ref[...] = mine_ref[:, :count] + near_ref[:, :count]
-    tgt_ref[...] = mine_ref[:, count:] + near_ref[:, count:]
+    src_ref[...] = mine_ref[:, :count] + far_ref[:, :count] + near_ref[:, :count]
+    tgt_ref[...] = mine_ref[:, count:] + far_ref[:, count:] + near_ref[:, count:]
 
 
 def body(src_latent, src_potential, tgt_latent, tgt_potential):
@@ -295,14 +295,13 @@
     last, send = lax.optimization_barrier((last, send))
     mine, near = terms([packed, beside], [near_z, last], [mine, near], [((0, 1), (0, 1), False)])
     near = swap(near, 1)
-    mine = mine + far
     return pl.pallas_call(
         finish_kernel,
         out_shape=[jax.ShapeDtypeStruct(src_latent.shape, f32), jax.ShapeDtypeStruct(tgt_latent.shape, f32)],
-        in_specs=[vmem] * 2,
+        in_specs=[vmem] * 3,
         out_specs=[vmem] * 2,
         compiler_params=pltpu.CompilerParams(vmem_limit_bytes=4 * 2**20),
-    )(mine, near)
+    )(mine, far, near)
 
 
 def solution(mesh):

time: 23.9 us -> 26.1 us (1.092)
  waiting for transfers between devices: 2.46 us -> 4.54 us
    ppermute x9, waiting for transfers between devices: 2.46 us -> 4.54 us  [swap(): return lax.ppermute(value, 'src', [(i, i ^ bits) for i in range(devices)])]
  transfers between devices with their start and end apart: 9 -> 9, of which waited for: 4 -> 4; matrix products, arithmetic and copies ran while one was open for 0% -> 0% of each run, Pallas kernels for 36% -> 26%
where the time goes in v8:
time: 26.1 us; the launch traced here: 25.9 us
  Pallas kernels  10.8 us (41%)
  starting transfers between devices  9.85 us (38%)
  waiting for transfers between devices  4.54 us (17%)
  between operations  0.73 us (3%)
    ppermute x9, starting transfers between devices, swap(): return lax.ppermute(value, 'src', [(i, i ^ bits) for i in range(devices)])  9.85 us
    pallas_call x5, Pallas kernels, pair_terms(): pl.pallas_call(functools.partial(pair_kernel, shape, len(rows), len(cols)...  6.95 us
    ppermute x9, waiting for transfers between devices, swap(): return lax.ppermute(value, 'src', [(i, i ^ bits) for i in range(devices)])  4.54 us
    pallas_call x3, Pallas kernels, late_terms(): pl.pallas_call(functools.partial(late_kernel, shape, totals), out_shape=j...  2.29 us
    pallas_call x1, Pallas kernels, body(): pl.pallas_call(functools.partial(pack_kernel, slabs, feats), out_shape=pl...  0.87 us
    pallas_call x1, Pallas kernels, body(): pl.pallas_call(finish_kernel, out_shape=[jax.ShapeDtypeStruct(src_latent....  0.65 us
  transfers between devices with their start and end apart: 9, of which 4 were waited for; matrix products, arithmetic and copies ran while one was open for 0% of the time, Pallas kernels for 26%

profile of v8, /device:TPU:0, one launch (start us, length us, event | category | flops | bytes accessed | tf_op | source)
XLA Modules:
  0.0 25.9 jit_solution(16050233931880105777)
XLA Ops:
  0.6 0.9 %shard_map.59.refs_0_.refs_1_.block.refs_2_ = f32[200,128]{1,0:T(8,128)S(1)} custom-call(f32[64,256]{1,0:T(8,128)} %src_ref.1, f32[2,256]{1,0:T(2,128)} %srcp_ref.1, f32[64,128]{1,0:T(8,128)} %tgt_ref.1, f32[2,128]{1,0:T(2,128)} %tgtp_ref.1), custom_call_target="tpu_custom_call" | custom-call | tf_op jit(solution)/shard_map/pallas_call | solution.py:254
  1.5 5.1 %collective-permute-start = (f32[200,128]{1,0:T(8,128)S(1)}, f32[200,128]{1,0:T(8,128)S(1)}, u32[]{:S(2)}, u32[]{:S(2)}) collective-permute-start(f32[200,128]{1,0:T(8,128)S(1)} %shard_map.59.refs_0_.refs_1_.block.refs_2_), channel_id=1, source_target_pairs={{0,12},{1,13},{2,14},{3,15},{4,8},{5,9},{6,10},{7,11},{8,4},{9,5},... | collective-permute-start | bytes 307208 | tf_op jit(solution)/shard_map/ppermute | solution.py:268
  6.6 1.5 %collective-permute-start.1 = (f32[200,128]{1,0:T(8,128)S(1)}, f32[200,128]{1,0:T(8,128)S(1)}, u32[]{:S(2)}, u32[]{:S(2)}) collective-permute-start(f32[200,128]{1,0:T(8,128)S(1)} %shard_map.59.refs_0_.refs_1_.block.refs_2_), channel_id=1, source_target_pairs={{0,2},{1,3},{2,0},{3,1},{4,6},{5,7},{6,4},{7,5},{8,10},{9,11},{10,... | collective-permute-start | bytes 307208 | tf_op jit(solution)/shard_map/ppermute | solution.py:268
  8.1 0.0 collective-permute-start.4
  8.1 0.8 %collective-permute-start.5 = (f32[200,128]{1,0:T(8,128)S(1)}, f32[200,128]{1,0:T(8,128)S(1)}, u32[]{:S(2)}, u32[]{:S(2)}) collective-permute-start(f32[200,128]{1,0:T(8,128)S(1)} %shard_map.59.refs_0_.refs_1_.block.refs_2_), channel_id=1, source_target_pairs={{0,8},{1,9},{2,10},{3,11},{4,12},{5,13},{6,14},{7,15},{8,0},{9,1},... | collective-permute-start | bytes 307208 | tf_op jit(solution)/shard_map/ppermute | solution.py:268
  8.9 1.0 %shard_map.60 = (f32[64,384]{1,0:T(8,128)S(1)}, bf16[384,256]{1,0:T(8,128)(2,1)S(1)}, f32[2,384,128]{2,1,0:T(8,128)S(1)}) custom-call(f32[200,128]{1,0:T(8,128)S(1)} %shard_map.59.refs_0_.refs_1_.block.refs_2_, f32[200,128]{1,0:T(8,128)S(1)} %shard_map.59.refs_0_.refs_1_.block.refs_2_), custom_call_target="tpu_custom_call" | custom-call | bytes 1048576 | tf_op jit(solution)/shard_map/pallas_call | solution.py:169
  9.9 0.4 %collective-permute-done.col.refs_2_.refs_3_ = f32[200,128]{1,0:T(8,128)S(1)} collective-permute-done((f32[200,128]{1,0:T(8,128)S(1)}, f32[200,128]{1,0:T(8,128)S(1)}, u32[]{:S(2)}, u32[]{:S(2)}) %collective-permute-start) | collective-permute-done | bytes 102432 | tf_op jit(solution)/shard_map/ppermute | solution.py:268
  10.3 0.8 %shard_map.61.refs_4_ = f32[64,384]{1,0:T(8,128)S(1)} custom-call(f32[200,128]{1,0:T(8,128)S(1)} %shard_map.59.refs_0_.refs_1_.block.refs_2_, bf16[384,256]{1,0:T(8,128)(2,1)S(1)} %get-tuple-element.23.lhs_ref, f32[2,384,128]{2,1,0:T(8,128)S(1)} %get-tuple-element.24.vec_ref, f32[200,128]{1,0:T(8,128)S(1)} %collective-permute-done.col.refs_2_.refs_3_, ...), custom_call_target="tpu_custom_call" | custom-call | bytes 1048576 | tf_op jit(solution)/shard_map/pallas_call | solution.py:226
  11.1 0.2 collective-permute-done.1.refs_0_.block
  11.3 0.0 collective-permute-start.2
  11.3 0.5 %collective-permute-start.3 = (f32[200,128]{1,0:T(8,128)S(1)}, f32[200,128]{1,0:T(8,128)S(1)}, u32[]{:S(2)}, u32[]{:S(2)}) collective-permute-start(f32[200,128]{1,0:T(8,128)S(1)} %shard_map.59.refs_0_.refs_1_.block.refs_2_), channel_id=1, source_target_pairs={{0,1},{1,0},{2,3},{3,2},{4,5},{5,4},{6,7},{7,6},{8,9},{9,8},{10,11... | collective-permute-start | bytes 307208 | tf_op jit(solution)/shard_map/ppermute | solution.py:268
  11.8 1.3 %shard_map.62 = (f32[64,384]{1,0:T(8,128)S(1)}, bf16[384,256]{1,0:T(8,128)(2,1)S(1)}, f32[2,384,128]{2,1,0:T(8,128)S(1)}) custom-call(f32[200,128]{1,0:T(8,128)S(1)} %collective-permute-done.1.refs_0_.block, f32[200,128]{1,0:T(8,128)S(1)} %shard_map.59.refs_0_.refs_1_.block.refs_2_, f32[200,128]{1,0:T(8,128)S(1)} %collective-permute-done.col.refs_2_.refs_3_), custom_call_target="tpu_custom_call" | custom-call | flops 10000000000 | bytes 1048576 | tf_op jit(solution)/shard_map/pallas_call | solution.py:169
  13.1 0.0 collective-permute-done.2.refs_1_.block
  13.1 0.0 collective-permute-done.3.refs_0_.refs_1_
  13.1 1.8 %shard_map.63 = (f32[64,384]{1,0:T(8,128)S(1)}, f32[64,384]{1,0:T(8,128)S(1)}, bf16[384,256]{1,0:T(8,128)(2,1)S(1)}, f32[2,384,128]{2,1,0:T(8,128)S(1)}) custom-call(f32[200,128]{1,0:T(8,128)S(1)} %collective-permute-done.3.refs_0_.refs_1_, f32[200,128]{1,0:T(8,128)S(1)} %collective-permute-done.2.refs_1_.block, ...), custom_call_target="tpu_custom_call" | custom-call | bytes 1048576 | tf_op jit(solution)/shard_map/pallas_call | solution.py:169
  14.9 0.0 collective-permute-done.4.refs_2_
  14.9 1.1 %shard_map.64 = (f32[64,384]{1,0:T(8,128)S(1)}, f32[64,384]{1,0:T(8,128)S(1)}) custom-call(f32[200,128]{1,0:T(8,128)S(1)} %collective-permute-done.1.refs_0_.block, f32[200,128]{1,0:T(8,128)S(1)} %collective-permute-done.2.refs_1_.block, f32[200,128]{1,0:T(8,128)S(1)} %collective-permute-done.4.refs_2_, f32[64,384]{1,0:T(8,128)S(1)} %get-tuple-element.33.refs_3_, ...), custom_call_target="tpu_custom_call" | custom-call | bytes 1048576 | tf_op jit(solution)/shard_map/pallas_call | solution.py:169
  16.0 0.0 collective-permute-done.5.col.refs_3_
  16.0 0.8 %shard_map.66 = f32[64,384]{1,0:T(8,128)S(1)} custom-call(f32[200,128]{1,0:T(8,128)S(1)} %collective-permute-done.2.refs_1_.block, bf16[384,256]{1,0:T(8,128)(2,1)S(1)} %get-tuple-element.36.lhs_ref, f32[2,384,128]{2,1,0:T(8,128)S(1)} %get-tuple-element.37.vec_ref, f32[200,128]{1,0:T(8,128)S(1)} %collective-permute-done.5.col.refs_3_, ...), custom_call_target="tpu_custom_call" | custom-call | bytes 1048576 | tf_op jit(solution)/shard_map/pallas_call | solution.py:226
  16.8 0.1 collective-permute-start.6
  16.8 0.8 %shard_map.65 = f32[64,384]{1,0:T(8,128)S(1)} custom-call(f32[200,128]{1,0:T(8,128)S(1)} %collective-permute-done.1.refs_0_.block, bf16[384,256]{1,0:T(8,128)(2,1)S(1)} %get-tuple-element.30.lhs_ref, f32[2,384,128]{2,1,0:T(8,128)S(1)} %get-tuple-element.31.vec_ref, f32[200,128]{1,0:T(8,128)S(1)} %collective-permute-done.5.col.refs_3_, ...), custom_call_target="tpu_custom_call" | custom-call | bytes 1048576 | tf_op jit(solution)/shard_map/pallas_call | solution.py:226
  17.6 0.5 %collective-permute-done.6 = f32[64,384]{1,0:T(8,128)S(1)} collective-permute-done((f32[64,384]{1,0:T(8,128)S(1)}, f32[64,384]{1,0:T(8,128)S(1)}, u32[]{:S(2)}, u32[]{:S(2)}) %collective-permute-start.6) | collective-permute-done | bytes 98336 | tf_op jit(solution)/shard_map/ppermute | solution.py:268
  18.1 1.8 %shard_map.67 = (f32[64,384]{1,0:T(8,128)S(1)}, f32[64,384]{1,0:T(8,128)S(1)}) custom-call(f32[200,128]{1,0:T(8,128)S(1)} %shard_map.59.refs_0_.refs_1_.block.refs_2_, f32[200,128]{1,0:T(8,128)S(1)} %collective-permute-done.3.refs_0_.refs_1_, f32[200,128]{1,0:T(8,128)S(1)} %collective-permute-done.4.refs_2_, ...), custom_call_target="tpu_custom_call" | custom-call | bytes 1048576 | tf_op jit(solution)/shard_map/pallas_call | solution.py:169
  20.0 0.2 collective-permute-start.8
  20.2 1.6 %collective-permute-start.7 = (f32[64,384]{1,0:T(8,128)S(1)}, f32[64,384]{1,0:T(8,128)S(1)}, u32[]{:S(2)}, u32[]{:S(2)}) collective-permute-start(f32[64,384]{1,0:T(8,128)S(1)} %add.3), channel_id=1, source_target_pairs={{0,2},{1,3},{2,0},{3,1},{4,6},{5,7},{6,4},{7,5},{8,10},{9,11},{10,... | collective-permute-start | bytes 294920 | tf_op jit(solution)/shard_map/ppermute | solution.py:268
  21.8 0.0 collective-permute-done.8.near_ref
  21.8 3.4 %collective-permute-done.7.far_ref = f32[64,384]{1,0:T(8,128)S(1)} collective-permute-done((f32[64,384]{1,0:T(8,128)S(1)}, f32[64,384]{1,0:T(8,128)S(1)}, u32[]{:S(2)}, u32[]{:S(2)}) %collective-permute-start.7) | collective-permute-done | bytes 98336 | tf_op jit(solution)/shard_map/ppermute | solution.py:268
  25.2 0.7 %shard_map.68 = (f32[64,256]{1,0:T(8,128)}, f32[64,128]{1,0:T(8,128)}) custom-call(f32[64,384]{1,0:T(8,128)S(1)} %get-tuple-element.42.mine_ref, f32[64,384]{1,0:T(8,128)S(1)} %collective-permute-done.7.far_ref, f32[64,384]{1,0:T(8,128)S(1)} %collective-permute-done.8.near_ref), custom_call_target="tpu_custom_call" | custom-call | tf_op jit(solution)/shard_map/pallas_call | solution.py:298
  (1 shorter events, 0.0 us)
Async XLA Ops:
  1.5 8.8 %collective-permute-start = (f32[200,128]{1,0:T(8,128)S(1)}, f32[200,128]{1,0:T(8,128)S(1)}, u32[]{:S(2)}, u32[]{:S(2)}) collective-permute-start(f32[200,128]{1,0:T(8,128)S(1)} %shard_map.59.refs_0_.refs_1_.block.refs_2_), channel_id=1, source_target_pairs={{0,12},{1,13},{2,14},{3,15},{4,8},{5,9},{6,10},{7,11},{8,4},{9,5},... | collective-permute-start | bytes 307208 | tf_op jit(solution)/shard_map/ppermute | solution.py:268
  6.6 4.7 %collective-permute-start.1 = (f32[200,128]{1,0:T(8,128)S(1)}, f32[200,128]{1,0:T(8,128)S(1)}, u32[]{:S(2)}, u32[]{:S(2)}) collective-permute-start(f32[200,128]{1,0:T(8,128)S(1)} %shard_map.59.refs_0_.refs_1_.block.refs_2_), channel_id=1, source_target_pairs={{0,2},{1,3},{2,0},{3,1},{4,6},{5,7},{6,4},{7,5},{8,10},{9,11},{10,... | collective-permute-start | bytes 307208 | tf_op jit(solution)/shard_map/ppermute | solution.py:268
  8.1 6.8 %collective-permute-start.4 = (f32[200,128]{1,0:T(8,128)S(1)}, f32[200,128]{1,0:T(8,128)S(1)}, u32[]{:S(2)}, u32[]{:S(2)}) collective-permute-start(f32[200,128]{1,0:T(8,128)S(1)} %shard_map.59.refs_0_.refs_1_.block.refs_2_), channel_id=1, source_target_pairs={{0,4},{1,5},{2,6},{3,7},{4,0},{5,1},{6,2},{7,3},{8,12},{9,13},{10,... | collective-permute-start | bytes 307208 | tf_op jit(solution)/shard_map/ppermute | solution.py:268
  8.1 7.9 %collective-permute-start.5 = (f32[200,128]{1,0:T(8,128)S(1)}, f32[200,128]{1,0:T(8,128)S(1)}, u32[]{:S(2)}, u32[]{:S(2)}) collective-permute-start(f32[200,128]{1,0:T(8,128)S(1)} %shard_map.59.refs_0_.refs_1_.block.refs_2_), channel_id=1, source_target_pairs={{0,8},{1,9},{2,10},{3,11},{4,12},{5,13},{6,14},{7,15},{8,0},{9,1},... | collective-permute-start | bytes 307208 | tf_op jit(solution)/shard_map/ppermute | solution.py:268
  11.3 1.8 %collective-permute-start.2 = (f32[200,128]{1,0:T(8,128)S(1)}, f32[200,128]{1,0:T(8,128)S(1)}, u32[]{:S(2)}, u32[]{:S(2)}) collective-permute-start(f32[200,128]{1,0:T(8,128)S(1)} %collective-permute-done.1.refs_0_.block), channel_id=1, source_target_pairs={{0,1},{1,0},{2,3},{3,2},{4,5},{5,4},{6,7},{7,6},{8,9},{9,8},{10,11... | collective-permute-start | bytes 307208 | tf_op jit(solution)/shard_map/ppermute | solution.py:268
  11.3 1.8 %collective-permute-start.3 = (f32[200,128]{1,0:T(8,128)S(1)}, f32[200,128]{1,0:T(8,128)S(1)}, u32[]{:S(2)}, u32[]{:S(2)}) collective-permute-start(f32[200,128]{1,0:T(8,128)S(1)} %shard_map.59.refs_0_.refs_1_.block.refs_2_), channel_id=1, source_target_pairs={{0,1},{1,0},{2,3},{3,2},{4,5},{5,4},{6,7},{7,6},{8,9},{9,8},{10,11... | collective-permute-start | bytes 307208 | tf_op jit(solution)/shard_map/ppermute | solution.py:268
  16.8 1.4 %collective-permute-start.6 = (f32[64,384]{1,0:T(8,128)S(1)}, f32[64,384]{1,0:T(8,128)S(1)}, u32[]{:S(2)}, u32[]{:S(2)}) collective-permute-start(f32[64,384]{1,0:T(8,128)S(1)} %shard_map.66), channel_id=1, source_target_pairs={{0,1},{1,0},{2,3},{3,2},{4,5},{5,4},{6,7},{7,6},{8,9},{9,8},{10,11... | collective-permute-start | bytes 294920 | tf_op jit(solution)/shard_map/ppermute | solution.py:268
  20.0 1.9 %collective-permute-start.8 = (f32[64,384]{1,0:T(8,128)S(1)}, f32[64,384]{1,0:T(8,128)S(1)}, u32[]{:S(2)}, u32[]{:S(2)}) collective-permute-start(f32[64,384]{1,0:T(8,128)S(1)} %get-tuple-element.43), channel_id=1, source_target_pairs={{0,1},{1,0},{2,3},{3,2},{4,5},{5,4},{6,7},{7,6},{8,9},{9,8},{10,11... | collective-permute-start | bytes 294920 | tf_op jit(solution)/shard_map/ppermute | solution.py:268
  20.2 5.0 %collective-permute-start.7 = (f32[64,384]{1,0:T(8,128)S(1)}, f32[64,384]{1,0:T(8,128)S(1)}, u32[]{:S(2)}, u32[]{:S(2)}) collective-permute-start(f32[64,384]{1,0:T(8,128)S(1)} %add.3), channel_id=1, source_target_pairs={{0,2},{1,3},{2,0},{3,1},{4,6},{5,7},{6,4},{7,5},{8,10},{9,11},{10,... | collective-permute-start | bytes 294920 | tf_op jit(solution)/shard_map/ppermute | solution.py:268
